TPU v7x, 512 devices: a whole 4x4x16 slice. The times are simulated.
512 devices in a mesh: dp: 128 (over z, y, core), section: 4 (over x).
Axes of the slice: x: 4, y: 4, z: 16, core: 2. Of those that a mesh axis runs over, the one named last changes fastest.
Arguments:
- frames: bfloat16 [768, 128, 1280], P('dp'), may hold values from -300 to 300
- block_utt: int32 [768], replicated, may hold values from -1 to 767, as said below
- block_dest: int32 [768], replicated, may hold values from -1 to 511, as said below
- ln_gain: float32 [1280], replicated, may hold values from 0.5 to 1.5
- ln_shift: float32 [1280], replicated, may hold values from -3 to 3
- w_qkv: bfloat16 [3, 1280, 1280], P(None, 'dp', 'section'), may hold values from -10 to 10
- w_out: bfloat16 [1280, 1280], P('section', 'dp'), may hold values from -0.15625 to 0.15625
- post_gain: float32 [1280], replicated, may hold values from 0.5 to 1.5
- post_shift: float32 [1280], replicated, may hold values from -3 to 3
- w_proj: bfloat16 [1280, 4096], P('dp', 'section'), may hold values from -0.15625 to 0.15625
- proj_bias: float32 [4096], P('section'), may hold values from -3 to 3
Outputs:
- lm_rows: bfloat16 [32768, 4096], P(('dp', 'section'))
Inputs may be any that keep to these rules, and one draw needn't show every extreme that they name: `block_utt`: -1 marks an empty slot; equal values mark the blocks of one utterance, which lie on one device of dp and share one destination device. `block_dest`: -1 exactly where block_utt is -1; otherwise a device of dp times 4 plus a slot; the device is the block's own or one beside it; no two blocks name the same slot; at most 1 block of one device go to each neighbouring device, and on some device exactly 1 go each way.
All inputs are finite; a program needn't handle non-finite values.
Results may differ from a plain program's by a relative error of at most 0.012.
Values may be sent and summed in bfloat16 or wider, within the bound.
No kernel may reach another device: no remote copies, remote signals or barrier semaphores. Data moves between devices by JAX's collectives and lax.ppermute only.
A program may use at most 64 MiB of HBM per device.

v0:
```python
import jax
import jax.numpy as jnp
from jax import lax
from jax.sharding import PartitionSpec as P

SEND = 1
CAP = 4
HEAD = 64


def padded(array, sides, width):
    for axis, dim in sides:
        count, length = (lax.axis_size(axis), array.shape[dim])
        up = [(i, (i + 1) % count) for i in range(count - 1)]
        down = [(j, i) for i, j in up]
        last = lax.slice_in_dim(array, length - width, length, axis=dim)
        leading = lax.slice_in_dim(array, 0, width, axis=dim)
        before = lax.ppermute(last, axis, up)
        after = lax.ppermute(leading, axis, down)
        array = jnp.concatenate([before, array, after], axis=dim)
    return array


def normalize(values, scale_gain, offset_term):
    centre = jnp.mean(values, axis=-1, keepdims=True)
    centred = values - centre
    spread = jnp.mean(centred * centred, axis=-1, keepdims=True)
    return centred * lax.rsqrt(spread + 1e-05) * scale_gain + offset_term


def route_table(targets, device, width_blocks):
    moving = (targets >= 0) & (targets // CAP == device)
    ranking = jnp.cumsum(moving.astype(jnp.int32)) - 1
    picks = jnp.arange(width_blocks, dtype=jnp.int32)
    return moving[None, :] & (ranking[None, :] == picks[:, None])


def arriving(targets, owners, device, allowed, width_blocks):
    table = route_table(targets, device, width_blocks) & allowed
    present = jnp.any(table, axis=1)
    slot_ids = jnp.sum(jnp.where(table, targets[None, :] % CAP, 0), axis=1)
    owner_ids = jnp.sum(jnp.where(table, owners[None, :] + 1, 0), axis=1) - 1
    return (jnp.where(present, slot_ids, -1), jnp.where(present, owner_ids, -1))


def select_rows(table, blocks):
    return jnp.dot(table.astype(jnp.bfloat16), blocks, preferred_element_type=jnp.float32).astype(
        jnp.bfloat16
    )


def plan_moves(block_utt, block_dest, own_index, dp_count, slot_count):
    own_targets = lax.dynamic_slice_in_dim(block_dest, own_index * slot_count, slot_count)
    own_owners = lax.dynamic_slice_in_dim(block_utt, own_index * slot_count, slot_count)
    lower_index = jnp.maximum(own_index - 1, 0)
    upper_index = jnp.minimum(own_index + 1, dp_count - 1)
    lower_slots, lower_owners = arriving(
        lax.dynamic_slice_in_dim(block_dest, lower_index * slot_count, slot_count),
        lax.dynamic_slice_in_dim(block_utt, lower_index * slot_count, slot_count),
        own_index,
        own_index > 0,
        SEND,
    )
    upper_slots, upper_owners = arriving(
        lax.dynamic_slice_in_dim(block_dest, upper_index * slot_count, slot_count),
        lax.dynamic_slice_in_dim(block_utt, upper_index * slot_count, slot_count),
        own_index,
        own_index < dp_count - 1,
        SEND,
    )
    outgoing = jnp.concatenate(
        [
            route_table(own_targets, own_index - 1, SEND),
            route_table(own_targets, own_index + 1, SEND),
        ],
        axis=0,
    )
    staying = (own_targets >= 0) & (own_targets // CAP == own_index)
    own_slots = jnp.where(staying, own_targets % CAP, -1)
    every_slot = jnp.concatenate([own_slots, lower_slots, upper_slots])
    every_owner = jnp.concatenate([own_owners, lower_owners, upper_owners])
    placing = every_slot[None, :] == jnp.arange(CAP, dtype=jnp.int32)[:, None]
    slot_owners = jnp.sum(jnp.where(placing, every_owner[None, :] + 1, 0), axis=1) - 1
    return (outgoing, placing, slot_owners, own_owners)


def shards(
    frames,
    block_utt,
    block_dest,
    ln_gain,
    ln_shift,
    w_qkv,
    w_out,
    post_gain,
    post_shift,
    w_proj,
    proj_bias,
):
    own_index = lax.axis_index("dp")
    dp_count = lax.axis_size("dp")
    slot_count, frame_count, features = frames.shape
    qkv_all, out_rows = (
        lax.all_gather(w_qkv, "dp", axis=1, tiled=True),
        lax.all_gather(w_out, "dp", axis=1, tiled=True),
    )
    outgoing, placing, slot_owners, own_owners = plan_moves(
        block_utt, block_dest, own_index, dp_count, slot_count
    )
    flat_frames = frames.reshape(slot_count, frame_count * features)
    leaving = select_rows(outgoing, flat_frames)
    extended = padded(leaving, (("dp", 0),), SEND)
    sources = jnp.concatenate([flat_frames, extended[:SEND], extended[3 * SEND :]], axis=0)
    placed = select_rows(placing, sources).reshape(CAP, frame_count, features)
    row_count = placed.shape[0] * frame_count
    inputs = placed.reshape(row_count, features).astype(jnp.float32)
    normed = normalize(inputs, ln_gain, ln_shift).astype(jnp.bfloat16)
    projected_qkv = jnp.einsum(
        "rd,tdc->trc", normed, qkv_all, preferred_element_type=jnp.float32
    ).astype(jnp.bfloat16)
    local_heads = projected_qkv.shape[2] // HEAD
    row_owner = jnp.repeat(slot_owners, frame_count)
    same_owner = row_owner[:, None] == row_owner[None, :]
    head_results = []
    for head_index in range(local_heads):
        lower_col = head_index * HEAD
        query = projected_qkv[0, :, lower_col : lower_col + HEAD]
        keyed = projected_qkv[1, :, lower_col : lower_col + HEAD]
        valued = projected_qkv[2, :, lower_col : lower_col + HEAD]
        scores = lax.dot_general(
            query, keyed, (((1,), (1,)), ((), ())), preferred_element_type=jnp.float32
        ) * HEAD ** (-0.5)
        scores = jnp.where(same_owner, scores, -1e30)
        row_max = jnp.max(scores, axis=1, keepdims=True)
        weights = jnp.exp(scores - row_max)
        weights = (weights / jnp.sum(weights, axis=1, keepdims=True)).astype(jnp.bfloat16)
        head_results.append(
            jnp.dot(weights, valued, preferred_element_type=jnp.float32).astype(jnp.bfloat16)
        )
    attended = jnp.concatenate(head_results, axis=1)
    partial_terms = jnp.dot(attended, out_rows, preferred_element_type=jnp.float32)
    summed = lax.psum(partial_terms.astype(jnp.bfloat16), "section").astype(jnp.float32)
    resid = inputs + summed
    pooled = resid.reshape(row_count // 2, 2, features).mean(axis=1)
    pooled_norm = normalize(pooled, post_gain, post_shift).astype(jnp.bfloat16)
    projected = jnp.dot(
        pooled_norm,
        lax.all_gather(w_proj, "dp", axis=0, tiled=True),
        preferred_element_type=jnp.float32,
    )
    lm_local = (projected + proj_bias).astype(jnp.bfloat16)
    live_rows = jnp.repeat(slot_owners >= 0, frame_count // 2)
    lm_local = jnp.where(live_rows[:, None], lm_local, jnp.zeros_like(lm_local))
    return lax.all_to_all(lm_local, "section", split_axis=0, concat_axis=1, tiled=True)


def solution(mesh):
    return jax.shard_map(
        shards,
        mesh=mesh,
        in_specs=(
            P("dp", None, None),
            P(),
            P(),
            P(),
            P(),
            P(None, "dp", "section"),
            P("section", "dp"),
            P(),
            P(),
            P("dp", "section"),
            P("section"),
        ),
        out_specs=P(("dp", "section"), None),
        check_vma=False,
    )
```

profile of v0, /device:TPU:8, one launch (start us, length us, event | category | flops | bytes accessed | tf_op | source)
XLA Modules:
  0.0 393.3 jit_solution(182898660284599310)
XLA Ops:
  7.3 0.9 convert_bitcast_fusion.2
  9.2 1.6 fusion.48
  11.2 2.6 copy.21
  13.8 0.8 convolution_convert_fusion.1
  14.7 1.7 fusion.55
  16.3 1.9 collective-permute-start
  18.3 3.6 collective-permute-start.1
  27.9 116.9 %all-gather = bf16[128,10,320]{2,1,0:T(8,128)(2,1)} all-gather(bf16[1,10,320]{2,1,0:T(8,128)(2,1)S(1)} %bitcast.126), channel_id=1, replica_groups=mesh['dp'=128,'section'=4] {'dp'}, dimensions={0}, use_global_device_ids=true | all-gather | bytes 825600 | tf_op jit(solution)/shard_map/all_gather | solution.py:105
  144.8 3.2 reshape.251
  148.0 5.0 %fusion = f32[4,163840]{1,0:T(4,128)} fusion(bf16[1,163840]{1,0:T(2,128)(2,1)} %collective-permute-done.1, bf16[1,163840]{1,0:T(2,128)(2,1)} %collective-permute-done, bf16[6,163840]{1,0:T(8,128)(2,1)S(1)} %bitcast.121, s32[8]{0:T(128)S(1)} %pad_add_fusion), kind=kOutput, calls=%fused_computation.1 | convolution fusion | flops 19660832 | bytes 5242912 | tf_op jit(solution)/shard_map/dot_general | solution.py:47
  153.0 3.6 reshape.249
  157.3 3.9 fusion.11
  165.6 0.9 copy-done
  166.5 2.1 convolution_convert_fusion.2
  168.7 127.5 %all-gather.7.cloned.1.call-done = bf16[128,10,1024]{2,1,0:T(8,128)(2,1)} async-done(((bf16[1,10,1024]{2,1,0:T(8,128)(2,1)}), bf16[128,10,1024]{2,1,0:T(8,128)(2,1)}) %all-gather.7.cloned.1.call-update) | async-done | bytes 2621456 | tf_op jit(solution)/shard_map/all_gather | solution.py:148
  296.3 6.1 %reshape.253 = bf16[1280,1024]{1,0:T(8,128)(2,1)} reshape(bf16[128,10,1024]{2,1,0:T(8,128)(2,1)} %all-gather.7.cloned.1.call-done) | data formatting | bytes 5242880
  302.4 56.7 %all-reduce.2.cloned.1.call-done = bf16[512,1280]{1,0:T(8,128)(2,1)} async-done(((bf16[512,1280]{1,0:T(8,128)(2,1)}), bf16[512,1280]{1,0:T(8,128)(2,1)}) %all-reduce.2.cloned.1.call-update) | async-done | bytes 1310736 | tf_op jit(solution)/shard_map/psum | solution.py:142
  359.1 3.1 convert_add_fusion
  362.1 4.4 %reshape.244 = f32[256,2,1280]{2,1,0:T(2,128)} reshape(f32[512,1280]{1,0:T(8,128)} %convert_add_fusion) | data formatting | bytes 5242880 | tf_op jit(solution)/shard_map/reshape | solution.py:144
  366.6 4.9 %reduce_sum.147 = f32[256,1280]{1,0:T(8,128)S(1)} reduce(f32[256,2,1280]{2,1,0:T(2,128)} %reshape.244, f32[]{:T(128)} %constant.120.clone.1), dimensions={1}, to_apply=%region_24.25 | reduce | flops 327680 | bytes 3932164 | tf_op jit(solution)/shard_map/reduce_sum | solution.py:144
  372.0 1.2 copy-done.1
  373.2 1.0 fusion.21
  374.1 11.8 %all_to_all.19 = bf16[4,64,1024]{2,1,0:T(8,128)(2,1)S(1)} all-to-all(bf16[4,64,1024]{2,1,0:T(8,128)(2,1)S(1)} %bitcast.124), channel_id=1, replica_groups=mesh['dp'=128,'section'=4] {'section'}, dimensions={0} | all-to-all | bytes 1048576 | tf_op jit(solution)/shard_map/all_to_all | solution.py:154
  385.9 0.8 copy.20
  (63 shorter events, 9.0 us)
Async XLA Ops:
  6.5 150.7 %all-gather.5.cloned.1.call-start = ((), (), s32[]{:S(2)}) async-start(), calls=%async_computation.1 | async-start | bytes 3962880 | tf_op jit(solution)/shard_map/all_gather | solution.py:104
  7.3 289.0 %all-gather.7.cloned.1.call-start = ((), (), s32[]{:S(2)}) async-start(), calls=%async_computation.3 | async-start | bytes 4227072 | tf_op jit(solution)/shard_map/all_gather | solution.py:148
  14.7 13.2 %copy-start.2 = (bf16[320,10]{0,1:T(8,128)(2,1)S(1)}, bf16[320,10]{0,1:T(8,128)(2,1)}, u32[]{:S(2)}) copy-start(bf16[320,10]{0,1:T(8,128)(2,1)} %param.17) | copy-start | bytes 19204
  16.3 131.6 %collective-permute-start = (bf16[1,163840]{1,0:T(2,128)(2,1)}, bf16[1,163840]{1,0:T(2,128)(2,1)}, u32[]{:S(2)}, u32[]{:S(2)}) collective-permute-start(bf16[1,163840]{1,0:T(2,128)(2,1)} %get-tuple-element.21), channel_id=1, source_target_pairs={{0,4},{4,8},{8,12},{12,16},{16,20},{20,24},{24,28},{28,32},{32,36}... | collective-permute-start | bytes 983048 | tf_op jit(solution)/shard_map/ppermute | solution.py:18
  18.3 129.7 %collective-permute-start.1 = (bf16[1,163840]{1,0:T(2,128)(2,1)S(1)}, bf16[1,163840]{1,0:T(2,128)(2,1)}, u32[]{:S(2)}, u32[]{:S(2)}) collective-permute-start(bf16[1,163840]{1,0:T(2,128)(2,1)S(1)} %get-tuple-element.22), channel_id=1, source_target_pairs={{4,0},{8,4},{12,8},{16,12},{20,16},{24,20},{28,24},{32,28},{36,32}... | collective-permute-start | bytes 983048 | tf_op jit(solution)/shard_map/ppermute | solution.py:19
  21.9 337.1 %all-reduce.2.cloned.1.call-start = ((), (), s32[]{:S(2)}) async-start(), calls=%async_computation.2 | async-start | bytes 2621440 | tf_op jit(solution)/shard_map/psum | solution.py:142
  156.6 0.7 copy-start.3
  156.6 0.7 copy-start.4
  165.3 1.2 copy-start
  366.6 5.4 %copy-start.5 = (f32[1280]{0:T(1024)S(1)}, f32[1280]{0:T(1024)}, u32[]{:S(2)}) copy-start(f32[1280]{0:T(1024)} %param.19) | copy-start | bytes 15364
  366.6 5.4 %copy-start.6 = (f32[1280]{0:T(1024)S(1)}, f32[1280]{0:T(1024)}, u32[]{:S(2)}) copy-start(f32[1280]{0:T(1024)} %param.18) | copy-start | bytes 15364
  366.6 5.4 %copy-start.7 = (f32[1024]{0:T(1024)S(1)}, f32[1024]{0:T(1024)}, u32[]{:S(2)}) copy-start(f32[1024]{0:T(1024)} %param.21) | copy-start | bytes 12292
  371.4 1.7 copy-start.1
Sparse Core Ops, SparseCore 0:
  10.4 145.2 all-gather.4
  158.8 137.3 all-gather.6
  298.6 60.4 all-reduce.1
where the time goes:
time: 394 us; the launch traced here: 393 us
  waiting for transfers between devices  185 us (47%)
  blocking collectives  129 us (33%)
  local copies, waits for them, and re-layouts  24.9 us (6%)
  between operations  18.2 us (5%)
  matrix products  16.1 us (4%)
  other arithmetic  14.8 us (4%)
  starting transfers between devices  5.63 us (1%)
    all_gather x1, waiting for transfers between devices, shards(): lax.all_gather(w_proj, 'dp', axis=0, tiled=True)  128 us
    all_gather x1, blocking collectives, shards(): lax.all_gather(w_out, 'dp', axis=1, tiled=True)  117 us
    psum x1, waiting for transfers between devices, shards(): lax.psum(partial_terms.astype(jnp.bfloat16), 'section').astype(jnp.float32)  56.7 us
    unnamed x19, local copies, waits for them, and re-layouts  14.1 us
    all_to_all x1, blocking collectives, shards(): lax.all_to_all(lm_local, 'section', split_axis=0, concat_axis=1, tiled=True)  11.8 us
  transfers between devices with their start and end apart: 5, of which 2 were waited for; matrix products, arithmetic and copies ran while one was open for 10% of the time, Pallas kernels for 0%

commit v1 on v0

v1 whole, which is shorter than its diff:
```python
import functools

import jax
import jax.numpy as jnp
import numpy as np
from jax import lax
from jax.experimental import pallas as pl
from jax.experimental.pallas import tpu as pltpu
from jax.sharding import Mesh, PartitionSpec as P

CAP = 4
BLK_IN = 6
FRAMES = 128
D = 1280
HEAD = 64
PART = 320
PROJ = 1024
NY = 4
NC = 2
K_DEV = 10
TILES = 18
PACKED = 192
SLAB = 160
HALF = FRAMES // 2
POOLED = CAP * HALF
ROWS = CAP * FRAMES
EPS = 1e-05
NEG = -1e30
F32 = jnp.float32
BF16 = jnp.bfloat16
DP = ("z", "y", "core")
MIB = 1024 * 1024

VMEM = functools.partial(pl.BlockSpec, memory_space=pltpu.VMEM)
SMEM = functools.partial(pl.BlockSpec, memory_space=pltpu.SMEM)
ANY = functools.partial(pl.BlockSpec, memory_space=pl.ANY)

NT = (((1,), (1,)), ((), ()))


def dp_index():
    return (lax.axis_index("z") * NY + lax.axis_index("y")) * NC + lax.axis_index("core")


def feature_order(nz):
    order = np.arange(D).reshape(nz, NY * NC, K_DEV).transpose(1, 0, 2).reshape(1, D)
    return jnp.asarray(order, jnp.int32)


def plan_kernel(utt, dest, frames, wq, wo, wp, plan, down, up, packed, stage, sems):
    device = dp_index()
    last = dest.shape[0] // BLK_IN - 1
    base = device * BLK_IN
    to_down = jnp.int32(0)
    to_up = jnp.int32(0)
    for g in range(CAP):
        plan[g] = -1
        plan[CAP + g] = -1

    def take(position, code):
        target = dest[position]

        @pl.when((target >= 0) & (target // CAP == device))
        def _():
            slot = target % CAP
            plan[slot] = code
            plan[CAP + slot] = utt[position]

        return target

    for j in range(BLK_IN):
        target = take(base + j, j)
        owner = jnp.where(target >= 0, target // CAP, -9)
        to_down = jnp.where(owner == device - 1, j, to_down)
        to_up = jnp.where(owner == device + 1, j, to_up)
    down_copy = pltpu.make_async_copy(frames.at[to_down], down, sems.at[0])
    up_copy = pltpu.make_async_copy(frames.at[to_up], up, sems.at[1])
    down_copy.start()
    up_copy.start()
    for j in range(BLK_IN):

        @pl.when(device > 0)
        def _():
            take(base - BLK_IN + j, BLK_IN)

        @pl.when(device < last)
        def _():
            take(base + BLK_IN + j, BLK_IN + 1)

    rows = lax.broadcasted_iota(jnp.int32, (K_DEV, K_DEV), 0)
    cols = lax.broadcasted_iota(jnp.int32, (K_DEV, K_DEV), 1)
    eye = jnp.where(rows == cols, 1.0, 0.0).astype(BF16)
    w_out = lax.dot_general(eye, wo[...], NT, preferred_element_type=F32)
    parts = [wq[0].astype(F32), wq[1].astype(F32), wq[2].astype(F32), w_out]
    tiles = []
    for part in parts:
        tiles += [part[:, :128], part[:, 128:256]]
    tails = [part[:, 256:320] for part in parts]
    tiles.append(jnp.concatenate(tails[:2], axis=1))
    tiles.append(jnp.concatenate(tails[2:], axis=1))
    proj = wp[...].astype(F32)
    tiles += [proj[:, i * 128 : (i + 1) * 128] for i in range(PROJ // 128)]
    for i, tile in enumerate(tiles):
        stage[i * K_DEV : (i + 1) * K_DEV, :] = tile
    used = TILES * K_DEV
    stage[used:, :] = jnp.zeros((PACKED - used, 128), F32)
    packed[...] = stage[...].astype(BF16)
    down_copy.wait()
    up_copy.wait()


def plan_call(block_utt, block_dest, frames, w_qkv, w_out, w_proj):
    block = jax.ShapeDtypeStruct((FRAMES, D), BF16)
    return pl.pallas_call(
        plan_kernel,
        out_shape=(
            jax.ShapeDtypeStruct((2 * CAP,), jnp.int32),
            block,
            block,
            jax.ShapeDtypeStruct((PACKED, 128), BF16),
        ),
        in_specs=[SMEM(), SMEM(), ANY(), VMEM(), VMEM(), VMEM()],
        out_specs=(SMEM(), ANY(), ANY(), VMEM()),
        scratch_shapes=[pltpu.VMEM((PACKED, 128), F32), pltpu.SemaphoreType.DMA((2,))],
        name="plan",
    )(block_utt, block_dest, frames, w_qkv, w_out, w_proj)


def unpack_kernel(gathered, main, proj, flat, stage):
    nz = gathered.shape[0] // PACKED
    for z in range(nz):
        flat[...] = gathered[z * PACKED : (z + 1) * PACKED, :].astype(F32)
        for i in range(TILES):
            stage[z * K_DEV : (z + 1) * K_DEV, i * 128 : (i + 1) * 128] = flat[
                i * K_DEV : (i + 1) * K_DEV, :
            ]
    main[...] = stage[:, :D].astype(BF16)
    proj[...] = stage[:, D:].astype(BF16)


def unpack_call(gathered):
    slab = gathered.shape[0] // PACKED * K_DEV
    return pl.pallas_call(
        unpack_kernel,
        out_shape=(
            jax.ShapeDtypeStruct((slab, D), BF16),
            jax.ShapeDtypeStruct((slab, PROJ), BF16),
        ),
        in_specs=[VMEM()],
        out_specs=(VMEM(), VMEM()),
        scratch_shapes=[
            pltpu.VMEM((PACKED, 128), F32),
            pltpu.VMEM((slab, D + PROJ), F32),
        ],
        compiler_params=pltpu.CompilerParams(vmem_limit_bytes=32 * MIB),
        cost_estimate=pl.CostEstimate(flops=0, bytes_accessed=2 * MIB, transcendentals=0),
        name="unpack",
    )(gathered)


def layer_norm(values, gain, shift):
    centre = jnp.mean(values, axis=-1, keepdims=True)
    centred = values - centre
    spread = jnp.mean(centred * centred, axis=-1, keepdims=True)
    return centred * lax.rsqrt(spread + EPS) * gain + shift


def split_exact(values):
    high = values.astype(BF16)
    rest = values - high.astype(F32)
    middle = rest.astype(BF16)
    low = (rest - middle.astype(F32)).astype(BF16)
    return [high, middle, low]


def prepare_kernel(
    plan, frames, from_lower, from_upper, gain, shift, post_gain, post_shift, order,
    normed, residual, post, blocks, stack, sems,
):
    for g in range(CAP):
        source = plan[g]

        @pl.when((source >= 0) & (source < BLK_IN))
        def _():
            pltpu.make_async_copy(frames.at[source], blocks.at[g], sems.at[g]).start()

        @pl.when(source == BLK_IN)
        def _():
            pltpu.make_async_copy(from_lower, blocks.at[g], sems.at[g]).start()

        @pl.when(source == BLK_IN + 1)
        def _():
            pltpu.make_async_copy(from_upper, blocks.at[g], sems.at[g]).start()

        @pl.when(source < 0)
        def _():
            blocks[g] = jnp.zeros((FRAMES, D), BF16)

    parts = split_exact(post_gain[...]) + split_exact(post_shift[...])
    stack[ROWS + FRAMES :, :] = jnp.concatenate(
        parts + [jnp.zeros((10, D), BF16)], axis=0
    )
    for g in range(CAP):

        @pl.when(plan[g] >= 0)
        def _():
            pltpu.make_async_copy(from_lower, blocks.at[g], sems.at[g]).wait()

    rows = lax.broadcasted_iota(jnp.int32, (FRAMES, FRAMES), 0)
    cols = lax.broadcasted_iota(jnp.int32, (FRAMES, FRAMES), 1)
    picked = jnp.where(rows < HALF, 2 * rows, 2 * (rows - HALF) + 1)
    parity = jnp.where(cols == picked, 1.0, 0.0).astype(BF16)
    for g in range(CAP):
        sorted_rows = jnp.dot(parity, blocks[g], preferred_element_type=F32)
        done = layer_norm(sorted_rows, gain[...], shift[...]).astype(BF16)
        stack[g * HALF : (g + 1) * HALF, :] = done[:HALF]
        stack[POOLED + g * HALF : POOLED + (g + 1) * HALF, :] = done[HALF:]
    own = blocks[lax.axis_index("section")]
    stack[ROWS : ROWS + FRAMES, :] = jnp.dot(
        parity, own, preferred_element_type=F32
    ).astype(BF16)
    for start in range(0, D, 256):
        feature = lax.broadcasted_iota(jnp.int32, (D, 256), 0)
        wanted = order[:, start : start + 256]
        select = jnp.where(feature == wanted, 1.0, 0.0).astype(BF16)
        moved = jnp.dot(stack[...], select, preferred_element_type=F32)
        span = slice(start, start + 256)
        normed[:, span] = moved[:ROWS].astype(BF16)
        residual[:, span] = 0.5 * (
            moved[ROWS : ROWS + HALF] + moved[ROWS + HALF : ROWS + FRAMES]
        )
        tail = moved[ROWS + FRAMES :]
        post[0:1, span] = tail[0:1] + (tail[1:2] + tail[2:3])
        post[1:2, span] = tail[3:4] + (tail[4:5] + tail[5:6])


def prepare_call(plan, frames, from_lower, from_upper, vectors, order):
    return pl.pallas_call(
        prepare_kernel,
        out_shape=(
            jax.ShapeDtypeStruct((ROWS, D), BF16),
            jax.ShapeDtypeStruct((HALF, D), F32),
            jax.ShapeDtypeStruct((2, D), F32),
        ),
        in_specs=[SMEM(), ANY(), ANY(), ANY()] + [VMEM()] * 5,
        out_specs=(VMEM(), VMEM(), VMEM()),
        scratch_shapes=[
            pltpu.VMEM((CAP, FRAMES, D), BF16),
            pltpu.VMEM((ROWS + FRAMES + 16, D), BF16),
            pltpu.SemaphoreType.DMA((CAP,)),
        ],
        compiler_params=pltpu.CompilerParams(vmem_limit_bytes=40 * MIB),
        cost_estimate=pl.CostEstimate(
            flops=4 * 656 * D * D, bytes_accessed=8 * MIB, transcendentals=0
        ),
        name="prepare",
    )(plan, frames, from_lower, from_upper, *vectors, order)


def attend_kernel(plan, normed, mine, other, terms, weights, sems):
    core = lax.axis_index("core")
    y = lax.axis_index("y")
    copies = []
    for i, (source, side) in enumerate(((mine, core), (other, 1 - core))):
        for r in range(NY):
            row = ((y + r) % NY * NC + side) * SLAB
            row = pl.multiple_of(row, 32)
            copies.append(
                pltpu.make_async_copy(
                    source.at[pl.ds(r * SLAB, SLAB)],
                    weights.at[pl.ds(row, SLAB)],
                    sems.at[i * NY + r],
                )
            )
    for copy in copies:
        copy.start()
    slot_row = lax.broadcasted_iota(jnp.int32, (ROWS, 1), 0) % POOLED // HALF
    slot_col = lax.broadcasted_iota(jnp.int32, (1, ROWS), 1) % POOLED // HALF
    owner_row = jnp.full((ROWS, 1), -1, jnp.int32)
    owner_col = jnp.full((1, ROWS), -1, jnp.int32)
    for g in range(CAP):
        owner = plan[CAP + g]
        owner_row = jnp.where(slot_row == g, owner, owner_row)
        owner_col = jnp.where(slot_col == g, owner, owner_col)
    same = owner_row == owner_col
    low = lax.broadcasted_iota(jnp.int32, (1, 128), 1) < HEAD
    for copy in copies:
        copy.wait()
    x = normed[...]

    def project(start, size):
        return jnp.dot(x, weights[:, start : start + size], preferred_element_type=F32)

    def head(query, keyed, valued, use_low):
        query = jnp.where(low == use_low, query, 0.0).astype(BF16)
        scores = lax.dot_general(query, keyed, NT, preferred_element_type=F32)
        scores = jnp.where(same, scores * HEAD ** (-0.5), NEG)
        peak = jnp.max(scores, axis=1, keepdims=True)
        weight = jnp.exp(scores - peak)
        total = jnp.sum(weight, axis=1, keepdims=True)
        weight = (weight / total).astype(BF16)
        out = jnp.dot(weight, valued, preferred_element_type=F32)
        return 0.5 * (out[:POOLED] + out[POOLED:])

    queries = project(0, 256)
    keys = project(256, 256).astype(BF16)
    values = project(512, 256).astype(BF16)
    tail = project(1024, 256)
    pieces = []
    for pair in range(2):
        span = slice(pair * 128, (pair + 1) * 128)
        query, keyed, valued = queries[:, span], keys[:, span], values[:, span]
        first = head(query, keyed, valued, True)
        second = head(query, keyed, valued, False)
        pieces.append(jnp.where(low, first, second).astype(BF16))
    pair = tail[:, :128]
    rolled = pltpu.roll(pair, HEAD, 1).astype(BF16)
    fifth = head(pair, rolled, tail[:, 128:].astype(BF16), True)
    fifth = pltpu.roll(fifth, HEAD, 1)
    fifth = jnp.where(low, 0.0, fifth).astype(BF16)
    pooled = jnp.concatenate(pieces + [fifth], axis=1)
    for start in range(0, D, 256):
        rows = slice(start, start + 256)
        out = lax.dot_general(
            pooled[:, :256], weights[rows, 768:1024], NT, preferred_element_type=F32
        ) + lax.dot_general(
            pooled[:, 256:], weights[rows, 1152:1280], NT, preferred_element_type=F32
        )
        terms[:, rows] = out.astype(BF16)


def attend_call(plan, normed, mine, other):
    return pl.pallas_call(
        attend_kernel,
        out_shape=jax.ShapeDtypeStruct((POOLED, D), BF16),
        in_specs=[SMEM(), VMEM(), ANY(), ANY()],
        out_specs=VMEM(),
        scratch_shapes=[
            pltpu.VMEM((D, D), BF16),
            pltpu.SemaphoreType.DMA((2 * NY,)),
        ],
        compiler_params=pltpu.CompilerParams(vmem_limit_bytes=48 * MIB),
        cost_estimate=pl.CostEstimate(
            flops=3 * 10**9, bytes_accessed=8 * MIB, transcendentals=5 * ROWS * ROWS
        ),
        name="attend",
    )(plan, normed, mine, other)


def finish_kernel(terms, residual, post, out):
    total = residual[...]
    for s in range(terms.shape[0] // HALF):
        total += terms[s * HALF : (s + 1) * HALF, :].astype(F32)
    out[...] = layer_norm(total, post[0:1, :], post[1:2, :]).astype(BF16)


def finish_call(terms, residual, post):
    return pl.pallas_call(
        finish_kernel,
        out_shape=jax.ShapeDtypeStruct((HALF, D), BF16),
        in_specs=[VMEM()] * 3,
        out_specs=VMEM(),
        compiler_params=pltpu.CompilerParams(vmem_limit_bytes=16 * MIB),
        name="finish",
    )(terms, residual, post)


def project_kernel(plan, rows, weights, bias, out):
    for g in range(CAP):
        span = slice(g * HALF, (g + 1) * HALF)
        value = jnp.dot(rows[span, :], weights[...], preferred_element_type=F32)
        value = value + bias[...]
        out[span, :] = jnp.where(plan[CAP + g] >= 0, value, 0.0).astype(BF16)


def project_call(plan, rows, weights, bias):
    return pl.pallas_call(
        project_kernel,
        out_shape=jax.ShapeDtypeStruct((POOLED, PROJ), BF16),
        in_specs=[SMEM(), VMEM(), VMEM(), VMEM()],
        out_specs=VMEM(),
        compiler_params=pltpu.CompilerParams(vmem_limit_bytes=32 * MIB),
        cost_estimate=pl.CostEstimate(
            flops=2 * POOLED * D * PROJ, bytes_accessed=4 * MIB, transcendentals=0
        ),
        name="project",
    )(plan, rows, weights, bias)


def shards(
    frames,
    block_utt,
    block_dest,
    ln_gain,
    ln_shift,
    w_qkv,
    w_out,
    post_gain,
    post_shift,
    w_proj,
    proj_bias,
):
    plan, down, up, packed = plan_call(
        block_utt, block_dest, frames, w_qkv, w_out, w_proj
    )
    up_ring = [(i, i + 1) for i in range(lax.axis_size(DP) - 1)]
    from_lower = lax.ppermute(up, DP, up_ring)
    from_upper = lax.ppermute(down, DP, [(j, i) for i, j in up_ring])
    gathered = lax.all_gather(packed, "z", axis=0, tiled=True)
    main, proj = unpack_call(gathered)
    proj_all = lax.all_gather(proj, ("y", "core"), axis=0, tiled=True)
    slabs = [main]
    for r in range(1, NY):
        ring = [((i + r) % NY, i) for i in range(NY)]
        slabs.append(lax.ppermute(main, "y", ring))
    mine = jnp.concatenate(slabs, axis=0)
    other = lax.ppermute(mine, "core", [(0, 1), (1, 0)])
    order = feature_order(lax.axis_size("z"))
    vectors = [v.reshape(1, D) for v in (ln_gain, ln_shift, post_gain, post_shift)]
    normed, residual, post = prepare_call(
        plan, frames, from_lower, from_upper, vectors, order
    )
    terms = attend_call(plan, normed, mine, other)
    terms = lax.all_to_all(terms, "section", split_axis=0, concat_axis=0, tiled=True)
    pooled_norm = finish_call(terms, residual, post)
    rows = lax.all_gather(pooled_norm, "section", axis=0, tiled=True)
    lm_local = project_call(plan, rows, proj_all, proj_bias.reshape(1, PROJ))
    return lax.all_to_all(lm_local, "section", split_axis=0, concat_axis=1, tiled=True)


def solution(mesh):
    dp, section = mesh.devices.shape
    shape = (dp // (NY * NC), NY, NC, section)
    fine = Mesh(mesh.devices.reshape(shape), DP + ("section",))
    return jax.shard_map(
        shards,
        mesh=fine,
        in_specs=(
            P(DP, None, None),
            P(),
            P(),
            P(),
            P(),
            P(None, DP, "section"),
            P("section", DP),
            P(),
            P(),
            P(DP, "section"),
            P("section"),
        ),
        out_specs=P(DP + ("section",), None),
        check_vma=False,
    )
```

time: 394 us -> 177 us (0.45)
  waiting for transfers between devices: 185 us -> 19.1 us
  blocking collectives: 129 us -> 79.7 us
  Pallas kernels: 0 us -> 37.4 us
  local copies, waits for them, and re-layouts: 24.9 us -> 5.58 us
  matrix products: 16.1 us -> 0 us
  starting transfers between devices: 5.63 us -> 20.9 us
  other arithmetic: 14.8 us -> 0 us
  between operations: 18.2 us -> 13.7 us
    all_gather x2 -> x1, waiting for transfers between devices: 128 us -> 0.01 us  [shards(): proj_all = lax.all_gather(proj, ('y', 'core'), axis=0, tiled=True)]
    all_gather x1 -> x2, blocking collectives: 117 us -> 54 us  [the longest x1 40.4 us: shards(): gathered = lax.all_gather(packed, 'z', axis=0, tiled=True)]
    psum x1 -> x0, waiting for transfers between devices: 56.7 us -> none  [shards(): lax.psum(partial_terms.astype(jnp.bfloat16), 'section').astype(jnp.float32)]
    pallas_call x0 -> x6, Pallas kernels: none -> 37.4 us  [the longest x1 22.6 us: plan_call(): pl.pallas_call(plan_kernel, out_shape=(jax.ShapeDtypeStruct((2 * CAP,), j...]
    ppermute x2 -> x6, waiting for transfers between devices: 0.01 us -> 19.1 us  [the longest x3 14.6 us: shards(): slabs.append(lax.ppermute(main, 'y', ring))]
    dot_general x15 -> x0, matrix products: 16.1 us -> none  [the longest x2 5.84 us: select_rows(): jnp.dot(table.astype(jnp.bfloat16), blocks, preferred_element_type=jnp.fl...]
    ppermute x2 -> x6, starting transfers between devices: 5.55 us -> 20.9 us  [the longest x3 10.8 us: shards(): slabs.append(lax.ppermute(main, 'y', ring))]
    all_to_all x0 -> x1, blocking collectives: none -> 15 us  [shards(): lax.all_to_all(terms, 'section', split_axis=0, concat_axis=0, tiled=True)]
  transfers between devices with their start and end apart: 5 -> 7, of which waited for: 2 -> 5; matrix products, arithmetic and copies ran while one was open for 10% -> 0% of each run, Pallas kernels for 0% -> 6%
where the time goes in v1:
time: 177 us; the launch traced here: 176 us
  blocking collectives  79.7 us (45%)
  Pallas kernels  37.4 us (21%)
  starting transfers between devices  20.9 us (12%)
  waiting for transfers between devices  19.1 us (11%)
  between operations  13.7 us (8%)
  local copies, waits for them, and re-layouts  5.58 us (3%)
    all_gather x1, blocking collectives, shards(): gathered = lax.all_gather(packed, 'z', axis=0, tiled=True)  40.4 us
    pallas_call x1, Pallas kernels, plan_call(): pl.pallas_call(plan_kernel, out_shape=(jax.ShapeDtypeStruct((2 * CAP,), j...  22.6 us
    all_to_all x1, blocking collectives, shards(): lax.all_to_all(terms, 'section', split_axis=0, concat_axis=0, tiled=True)  15 us
    ppermute x3, waiting for transfers between devices, shards(): slabs.append(lax.ppermute(main, 'y', ring))  14.6 us
    all_gather x1, blocking collectives, shards(): rows = lax.all_gather(pooled_norm, 'section', axis=0, tiled=True)  13.6 us
    ppermute x3, starting transfers between devices, shards(): slabs.append(lax.ppermute(main, 'y', ring))  10.8 us
    all_to_all x1, blocking collectives, shards(): lax.all_to_all(lm_local, 'section', split_axis=0, concat_axis=1, tiled=True)  10.6 us
    pallas_call x1, Pallas kernels, attend_call(): pl.pallas_call(attend_kernel, out_shape=jax.ShapeDtypeStruct((POOLED, D),...  6.69 us
  transfers between devices with their start and end apart: 7, of which 5 were waited for; matrix products, arithmetic and copies ran while one was open for 0% of the time, Pallas kernels for 6%

profile of v1, /device:TPU:8, one launch (start us, length us, event | category | flops | bytes accessed | tf_op | source)
XLA Modules:
  0.0 176.3 jit_solution(16485032124060332158)
XLA Ops:
  6.5 1.5 copy.14.wo
  8.0 1.4 copy.13.wq
  9.4 22.6 %plan.1 = (s32[8]{0:T(128)}, bf16[128,1280]{1,0:T(8,128)(2,1)}, bf16[128,1280]{1,0:T(8,128)(2,1)}, bf16[192,128]{1,0:T(8,128)(2,1)}) custom-call(s32[768]{0:T(1024)} %utt.1, s32[768]{0:T(1024)} %dest.1, bf16[6,128,1280]{2,1,0:T(8,128)(2,1)} %frames.3, bf16[3,10,320]{2,1,0:T(8,128)(2,1)} %copy.13.wq, bf16[320,10]{1,0:T(8,128)(2,1)} %copy.14.wo, ...), custom_call_target="tpu_custom_call" | custom-call | tf_op jit(solution)/shard_map/plan/pallas_call | solution.py:114
  31.9 40.4 %all_gather.9.gathered = bf16[3072,128]{1,0:T(8,128)(2,1)S(1)} all-gather(bf16[192,128]{1,0:T(8,128)(2,1)} %get-tuple-element.18), channel_id=1, replica_groups=mesh['z'=16,'y'=4,'core'=2,'section'=4] {'z'}, dimensions={0}, use_global_device_ids=true | all-gather | bytes 835584 | tf_op jit(solution)/shard_map/all_gather | solution.py:409
  72.3 1.1 unpack.1
  73.5 2.5 %collective-permute-start.2 = (bf16[160,1280]{1,0:T(8,128)(2,1)S(1)}, bf16[160,1280]{1,0:T(8,128)(2,1)S(1)}, u32[]{:S(2)}, u32[]{:S(2)}) collective-permute-start(bf16[160,1280]{1,0:T(8,128)(2,1)S(1)} %get-tuple-element.19), channel_id=1, source_target_pairs={{8,0},{16,8},{24,16},{0,24},{9,1},{17,9},{25,17},{1,25},{10,2},{18... | collective-permute-start | bytes 1228808 | tf_op jit(solution)/shard_map/ppermute | solution.py:415
  76.0 4.5 %collective-permute-start.3 = (bf16[160,1280]{1,0:T(8,128)(2,1)S(1)}, bf16[160,1280]{1,0:T(8,128)(2,1)S(1)}, u32[]{:S(2)}, u32[]{:S(2)}) collective-permute-start(bf16[160,1280]{1,0:T(8,128)(2,1)S(1)} %get-tuple-element.19), channel_id=1, source_target_pairs={{16,0},{24,8},{0,16},{8,24},{17,1},{25,9},{1,17},{9,25},{18,2},{26... | collective-permute-start | bytes 1228808 | tf_op jit(solution)/shard_map/ppermute | solution.py:415
  80.5 3.8 %collective-permute-start.4 = (bf16[160,1280]{1,0:T(8,128)(2,1)S(1)}, bf16[160,1280]{1,0:T(8,128)(2,1)S(1)}, u32[]{:S(2)}, u32[]{:S(2)}) collective-permute-start(bf16[160,1280]{1,0:T(8,128)(2,1)S(1)} %get-tuple-element.19), channel_id=1, source_target_pairs={{24,0},{0,8},{8,16},{16,24},{25,1},{1,9},{9,17},{17,25},{26,2},{2,... | collective-permute-start | bytes 1228808 | tf_op jit(solution)/shard_map/ppermute | solution.py:415
  84.4 0.7 collective-permute-done.2
  85.1 4.4 %collective-permute-done.3 = bf16[160,1280]{1,0:T(8,128)(2,1)S(1)} collective-permute-done((bf16[160,1280]{1,0:T(8,128)(2,1)S(1)}, bf16[160,1280]{1,0:T(8,128)(2,1)S(1)}, u32[]{:S(2)}, u32[]{:S(2)}) %collective-permute-start.3) | collective-permute-done | bytes 409632 | tf_op jit(solution)/shard_map/ppermute | solution.py:415
  89.5 9.5 %collective-permute-done.4 = bf16[160,1280]{1,0:T(8,128)(2,1)S(1)} collective-permute-done((bf16[160,1280]{1,0:T(8,128)(2,1)S(1)}, bf16[160,1280]{1,0:T(8,128)(2,1)S(1)}, u32[]{:S(2)}, u32[]{:S(2)}) %collective-permute-start.4) | collective-permute-done | bytes 409632 | tf_op jit(solution)/shard_map/ppermute | solution.py:415
  99.0 1.9 %collective-permute-start.5 = (bf16[640,1280]{1,0:T(8,128)(2,1)S(1)}, bf16[640,1280]{1,0:T(8,128)(2,1)S(1)}, u32[]{:S(2)}, u32[]{:S(2)}) collective-permute-start(bf16[640,1280]{1,0:T(8,128)(2,1)S(1)} %constant_dynamic-update-slice_fusion.mine), channel_id=1, source_target_pairs={{0,4},{4,0},{1,5},{5,1},{2,6},{6,2},{3,7},{7,3},{8,12},{12,8},{9,1... | collective-permute-start | bytes 4915208 | tf_op jit(solution)/shard_map/ppermute | solution.py:417
  101.0 2.4 %collective-permute-start = (bf16[128,1280]{1,0:T(8,128)(2,1)S(1)}, bf16[128,1280]{1,0:T(8,128)(2,1)S(1)}, u32[]{:S(2)}, u32[]{:S(2)}) collective-permute-start(bf16[128,1280]{1,0:T(8,128)(2,1)S(1)} %copy-done.10), channel_id=1, source_target_pairs={{0,4},{4,8},{8,12},{12,16},{16,20},{20,24},{24,28},{28,32},{32,36}... | collective-permute-start | bytes 983048 | tf_op jit(solution)/shard_map/ppermute | solution.py:407
  103.4 5.8 %collective-permute-start.1 = (bf16[128,1280]{1,0:T(8,128)(2,1)S(1)}, bf16[128,1280]{1,0:T(8,128)(2,1)S(1)}, u32[]{:S(2)}, u32[]{:S(2)}) collective-permute-start(bf16[128,1280]{1,0:T(8,128)(2,1)S(1)} %copy-done.9), channel_id=1, source_target_pairs={{4,0},{8,4},{12,8},{16,12},{20,16},{24,20},{28,24},{32,28},{36,32}... | collective-permute-start | bytes 983048 | tf_op jit(solution)/shard_map/ppermute | solution.py:408
  109.3 2.7 %collective-permute-done.from_lower = bf16[128,1280]{1,0:T(8,128)(2,1)S(1)} collective-permute-done((bf16[128,1280]{1,0:T(8,128)(2,1)S(1)}, bf16[128,1280]{1,0:T(8,128)(2,1)S(1)}, u32[]{:S(2)}, u32[]{:S(2)}) %collective-permute-start) | collective-permute-done | bytes 327712 | tf_op jit(solution)/shard_map/ppermute | solution.py:407
  112.0 1.8 %collective-permute-done.1.from_upper = bf16[128,1280]{1,0:T(8,128)(2,1)S(1)} collective-permute-done((bf16[128,1280]{1,0:T(8,128)(2,1)S(1)}, bf16[128,1280]{1,0:T(8,128)(2,1)S(1)}, u32[]{:S(2)}, u32[]{:S(2)}) %collective-permute-start.1) | collective-permute-done | bytes 327712 | tf_op jit(solution)/shard_map/ppermute | solution.py:408
  113.8 4.3 %prepare.1 = (bf16[512,1280]{1,0:T(8,128)(2,1)S(1)}, f32[64,1280]{1,0:T(8,128)S(1)}, f32[2,1280]{1,0:T(2,128)S(1)}) custom-call(s32[8]{0:T(128)S(1)} %copy-done.3, bf16[6,128,1280]{2,1,0:T(8,128)(2,1)S(1)} %copy-done.1, bf16[128,1280]{1,0:T(8,128)(2,1)S(1)} %collective-permute-done.from_lower, bf16[128,1280]{1,0:T(8,128)(2,1)S(1)} %collective-permute-done.1.from_upper, ...), custom_call_target="tpu_custom_call" | custom-call | flops 4299161600 | bytes 8388608 | tf_op jit(solution)/shard_map/prepare/pallas_call | solution.py:238
  118.1 6.7 %attend.1 = bf16[256,1280]{1,0:T(8,128)(2,1)S(1)} custom-call(s32[8]{0:T(128)S(1)} %copy-done.3, bf16[512,1280]{1,0:T(8,128)(2,1)S(1)} %get-tuple-element.17.normed, bf16[640,1280]{1,0:T(8,128)(2,1)S(1)} %constant_dynamic-update-slice_fusion.mine, bf16[640,1280]{1,0:T(8,128)(2,1)S(1)} %collective-permute-done.5.other), custom_call_target="tpu_custom_call" | custom-call | flops 3000000000 | bytes 8388608 | tf_op jit(solution)/shard_map/attend/pallas_call | solution.py:333
  124.9 15.0 %all_to_all.30 = bf16[4,64,1280]{2,1,0:T(8,128)(2,1)S(1)} all-to-all(bf16[4,64,1280]{2,1,0:T(8,128)(2,1)S(1)} %bitcast.9), channel_id=1, replica_groups=mesh['z'=16,'y'=4,'core'=2,'section'=4] {'section'}, dimensions={0} | all-to-all | bytes 1310720 | tf_op jit(solution)/shard_map/all_to_all | solution.py:424
  140.2 13.6 %all_gather.10.rows = bf16[256,1280]{1,0:T(8,128)(2,1)S(1)} all-gather(bf16[64,1280]{1,0:T(8,128)(2,1)S(1)} %finish.1), channel_id=1, replica_groups=mesh['z'=16,'y'=4,'core'=2,'section'=4] {'section'}, dimensions={0}, use_global_device_ids=true | all-gather | bytes 819200 | tf_op jit(solution)/shard_map/all_gather | solution.py:426
  153.8 1.7 copy-done
  155.5 2.5 %project.1 = bf16[256,1024]{1,0:T(8,128)(2,1)S(1)} custom-call(s32[8]{0:T(128)S(1)} %copy-done.3, bf16[256,1280]{1,0:T(8,128)(2,1)S(1)} %all_gather.10.rows, bf16[1280,1024]{1,0:T(8,128)(2,1)S(1)} %copy-done, f32[1,1024]{1,0:T(1,128)S(1)} %bitcast.10), custom_call_target="tpu_custom_call" | custom-call | flops 671088640 | bytes 4194304 | tf_op jit(solution)/shard_map/project/pallas_call | solution.py:377
  158.0 10.6 %all_to_all.31 = bf16[4,64,1024]{2,1,0:T(8,128)(2,1)S(1)} all-to-all(bf16[4,64,1024]{2,1,0:T(8,128)(2,1)S(1)} %bitcast.8), channel_id=1, replica_groups=mesh['z'=16,'y'=4,'core'=2,'section'=4] {'section'}, dimensions={0} | all-to-all | bytes 1048576 | tf_op jit(solution)/shard_map/all_to_all | solution.py:428
  168.7 0.8 copy.16
  (34 shorter events, 0.5 us)
Async XLA Ops:
  6.5 147.2 %all-gather.2.cloned.1.call-start = ((), (), s32[]{:S(2)}) async-start(), calls=%async_computation.2 | async-start | bytes 2949120 | tf_op jit(solution)/shard_map/all_gather | solution.py:411
  73.4 27.6 %copy-start.10 = (bf16[128,1280]{1,0:T(8,128)(2,1)S(1)}, bf16[128,1280]{1,0:T(8,128)(2,1)}, u32[]{:S(2)}) copy-start(bf16[128,1280]{1,0:T(8,128)(2,1)} %get-tuple-element.15) | copy-start | bytes 983044
  73.4 30.0 %copy-start.9 = (bf16[128,1280]{1,0:T(8,128)(2,1)S(1)}, bf16[128,1280]{1,0:T(8,128)(2,1)}, u32[]{:S(2)}) copy-start(bf16[128,1280]{1,0:T(8,128)(2,1)} %get-tuple-element.16) | copy-start | bytes 983044
  73.4 35.8 %copy-start.5 = (f32[1280]{0:T(1024)S(1)}, f32[1280]{0:T(1024)}, u32[]{:S(2)}) copy-start(f32[1280]{0:T(1024)} %param.15) | copy-start | bytes 15364
  73.4 35.8 %copy-start.6 = (f32[1280]{0:T(1024)S(1)}, f32[1280]{0:T(1024)}, u32[]{:S(2)}) copy-start(f32[1280]{0:T(1024)} %param.16) | copy-start | bytes 15364
  73.5 35.8 %copy-start.7 = (f32[1280]{0:T(1024)S(1)}, f32[1280]{0:T(1024)}, u32[]{:S(2)}) copy-start(f32[1280]{0:T(1024)} %param.19) | copy-start | bytes 15364
  73.5 35.8 %copy-start.8 = (f32[1280]{0:T(1024)S(1)}, f32[1280]{0:T(1024)}, u32[]{:S(2)}) copy-start(f32[1280]{0:T(1024)} %param.20) | copy-start | bytes 15364
  73.5 40.3 %copy-start.1 = (bf16[6,128,1280]{2,1,0:T(8,128)(2,1)S(1)}, bf16[6,128,1280]{2,1,0:T(8,128)(2,1)}, u32[]{:S(2)}) copy-start(bf16[6,128,1280]{2,1,0:T(8,128)(2,1)} %frames.3) | copy-start | bytes 5898244
  73.5 40.3 %copy-start.3 = (s32[8]{0:T(128)S(1)}, s32[8]{0:T(128)}, u32[]{:S(2)}) copy-start(s32[8]{0:T(128)} %get-tuple-element.14.plan) | copy-start | bytes 100
  73.5 40.3 %copy-start.4 = (s32[1,1280]{1,0:T(1,128)S(1)}, s32[1,1280]{1,0:T(1,128)}, u32[]{:S(2)}) copy-start(s32[1,1280]{1,0:T(1,128)} %constant.2.clone.order) | copy-start | bytes 15364
  73.5 11.6 %collective-permute-start.2 = (bf16[160,1280]{1,0:T(8,128)(2,1)S(1)}, bf16[160,1280]{1,0:T(8,128)(2,1)S(1)}, u32[]{:S(2)}, u32[]{:S(2)}) collective-permute-start(bf16[160,1280]{1,0:T(8,128)(2,1)S(1)} %get-tuple-element.19), channel_id=1, source_target_pairs={{8,0},{16,8},{24,16},{0,24},{9,1},{17,9},{25,17},{1,25},{10,2},{18... | collective-permute-start | bytes 1228808 | tf_op jit(solution)/shard_map/ppermute | solution.py:415
  76.0 13.5 %collective-permute-start.3 = (bf16[160,1280]{1,0:T(8,128)(2,1)S(1)}, bf16[160,1280]{1,0:T(8,128)(2,1)S(1)}, u32[]{:S(2)}, u32[]{:S(2)}) collective-permute-start(bf16[160,1280]{1,0:T(8,128)(2,1)S(1)} %get-tuple-element.19), channel_id=1, source_target_pairs={{16,0},{24,8},{0,16},{8,24},{17,1},{25,9},{1,17},{9,25},{18,2},{26... | collective-permute-start | bytes 1228808 | tf_op jit(solution)/shard_map/ppermute | solution.py:415
  80.5 18.5 %collective-permute-start.4 = (bf16[160,1280]{1,0:T(8,128)(2,1)S(1)}, bf16[160,1280]{1,0:T(8,128)(2,1)S(1)}, u32[]{:S(2)}, u32[]{:S(2)}) collective-permute-start(bf16[160,1280]{1,0:T(8,128)(2,1)S(1)} %get-tuple-element.19), channel_id=1, source_target_pairs={{24,0},{0,8},{8,16},{16,24},{25,1},{1,9},{9,17},{17,25},{26,2},{2,... | collective-permute-start | bytes 1228808 | tf_op jit(solution)/shard_map/ppermute | solution.py:415
  99.0 19.1 %collective-permute-start.5 = (bf16[640,1280]{1,0:T(8,128)(2,1)S(1)}, bf16[640,1280]{1,0:T(8,128)(2,1)S(1)}, u32[]{:S(2)}, u32[]{:S(2)}) collective-permute-start(bf16[640,1280]{1,0:T(8,128)(2,1)S(1)} %constant_dynamic-update-slice_fusion.mine), channel_id=1, source_target_pairs={{0,4},{4,0},{1,5},{5,1},{2,6},{6,2},{3,7},{7,3},{8,12},{12,8},{9,1... | collective-permute-start | bytes 4915208 | tf_op jit(solution)/shard_map/ppermute | solution.py:417
  101.0 11.0 %collective-permute-start = (bf16[128,1280]{1,0:T(8,128)(2,1)S(1)}, bf16[128,1280]{1,0:T(8,128)(2,1)S(1)}, u32[]{:S(2)}, u32[]{:S(2)}) collective-permute-start(bf16[128,1280]{1,0:T(8,128)(2,1)S(1)} %copy-done.10), channel_id=1, source_target_pairs={{0,4},{4,8},{8,12},{12,16},{16,20},{20,24},{24,28},{28,32},{32,36}... | collective-permute-start | bytes 983048 | tf_op jit(solution)/shard_map/ppermute | solution.py:407
  103.4 10.4 %collective-permute-start.1 = (bf16[128,1280]{1,0:T(8,128)(2,1)S(1)}, bf16[128,1280]{1,0:T(8,128)(2,1)S(1)}, u32[]{:S(2)}, u32[]{:S(2)}) collective-permute-start(bf16[128,1280]{1,0:T(8,128)(2,1)S(1)} %copy-done.9), channel_id=1, source_target_pairs={{4,0},{8,4},{12,8},{16,12},{20,16},{24,20},{28,24},{32,28},{36,32}... | collective-permute-start | bytes 983048 | tf_op jit(solution)/shard_map/ppermute | solution.py:408
  124.8 28.9 %copy-start.2 = (f32[1024]{0:T(1024)S(1)}, f32[1024]{0:T(1024)}, u32[]{:S(2)}) copy-start(f32[1024]{0:T(1024)} %param.22) | copy-start | bytes 12292
  153.8 1.7 copy-start
Sparse Core Ops, SparseCore 0:
  73.5 31.9 all-gather.1

commit v2 on v1

--- a/solution.py
+++ b/solution.py
@@ -17,6 +17,7 @@
 PROJ = 1024
 NY = 4
 NC = 2
+Y_ORDER = (0, 2, 1, 3)
 K_DEV = 10
 TILES = 18
 PACKED = 192
@@ -30,6 +31,7 @@
 BF16 = jnp.bfloat16
 DP = ("z", "y", "core")
 MIB = 1024 * 1024
+WIDE = 58 * MIB
 
 VMEM = functools.partial(pl.BlockSpec, memory_space=pltpu.VMEM)
 SMEM = functools.partial(pl.BlockSpec, memory_space=pltpu.SMEM)
@@ -47,15 +49,17 @@
     return jnp.asarray(order, jnp.int32)
 
 
-def plan_kernel(utt, dest, frames, wq, wo, wp, plan, down, up, packed, stage, sems):
+def plan_kernel(utt, dest, frames, wq, wo, wp, plan, packed, far, stage, sem):
+    core = lax.axis_index("core")
     device = dp_index()
     last = dest.shape[0] // BLK_IN - 1
     base = device * BLK_IN
     to_down = jnp.int32(0)
     to_up = jnp.int32(0)
-    for g in range(CAP):
+    from_lower = BLK_IN + core
+    from_upper = BLK_IN + 1 - core
+    for g in range(2 * CAP):
         plan[g] = -1
-        plan[CAP + g] = -1
 
     def take(position, code):
         target = dest[position]
@@ -73,25 +77,22 @@
         owner = jnp.where(target >= 0, target // CAP, -9)
         to_down = jnp.where(owner == device - 1, j, to_down)
         to_up = jnp.where(owner == device + 1, j, to_up)
-    down_copy = pltpu.make_async_copy(frames.at[to_down], down, sems.at[0])
-    up_copy = pltpu.make_async_copy(frames.at[to_up], up, sems.at[1])
-    down_copy.start()
-    up_copy.start()
+    leaving = jnp.where(core == 0, to_down, to_up)
+    plan[2 * CAP] = jnp.where(core == 0, to_up, to_down)
+    copy = pltpu.make_async_copy(frames.at[leaving], far, sem)
+    copy.start()
     for j in range(BLK_IN):
 
         @pl.when(device > 0)
         def _():
-            take(base - BLK_IN + j, BLK_IN)
+            take(base - BLK_IN + j, from_lower)
 
         @pl.when(device < last)
         def _():
-            take(base + BLK_IN + j, BLK_IN + 1)
-
-    rows = lax.broadcasted_iota(jnp.int32, (K_DEV, K_DEV), 0)
-    cols = lax.broadcasted_iota(jnp.int32, (K_DEV, K_DEV), 1)
-    eye = jnp.where(rows == cols, 1.0, 0.0).astype(BF16)
-    w_out = lax.dot_general(eye, wo[...], NT, preferred_element_type=F32)
-    parts = [wq[0].astype(F32), wq[1].astype(F32), wq[2].astype(F32), w_out]
+            take(base + BLK_IN + j, from_upper)
+
+    qkv = wq[...].astype(F32)
+    parts = [qkv[:, 0, :], qkv[:, 1, :], qkv[:, 2, :], wo[...].astype(F32)]
     tiles = []
     for part in parts:
         tiles += [part[:, :128], part[:, 128:256]]
@@ -105,25 +106,23 @@
     used = TILES * K_DEV
     stage[used:, :] = jnp.zeros((PACKED - used, 128), F32)
     packed[...] = stage[...].astype(BF16)
-    down_copy.wait()
-    up_copy.wait()
+    copy.wait()
 
 
 def plan_call(block_utt, block_dest, frames, w_qkv, w_out, w_proj):
-    block = jax.ShapeDtypeStruct((FRAMES, D), BF16)
     return pl.pallas_call(
         plan_kernel,
         out_shape=(
-            jax.ShapeDtypeStruct((2 * CAP,), jnp.int32),
-            block,
-            block,
+            jax.ShapeDtypeStruct((2 * CAP + 1,), jnp.int32),
             jax.ShapeDtypeStruct((PACKED, 128), BF16),
+            jax.ShapeDtypeStruct((FRAMES, D), BF16),
         ),
         in_specs=[SMEM(), SMEM(), ANY(), VMEM(), VMEM(), VMEM()],
-        out_specs=(SMEM(), ANY(), ANY(), VMEM()),
-        scratch_shapes=[pltpu.VMEM((PACKED, 128), F32), pltpu.SemaphoreType.DMA((2,))],
+        out_specs=(SMEM(), VMEM(), VMEM()),
+        scratch_shapes=[pltpu.VMEM((PACKED, 128), F32), pltpu.SemaphoreType.DMA],
+        compiler_params=pltpu.CompilerParams(vmem_limit_bytes=WIDE),
         name="plan",
-    )(block_utt, block_dest, frames, w_qkv, w_out, w_proj)
+    )(block_utt, block_dest, frames, w_qkv.transpose(1, 0, 2), w_out.T, w_proj)
 
 
 def unpack_kernel(gathered, main, proj, flat, stage):
@@ -139,23 +138,42 @@
 
 
 def unpack_call(gathered):
-    slab = gathered.shape[0] // PACKED * K_DEV
+    rows = gathered.shape[0] // PACKED * K_DEV
     return pl.pallas_call(
         unpack_kernel,
         out_shape=(
-            jax.ShapeDtypeStruct((slab, D), BF16),
-            jax.ShapeDtypeStruct((slab, PROJ), BF16),
+            jax.ShapeDtypeStruct((rows, D), BF16),
+            jax.ShapeDtypeStruct((rows, PROJ), BF16),
         ),
         in_specs=[VMEM()],
         out_specs=(VMEM(), VMEM()),
         scratch_shapes=[
             pltpu.VMEM((PACKED, 128), F32),
-            pltpu.VMEM((slab, D + PROJ), F32),
+            pltpu.VMEM((rows, D + PROJ), F32),
         ],
-        compiler_params=pltpu.CompilerParams(vmem_limit_bytes=32 * MIB),
+        compiler_params=pltpu.CompilerParams(vmem_limit_bytes=WIDE),
         cost_estimate=pl.CostEstimate(flops=0, bytes_accessed=2 * MIB, transcendentals=0),
         name="unpack",
     )(gathered)
+
+
+def leave_kernel(plan, frames, near, sem):
+    copy = pltpu.make_async_copy(frames.at[plan[2 * CAP]], near, sem)
+    copy.start()
+    copy.wait()
+
+
+def leave_call(plan, frames):
+    return pl.pallas_call(
+        leave_kernel,
+        out_shape=jax.ShapeDtypeStruct((FRAMES, D), BF16),
+        in_specs=[SMEM(), ANY()],
+        out_specs=VMEM(),
+        scratch_shapes=[pltpu.SemaphoreType.DMA],
+        compiler_params=pltpu.CompilerParams(vmem_limit_bytes=WIDE),
+        cost_estimate=pl.CostEstimate(flops=0, bytes_accessed=2 * MIB, transcendentals=0),
+        name="leave",
+    )(plan, frames)
 
 
 def layer_norm(values, gain, shift):
@@ -174,7 +192,7 @@
 
 
 def prepare_kernel(
-    plan, frames, from_lower, from_upper, gain, shift, post_gain, post_shift, order,
+    plan, frames, far, near, gain, shift, post_gain, post_shift, order,
     normed, residual, post, blocks, stack, sems,
 ):
     for g in range(CAP):
@@ -186,17 +204,20 @@
 
         @pl.when(source == BLK_IN)
         def _():
-            pltpu.make_async_copy(from_lower, blocks.at[g], sems.at[g]).start()
+            pltpu.make_async_copy(far, blocks.at[g], sems.at[g]).start()
 
         @pl.when(source == BLK_IN + 1)
         def _():
-            pltpu.make_async_copy(from_upper, blocks.at[g], sems.at[g]).start()
+            pltpu.make_async_copy(near, blocks.at[g], sems.at[g]).start()
 
         @pl.when(source < 0)
         def _():
             blocks[g] = jnp.zeros((FRAMES, D), BF16)
 
-    parts = split_exact(post_gain[...]) + split_exact(post_shift[...])
+    row = (1, D)
+    gain, shift = gain[...].reshape(row), shift[...].reshape(row)
+    parts = split_exact(post_gain[...].reshape(row))
+    parts += split_exact(post_shift[...].reshape(row))
     stack[ROWS + FRAMES :, :] = jnp.concatenate(
         parts + [jnp.zeros((10, D), BF16)], axis=0
     )
@@ -204,7 +225,7 @@
 
         @pl.when(plan[g] >= 0)
         def _():
-            pltpu.make_async_copy(from_lower, blocks.at[g], sems.at[g]).wait()
+            pltpu.make_async_copy(far, blocks.at[g], sems.at[g]).wait()
 
     rows = lax.broadcasted_iota(jnp.int32, (FRAMES, FRAMES), 0)
     cols = lax.broadcasted_iota(jnp.int32, (FRAMES, FRAMES), 1)
@@ -212,7 +233,7 @@
     parity = jnp.where(cols == picked, 1.0, 0.0).astype(BF16)
     for g in range(CAP):
         sorted_rows = jnp.dot(parity, blocks[g], preferred_element_type=F32)
-        done = layer_norm(sorted_rows, gain[...], shift[...]).astype(BF16)
+        done = layer_norm(sorted_rows, gain, shift).astype(BF16)
         stack[g * HALF : (g + 1) * HALF, :] = done[:HALF]
         stack[POOLED + g * HALF : POOLED + (g + 1) * HALF, :] = done[HALF:]
     own = blocks[lax.axis_index("section")]
@@ -234,7 +255,7 @@
         post[1:2, span] = tail[3:4] + (tail[4:5] + tail[5:6])
 
 
-def prepare_call(plan, frames, from_lower, from_upper, vectors, order):
+def prepare_call(plan, frames, far, near, vectors, order):
     return pl.pallas_call(
         prepare_kernel,
         out_shape=(
@@ -249,29 +270,43 @@
             pltpu.VMEM((ROWS + FRAMES + 16, D), BF16),
             pltpu.SemaphoreType.DMA((CAP,)),
         ],
-        compiler_params=pltpu.CompilerParams(vmem_limit_bytes=40 * MIB),
+        compiler_params=pltpu.CompilerParams(vmem_limit_bytes=WIDE),
         cost_estimate=pl.CostEstimate(
-            flops=4 * 656 * D * D, bytes_accessed=8 * MIB, transcendentals=0
+            flops=8 * 656 * D * D, bytes_accessed=8 * MIB, transcendentals=0
         ),
         name="prepare",
-    )(plan, frames, from_lower, from_upper, *vectors, order)
-
-
-def attend_kernel(plan, normed, mine, other, terms, weights, sems):
+    )(plan, frames, far, near, *vectors, order)
+
+
+def main_order(y, core):
+    return [(y + r) % NY for r in Y_ORDER]
+
+
+def proj_order(y, core):
+    first = jnp.where(core == 0, y ^ 1, y ^ 3)
+    second = jnp.where(core == 0, y ^ 3, y ^ 1)
+    return [y, first, second, y ^ 2]
+
+
+def slab_copies(order, mine, other, weights, sems):
     core = lax.axis_index("core")
     y = lax.axis_index("y")
     copies = []
     for i, (source, side) in enumerate(((mine, core), (other, 1 - core))):
-        for r in range(NY):
-            row = ((y + r) % NY * NC + side) * SLAB
-            row = pl.multiple_of(row, 32)
+        for j, place in enumerate(order(y, side)):
+            row = pl.multiple_of((place * NC + side) * SLAB, 32)
             copies.append(
                 pltpu.make_async_copy(
-                    source.at[pl.ds(r * SLAB, SLAB)],
+                    source.at[pl.ds(j * SLAB, SLAB)],
                     weights.at[pl.ds(row, SLAB)],
-                    sems.at[i * NY + r],
+                    sems.at[i * NY + j],
                 )
             )
+    return copies
+
+
+def attend_kernel(plan, normed, mine, other, terms, weights, sems):
+    copies = slab_copies(main_order, mine, other, weights, sems)
     for copy in copies:
         copy.start()
     slot_row = lax.broadcasted_iota(jnp.int32, (ROWS, 1), 0) % POOLED // HALF
@@ -365,7 +400,12 @@
     )(terms, residual, post)
 
 
-def project_kernel(plan, rows, weights, bias, out):
+def project_kernel(plan, rows, mine, other, bias, out, weights, sems):
+    copies = slab_copies(proj_order, mine, other, weights, sems)
+    for copy in copies:
+        copy.start()
+    for copy in copies:
+        copy.wait()
     for g in range(CAP):
         span = slice(g * HALF, (g + 1) * HALF)
         value = jnp.dot(rows[span, :], weights[...], preferred_element_type=F32)
@@ -373,18 +413,42 @@
         out[span, :] = jnp.where(plan[CAP + g] >= 0, value, 0.0).astype(BF16)
 
 
-def project_call(plan, rows, weights, bias):
+def project_call(plan, rows, mine, other, bias):
     return pl.pallas_call(
         project_kernel,
         out_shape=jax.ShapeDtypeStruct((POOLED, PROJ), BF16),
-        in_specs=[SMEM(), VMEM(), VMEM(), VMEM()],
+        in_specs=[SMEM(), VMEM(), ANY(), ANY(), VMEM()],
         out_specs=VMEM(),
-        compiler_params=pltpu.CompilerParams(vmem_limit_bytes=32 * MIB),
+        scratch_shapes=[
+            pltpu.VMEM((D, PROJ), BF16),
+            pltpu.SemaphoreType.DMA((2 * NY,)),
+        ],
+        compiler_params=pltpu.CompilerParams(vmem_limit_bytes=48 * MIB),
         cost_estimate=pl.CostEstimate(
             flops=2 * POOLED * D * PROJ, bytes_accessed=4 * MIB, transcendentals=0
         ),
         name="project",
-    )(plan, rows, weights, bias)
+    )(plan, rows, mine, other, bias)
+
+
+def y_slabs(slab):
+    slabs = [slab]
+    for r in Y_ORDER[1:]:
+        slabs.append(lax.ppermute(slab, "y", [((i + r) % NY, i) for i in range(NY)]))
+    return jnp.concatenate(slabs, axis=0)
+
+
+def y_swap(slabs, masks):
+    pairs = [
+        (y * NC + core, (y ^ masks[core]) * NC + core)
+        for y in range(NY)
+        for core in range(NC)
+    ]
+    return lax.ppermute(slabs, ("y", "core"), pairs)
+
+
+def other_core(slabs):
+    return lax.ppermute(slabs, "core", [(0, 1), (1, 0)])
 
 
 def shards(
@@ -400,31 +464,36 @@
     w_proj,
     proj_bias,
 ):
-    plan, down, up, packed = plan_call(
+    plan, packed, far = plan_call(
         block_utt, block_dest, frames, w_qkv, w_out, w_proj
     )
-    up_ring = [(i, i + 1) for i in range(lax.axis_size(DP) - 1)]
-    from_lower = lax.ppermute(up, DP, up_ring)
-    from_upper = lax.ppermute(down, DP, [(j, i) for i, j in up_ring])
+    odd = range(1, lax.axis_size(DP) - 1, 2)
+    far = lax.ppermute(
+        far, DP, [(i, i + 1) for i in odd] + [(i + 1, i) for i in odd]
+    )
     gathered = lax.all_gather(packed, "z", axis=0, tiled=True)
     main, proj = unpack_call(gathered)
-    proj_all = lax.all_gather(proj, ("y", "core"), axis=0, tiled=True)
-    slabs = [main]
-    for r in range(1, NY):
-        ring = [((i + r) % NY, i) for i in range(NY)]
-        slabs.append(lax.ppermute(main, "y", ring))
-    mine = jnp.concatenate(slabs, axis=0)
-    other = lax.ppermute(mine, "core", [(0, 1), (1, 0)])
+    main, plan = lax.optimization_barrier((main, plan))
+    mine = y_slabs(main)
+    near = other_core(leave_call(plan, frames))
     order = feature_order(lax.axis_size("z"))
-    vectors = [v.reshape(1, D) for v in (ln_gain, ln_shift, post_gain, post_shift)]
-    normed, residual, post = prepare_call(
-        plan, frames, from_lower, from_upper, vectors, order
-    )
+    vectors = (ln_gain, ln_shift, post_gain, post_shift)
+    normed, residual, post = prepare_call(plan, frames, far, near, vectors, order)
+    mine, normed, proj = lax.optimization_barrier((mine, normed, proj))
+    other = other_core(mine)
+    proj_pair = y_swap(proj, (1, 3))
     terms = attend_call(plan, normed, mine, other)
+    terms, proj_pair = lax.optimization_barrier((terms, proj_pair))
+    proj_pair = jnp.concatenate([proj, proj_pair], axis=0)
+    proj_rest = y_swap(proj_pair, (3, 1))
     terms = lax.all_to_all(terms, "section", split_axis=0, concat_axis=0, tiled=True)
     pooled_norm = finish_call(terms, residual, post)
+    pooled_norm, proj_rest = lax.optimization_barrier((pooled_norm, proj_rest))
+    proj_mine = jnp.concatenate([proj_pair, proj_rest], axis=0)
+    proj_other = other_core(proj_mine)
     rows = lax.all_gather(pooled_norm, "section", axis=0, tiled=True)
-    lm_local = project_call(plan, rows, proj_all, proj_bias.reshape(1, PROJ))
+    bias = proj_bias.reshape(1, PROJ)
+    lm_local = project_call(plan, rows, proj_mine, proj_other, bias)
     return lax.all_to_all(lm_local, "section", split_axis=0, concat_axis=1, tiled=True)
 
 

time: 177 us -> 147 us (0.83)
  between operations: 13.7 us -> 0.27 us
  blocking collectives: 79.7 us -> 66.8 us
  Pallas kernels: 37.4 us -> 25.1 us
  starting transfers between devices: 20.9 us -> 30.9 us
  local copies, waits for them, and re-layouts: 5.58 us -> 3.5 us
    pallas_call x2 -> x3, Pallas kernels: 23.6 us -> 7.55 us  [the longest x1 2.72 us: plan_call(): pl.pallas_call(plan_kernel, out_shape=(jax.ShapeDtypeStruct((2 * CAP + 1,...]
    all_to_all x1 -> x0, blocking collectives: 15 us -> none  [shards(): lax.all_to_all(terms, 'section', split_axis=0, concat_axis=0, tiled=True)]
    ppermute x6 -> x9, waiting for transfers between devices: 19.1 us -> 6.93 us  [the longest x3 6.91 us: y_slabs(): lax.ppermute(slab, 'y', [((i + r) % NY, i) for i in range(NY)])]
    all_to_all x0 -> x1, waiting for transfers between devices: none -> 11.4 us  [shards(): lax.all_to_all(terms, 'section', split_axis=0, concat_axis=0, tiled=True)]
    ppermute x6 -> x9, starting transfers between devices: 20.9 us -> 26.6 us  [the longest x3 10.3 us: y_slabs(): lax.ppermute(slab, 'y', [((i + r) % NY, i) for i in range(NY)])]
    all_to_all x0 -> x1, starting transfers between devices: none -> 4.3 us  [shards(): lax.all_to_all(terms, 'section', split_axis=0, concat_axis=0, tiled=True)]
    unnamed x27 -> x22, local copies, waits for them, and re-layouts: 4.7 us -> 1.53 us
    pallas_call x1, Pallas kernels: 4.33 us -> 6.36 us  [prepare_call(): pl.pallas_call(prepare_kernel, out_shape=(jax.ShapeDtypeStruct((ROWS, D),...]
  transfers between devices with their start and end apart: 7 -> 10, of which waited for: 5 -> 2; matrix products, arithmetic and copies ran while one was open for 0% -> 0% of each run, Pallas kernels for 6% -> 10%
where the time goes in v2:
time: 147 us; the launch traced here: 146 us
  blocking collectives  66.8 us (45%)
  starting transfers between devices  30.9 us (21%)
  Pallas kernels  25.1 us (17%)
  waiting for transfers between devices  18.4 us (13%)
  local copies, waits for them, and re-layouts  3.5 us (2%)
    all_gather x1, blocking collectives, shards(): gathered = lax.all_gather(packed, 'z', axis=0, tiled=True)  42.3 us
    all_gather x1, blocking collectives, shards(): rows = lax.all_gather(pooled_norm, 'section', axis=0, tiled=True)  13.8 us
    all_to_all x1, waiting for transfers between devices, shards(): lax.all_to_all(terms, 'section', split_axis=0, concat_axis=0, tiled=True)  11.4 us
    all_to_all x1, blocking collectives, shards(): lax.all_to_all(lm_local, 'section', split_axis=0, concat_axis=1, tiled=True)  10.6 us
    ppermute x3, starting transfers between devices, y_slabs(): lax.ppermute(slab, 'y', [((i + r) % NY, i) for i in range(NY)])  10.3 us
    ppermute x2, starting transfers between devices, y_swap(): return lax.ppermute(slabs, ('y', 'core'), pairs)  7.99 us
    pallas_call x1, Pallas kernels, attend_call(): pl.pallas_call(attend_kernel, out_shape=jax.ShapeDtypeStruct((POOLED, D),...  7.54 us
    ppermute x3, waiting for transfers between devices, y_slabs(): lax.ppermute(slab, 'y', [((i + r) % NY, i) for i in range(NY)])  6.91 us
  transfers between devices with their start and end apart: 10, of which 2 were waited for; matrix products, arithmetic and copies ran while one was open for 0% of the time, Pallas kernels for 10%

profile of v2, /device:TPU:8, one launch (start us, length us, event | category | flops | bytes accessed | tf_op | source)
XLA Modules:
  0.0 145.9 jit_solution(7425256964161975076)
XLA Ops:
  0.0 2.7 %plan.1 = (s32[9]{0:T(128)}, bf16[192,128]{1,0:T(8,128)(2,1)}, bf16[128,1280]{1,0:T(8,128)(2,1)}) custom-call(s32[768]{0:T(1024)} %utt.1, s32[768]{0:T(1024)} %dest.1, bf16[6,128,1280]{2,1,0:T(8,128)(2,1)} %frames.5, bf16[10,3,320]{2,1,0:T(4,128)(2,1)} %bitcast.13, bf16[10,320]{1,0:T(8,128)(2,1)} %bitcast.14, bf16[10,1024]{1,0:T(8,128)(2,1)} %wp.1), custom_call_target="tpu_custom_call" | custom-call | tf_op jit(solution)/shard_map/plan/pallas_call | solution.py:113
  2.7 42.3 %all_gather.6.gathered = bf16[3072,128]{1,0:T(8,128)(2,1)} all-gather(bf16[192,128]{1,0:T(8,128)(2,1)} %get-tuple-element.22), channel_id=1, replica_groups=mesh['z'=16,'y'=4,'core'=2,'section'=4] {'z'}, dimensions={0}, use_global_device_ids=true | all-gather | bytes 835584 | tf_op jit(solution)/shard_map/all_gather | solution.py:474
  45.1 2.3 %unpack.1 = (bf16[160,1280]{1,0:T(8,128)(2,1)}, bf16[160,1024]{1,0:T(8,128)(2,1)}) custom-call(bf16[3072,128]{1,0:T(8,128)(2,1)} %all_gather.6.gathered), custom_call_target="tpu_custom_call" | custom-call | bytes 2097152 | tf_op jit(solution)/shard_map/unpack/pallas_call | solution.py:142
  47.4 2.5 %leave.1 = bf16[128,1280]{1,0:T(8,128)(2,1)} custom-call(s32[9]{0:T(128)} %get-tuple-element.25.plan, bf16[6,128,1280]{2,1,0:T(8,128)(2,1)} %frames.5), custom_call_target="tpu_custom_call" | custom-call | bytes 2097152 | tf_op jit(solution)/shard_map/leave/pallas_call | solution.py:167
  49.9 1.9 %collective-permute-start.4 = (bf16[128,1280]{1,0:T(8,128)(2,1)}, bf16[128,1280]{1,0:T(8,128)(2,1)S(1)}, u32[]{:S(2)}, u32[]{:S(2)}) collective-permute-start(bf16[128,1280]{1,0:T(8,128)(2,1)} %leave.1), channel_id=1, source_target_pairs={{0,4},{4,0},{1,5},{5,1},{2,6},{6,2},{3,7},{7,3},{8,12},{12,8},{9,1... | collective-permute-start | bytes 983048 | tf_op jit(solution)/shard_map/ppermute | solution.py:451
  51.9 2.5 %collective-permute-start.3 = (bf16[128,1280]{1,0:T(8,128)(2,1)S(1)}, bf16[128,1280]{1,0:T(8,128)(2,1)S(1)}, u32[]{:S(2)}, u32[]{:S(2)}) collective-permute-start(bf16[128,1280]{1,0:T(8,128)(2,1)S(1)} %copy-done.7), channel_id=1, source_target_pairs={{4,8},{12,16},{20,24},{28,32},{36,40},{44,48},{52,56},{60,64},{68,... | collective-permute-start | bytes 983048 | tf_op jit(solution)/shard_map/ppermute | solution.py:471
  54.3 4.5 %collective-permute-start = (bf16[160,1280]{1,0:T(8,128)(2,1)S(1)}, bf16[160,1280]{1,0:T(8,128)(2,1)S(1)}, u32[]{:S(2)}, u32[]{:S(2)}) collective-permute-start(bf16[160,1280]{1,0:T(8,128)(2,1)S(1)} %copy-done.6), channel_id=1, source_target_pairs={{16,0},{24,8},{0,16},{8,24},{17,1},{25,9},{1,17},{9,25},{18,2},{26... | collective-permute-start | bytes 1228808 | tf_op jit(solution)/shard_map/ppermute | solution.py:437
  58.8 3.0 %collective-permute-start.1 = (bf16[160,1280]{1,0:T(8,128)(2,1)S(1)}, bf16[160,1280]{1,0:T(8,128)(2,1)S(1)}, u32[]{:S(2)}, u32[]{:S(2)}) collective-permute-start(bf16[160,1280]{1,0:T(8,128)(2,1)S(1)} %copy-done.6), channel_id=1, source_target_pairs={{8,0},{16,8},{24,16},{0,24},{9,1},{17,9},{25,17},{1,25},{10,2},{18... | collective-permute-start | bytes 1228808 | tf_op jit(solution)/shard_map/ppermute | solution.py:437
  61.8 2.9 %collective-permute-start.2 = (bf16[160,1280]{1,0:T(8,128)(2,1)S(1)}, bf16[160,1280]{1,0:T(8,128)(2,1)S(1)}, u32[]{:S(2)}, u32[]{:S(2)}) collective-permute-start(bf16[160,1280]{1,0:T(8,128)(2,1)S(1)} %copy-done.6), channel_id=1, source_target_pairs={{24,0},{0,8},{8,16},{16,24},{25,1},{1,9},{9,17},{17,25},{26,2},{2,... | collective-permute-start | bytes 1228808 | tf_op jit(solution)/shard_map/ppermute | solution.py:437
  66.2 6.4 %prepare.1 = (bf16[512,1280]{1,0:T(8,128)(2,1)}, f32[64,1280]{1,0:T(8,128)}, f32[2,1280]{1,0:T(2,128)}) custom-call(s32[9]{0:T(128)} %get-tuple-element.25.plan, bf16[6,128,1280]{2,1,0:T(8,128)(2,1)} %frames.5, bf16[128,1280]{1,0:T(8,128)(2,1)} %copy-done.9, bf16[128,1280]{1,0:T(8,128)(2,1)} %copy-done.8, f32[1280]{0:T(1024)} %gain.1, f32[1280]{0:T(1024)} %shift.1, ...), custom_call_target="tpu_custom_call" | custom-call | flops 8598323200 | bytes 8388608 | tf_op jit(solution)/shard_map/prepare/pallas_call | solution.py:259
  72.6 6.9 %collective-permute-done.1 = bf16[160,1280]{1,0:T(8,128)(2,1)S(1)} collective-permute-done((bf16[160,1280]{1,0:T(8,128)(2,1)S(1)}, bf16[160,1280]{1,0:T(8,128)(2,1)S(1)}, u32[]{:S(2)}, u32[]{:S(2)}) %collective-permute-start.1) | collective-permute-done | bytes 409632 | tf_op jit(solution)/shard_map/ppermute | solution.py:437
  79.6 1.9 %collective-permute-start.5 = (bf16[640,1280]{1,0:T(8,128)(2,1)S(1)}, bf16[640,1280]{1,0:T(8,128)(2,1)S(1)}, u32[]{:S(2)}, u32[]{:S(2)}) collective-permute-start(bf16[640,1280]{1,0:T(8,128)(2,1)S(1)} %pad_maximum_fusion.mine), channel_id=1, source_target_pairs={{0,4},{4,0},{1,5},{5,1},{2,6},{6,2},{3,7},{7,3},{8,12},{12,8},{9,1... | collective-permute-start | bytes 4915208 | tf_op jit(solution)/shard_map/ppermute | solution.py:451
  81.5 3.8 %collective-permute-start.6 = (bf16[160,1024]{1,0:T(8,128)(2,1)S(1)}, bf16[160,1024]{1,0:T(8,128)(2,1)S(1)}, u32[]{:S(2)}, u32[]{:S(2)}) collective-permute-start(bf16[160,1024]{1,0:T(8,128)(2,1)S(1)} %copy-done.5), channel_id=1, source_target_pairs={{0,8},{4,28},{8,0},{12,20},{16,24},{20,12},{24,16},{28,4},{1,9},{5... | collective-permute-start | bytes 983048 | tf_op jit(solution)/shard_map/ppermute | solution.py:447
  85.4 7.5 %attend.1 = bf16[256,1280]{1,0:T(8,128)(2,1)} custom-call(s32[9]{0:T(128)S(1)} %copy-done.3, bf16[512,1280]{1,0:T(8,128)(2,1)S(1)} %copy-done.4, bf16[640,1280]{1,0:T(8,128)(2,1)S(1)} %pad_maximum_fusion.mine, bf16[640,1280]{1,0:T(8,128)(2,1)S(1)} %collective-permute-done.5.other), custom_call_target="tpu_custom_call" | custom-call | flops 3000000000 | bytes 8388608 | tf_op jit(solution)/shard_map/attend/pallas_call | solution.py:368
  93.0 0.9 pad_maximum_fusion.1
  93.9 4.2 %collective-permute-start.7 = (bf16[320,1024]{1,0:T(8,128)(2,1)}, bf16[320,1024]{1,0:T(8,128)(2,1)}, u32[]{:S(2)}, u32[]{:S(2)}) collective-permute-start(bf16[320,1024]{1,0:T(8,128)(2,1)} %pad_maximum_fusion.1), channel_id=1, source_target_pairs={{0,24},{4,12},{8,16},{12,4},{16,8},{20,28},{24,0},{28,20},{1,25},{... | collective-permute-start | bytes 1966088 | tf_op jit(solution)/shard_map/ppermute | solution.py:447
  98.1 4.3 %all-to-all-start = ((bf16[4,64,1280]{2,1,0:T(8,128)(2,1)}), bf16[4,64,1280]{2,1,0:T(8,128)(2,1)S(1)}, u32[]{:S(2)}, u32[]{:S(2)}) async-start(bf16[4,64,1280]{2,1,0:T(8,128)(2,1)} %bitcast.2), calls=%async_computation | async-start | bytes 1310720 | tf_op jit(solution)/shard_map/all_to_all | solution.py:489
  102.4 11.4 %all-to-all-done = bf16[4,64,1280]{2,1,0:T(8,128)(2,1)S(1)} async-done(((bf16[4,64,1280]{2,1,0:T(8,128)(2,1)}), bf16[4,64,1280]{2,1,0:T(8,128)(2,1)S(1)}, u32[]{:S(2)}, u32[]{:S(2)}) %all-to-all-start) | async-done | bytes 655392 | tf_op jit(solution)/shard_map/all_to_all | solution.py:489
  114.2 1.1 constant_dynamic-update-slice_fusion.mine
  115.3 1.9 %collective-permute-start.8 = (bf16[640,1024]{1,0:T(8,128)(2,1)S(1)}, bf16[640,1024]{1,0:T(8,128)(2,1)S(1)}, u32[]{:S(2)}, u32[]{:S(2)}) collective-permute-start(bf16[640,1024]{1,0:T(8,128)(2,1)S(1)} %constant_dynamic-update-slice_fusion.mine), channel_id=1, source_target_pairs={{0,4},{4,0},{1,5},{5,1},{2,6},{6,2},{3,7},{7,3},{8,12},{12,8},{9,1... | collective-permute-start | bytes 3932168 | tf_op jit(solution)/shard_map/ppermute | solution.py:451
  117.2 13.8 %all_gather.7.rows = bf16[256,1280]{1,0:T(8,128)(2,1)S(1)} all-gather(bf16[64,1280]{1,0:T(8,128)(2,1)S(1)} %finish.1), channel_id=1, replica_groups=mesh['z'=16,'y'=4,'core'=2,'section'=4] {'section'}, dimensions={0}, use_global_device_ids=true | all-gather | bytes 819200 | tf_op jit(solution)/shard_map/all_gather | solution.py:494
  131.1 3.4 %project.1 = bf16[256,1024]{1,0:T(8,128)(2,1)S(1)} custom-call(s32[9]{0:T(128)S(1)} %copy-done.3, bf16[256,1280]{1,0:T(8,128)(2,1)S(1)} %all_gather.7.rows, bf16[640,1024]{1,0:T(8,128)(2,1)S(1)} %constant_dynamic-update-slice_fusion.mine, bf16[640,1024]{1,0:T(8,128)(2,1)S(1)} %collective-permute-done.8.other, f32[1,1024]{1,0:T(1,128)S(1)} %bitcast.11), custom_call_target="tpu_custom_call" | custom-call | flops 671088640 | bytes 4194304 | tf_op jit(solution)/shard_map/project/pallas_call | solution.py:417
  134.5 10.6 %all_to_all.30 = bf16[4,64,1024]{2,1,0:T(8,128)(2,1)S(1)} all-to-all(bf16[4,64,1024]{2,1,0:T(8,128)(2,1)S(1)} %bitcast.10), channel_id=1, replica_groups=mesh['z'=16,'y'=4,'core'=2,'section'=4] {'section'}, dimensions={0} | all-to-all | bytes 1048576 | tf_op jit(solution)/shard_map/all_to_all | solution.py:497
  145.1 0.8 copy.14
  (32 shorter events, 1.9 us)
Async XLA Ops:
  45.1 6.8 %copy-start.7 = (bf16[128,1280]{1,0:T(8,128)(2,1)S(1)}, bf16[128,1280]{1,0:T(8,128)(2,1)}, u32[]{:S(2)}) copy-start(bf16[128,1280]{1,0:T(8,128)(2,1)} %get-tuple-element.27) | copy-start | bytes 983044
  47.4 6.9 %copy-start.6 = (bf16[160,1280]{1,0:T(8,128)(2,1)S(1)}, bf16[160,1280]{1,0:T(8,128)(2,1)}, u32[]{:S(2)}) copy-start(bf16[160,1280]{1,0:T(8,128)(2,1)} %get-tuple-element.26) | copy-start | bytes 1228804
  49.9 14.8 %collective-permute-start.4 = (bf16[128,1280]{1,0:T(8,128)(2,1)}, bf16[128,1280]{1,0:T(8,128)(2,1)S(1)}, u32[]{:S(2)}, u32[]{:S(2)}) collective-permute-start(bf16[128,1280]{1,0:T(8,128)(2,1)} %leave.1), channel_id=1, source_target_pairs={{0,4},{4,0},{1,5},{5,1},{2,6},{6,2},{3,7},{7,3},{8,12},{12,8},{9,1... | collective-permute-start | bytes 983048 | tf_op jit(solution)/shard_map/ppermute | solution.py:451
  51.9 12.9 %collective-permute-start.3 = (bf16[128,1280]{1,0:T(8,128)(2,1)S(1)}, bf16[128,1280]{1,0:T(8,128)(2,1)S(1)}, u32[]{:S(2)}, u32[]{:S(2)}) collective-permute-start(bf16[128,1280]{1,0:T(8,128)(2,1)S(1)} %copy-done.7), channel_id=1, source_target_pairs={{4,8},{12,16},{20,24},{28,32},{36,40},{44,48},{52,56},{60,64},{68,... | collective-permute-start | bytes 983048 | tf_op jit(solution)/shard_map/ppermute | solution.py:471
  54.3 18.2 %collective-permute-start = (bf16[160,1280]{1,0:T(8,128)(2,1)S(1)}, bf16[160,1280]{1,0:T(8,128)(2,1)S(1)}, u32[]{:S(2)}, u32[]{:S(2)}) collective-permute-start(bf16[160,1280]{1,0:T(8,128)(2,1)S(1)} %copy-done.6), channel_id=1, source_target_pairs={{16,0},{24,8},{0,16},{8,24},{17,1},{25,9},{1,17},{9,25},{18,2},{26... | collective-permute-start | bytes 1228808 | tf_op jit(solution)/shard_map/ppermute | solution.py:437
  58.8 20.7 %collective-permute-start.1 = (bf16[160,1280]{1,0:T(8,128)(2,1)S(1)}, bf16[160,1280]{1,0:T(8,128)(2,1)S(1)}, u32[]{:S(2)}, u32[]{:S(2)}) collective-permute-start(bf16[160,1280]{1,0:T(8,128)(2,1)S(1)} %copy-done.6), channel_id=1, source_target_pairs={{8,0},{16,8},{24,16},{0,24},{9,1},{17,9},{25,17},{1,25},{10,2},{18... | collective-permute-start | bytes 1228808 | tf_op jit(solution)/shard_map/ppermute | solution.py:437
  61.8 17.7 %collective-permute-start.2 = (bf16[160,1280]{1,0:T(8,128)(2,1)S(1)}, bf16[160,1280]{1,0:T(8,128)(2,1)S(1)}, u32[]{:S(2)}, u32[]{:S(2)}) collective-permute-start(bf16[160,1280]{1,0:T(8,128)(2,1)S(1)} %copy-done.6), channel_id=1, source_target_pairs={{24,0},{0,8},{8,16},{16,24},{25,1},{1,9},{9,17},{17,25},{26,2},{2,... | collective-permute-start | bytes 1228808 | tf_op jit(solution)/shard_map/ppermute | solution.py:437
  64.7 0.8 copy-start.8
  65.5 0.7 copy-start.9
  72.5 9.0 %copy-start.5 = (bf16[160,1024]{1,0:T(8,128)(2,1)S(1)}, bf16[160,1024]{1,0:T(8,128)(2,1)}, u32[]{:S(2)}) copy-start(bf16[160,1024]{1,0:T(8,128)(2,1)} %get-tuple-element.32) | copy-start | bytes 983044
  72.6 12.8 %copy-start.3 = (s32[9]{0:T(128)S(1)}, s32[9]{0:T(128)}, u32[]{:S(2)}) copy-start(s32[9]{0:T(128)} %get-tuple-element.25.plan) | copy-start | bytes 112
  72.6 12.8 %copy-start.4 = (bf16[512,1280]{1,0:T(8,128)(2,1)S(1)}, bf16[512,1280]{1,0:T(8,128)(2,1)}, u32[]{:S(2)}) copy-start(bf16[512,1280]{1,0:T(8,128)(2,1)} %get-tuple-element.30.normed) | copy-start | bytes 3932164
  79.6 5.8 %collective-permute-start.5 = (bf16[640,1280]{1,0:T(8,128)(2,1)S(1)}, bf16[640,1280]{1,0:T(8,128)(2,1)S(1)}, u32[]{:S(2)}, u32[]{:S(2)}) collective-permute-start(bf16[640,1280]{1,0:T(8,128)(2,1)S(1)} %pad_maximum_fusion.mine), channel_id=1, source_target_pairs={{0,4},{4,0},{1,5},{5,1},{2,6},{6,2},{3,7},{7,3},{8,12},{12,8},{9,1... | collective-permute-start | bytes 4915208 | tf_op jit(solution)/shard_map/ppermute | solution.py:451
  81.5 11.4 %collective-permute-start.6 = (bf16[160,1024]{1,0:T(8,128)(2,1)S(1)}, bf16[160,1024]{1,0:T(8,128)(2,1)S(1)}, u32[]{:S(2)}, u32[]{:S(2)}) collective-permute-start(bf16[160,1024]{1,0:T(8,128)(2,1)S(1)} %copy-done.5), channel_id=1, source_target_pairs={{0,8},{4,28},{8,0},{12,20},{16,24},{20,12},{24,16},{28,4},{1,9},{5... | collective-permute-start | bytes 983048 | tf_op jit(solution)/shard_map/ppermute | solution.py:447
  93.9 20.0 %copy-start = (f32[64,1280]{1,0:T(8,128)S(1)}, f32[64,1280]{1,0:T(8,128)}, u32[]{:S(2)}) copy-start(f32[64,1280]{1,0:T(8,128)} %get-tuple-element.34.residual) | copy-start | bytes 983044
  93.9 20.0 %copy-start.1 = (f32[2,1280]{1,0:T(2,128)S(1)}, f32[2,1280]{1,0:T(2,128)}, u32[]{:S(2)}) copy-start(f32[2,1280]{1,0:T(2,128)} %get-tuple-element.35.post) | copy-start | bytes 30724
  93.9 20.3 %collective-permute-start.7 = (bf16[320,1024]{1,0:T(8,128)(2,1)}, bf16[320,1024]{1,0:T(8,128)(2,1)}, u32[]{:S(2)}, u32[]{:S(2)}) collective-permute-start(bf16[320,1024]{1,0:T(8,128)(2,1)} %pad_maximum_fusion.1), channel_id=1, source_target_pairs={{0,24},{4,12},{8,16},{12,4},{16,8},{20,28},{24,0},{28,20},{1,25},{... | collective-permute-start | bytes 1966088 | tf_op jit(solution)/shard_map/ppermute | solution.py:447
  98.1 15.8 %all-to-all-start = ((bf16[4,64,1280]{2,1,0:T(8,128)(2,1)}), bf16[4,64,1280]{2,1,0:T(8,128)(2,1)S(1)}, u32[]{:S(2)}, u32[]{:S(2)}) async-start(bf16[4,64,1280]{2,1,0:T(8,128)(2,1)} %bitcast.2), calls=%async_computation | async-start | bytes 1310720 | tf_op jit(solution)/shard_map/all_to_all | solution.py:489
  113.9 17.2 %copy-start.2 = (f32[1024]{0:T(1024)S(1)}, f32[1024]{0:T(1024)}, u32[]{:S(2)}) copy-start(f32[1024]{0:T(1024)} %param.22) | copy-start | bytes 12292
  115.3 15.8 %collective-permute-start.8 = (bf16[640,1024]{1,0:T(8,128)(2,1)S(1)}, bf16[640,1024]{1,0:T(8,128)(2,1)S(1)}, u32[]{:S(2)}, u32[]{:S(2)}) collective-permute-start(bf16[640,1024]{1,0:T(8,128)(2,1)S(1)} %constant_dynamic-update-slice_fusion.mine), channel_id=1, source_target_pairs={{0,4},{4,0},{1,5},{5,1},{2,6},{6,2},{3,7},{7,3},{8,12},{12,8},{9,1... | collective-permute-start | bytes 3932168 | tf_op jit(solution)/shard_map/ppermute | solution.py:451

commit v3 on v2

--- a/solution.py
+++ b/solution.py
@@ -2,7 +2,6 @@
 
 import jax
 import jax.numpy as jnp
-import numpy as np
 from jax import lax
 from jax.experimental import pallas as pl
 from jax.experimental.pallas import tpu as pltpu
@@ -22,6 +21,7 @@
 TILES = 18
 PACKED = 192
 SLAB = 160
+HALF_D = 640
 HALF = FRAMES // 2
 POOLED = CAP * HALF
 ROWS = CAP * FRAMES
@@ -44,12 +44,20 @@
     return (lax.axis_index("z") * NY + lax.axis_index("y")) * NC + lax.axis_index("core")
 
 
-def feature_order(nz):
-    order = np.arange(D).reshape(nz, NY * NC, K_DEV).transpose(1, 0, 2).reshape(1, D)
-    return jnp.asarray(order, jnp.int32)
-
-
-def plan_kernel(utt, dest, frames, wq, wo, wp, plan, packed, far, stage, sem):
+def y_step(index):
+    return jnp.where(index == 1, 2, jnp.where(index == 2, 1, index))
+
+
+def feature_at(position):
+    side, rest = position // HALF_D, position % HALF_D
+    place = (lax.axis_index("y") + y_step(rest // SLAB)) % NY
+    core = (lax.axis_index("core") + side) % NC
+    rest = rest % SLAB
+    owner = (rest // K_DEV * NY + place) * NC + core
+    return owner * K_DEV + rest % K_DEV
+
+
+def plan_kernel(utt, dest, frames, wq, wo, wp, plan, packed, far, near, stage, sems):
     core = lax.axis_index("core")
     device = dp_index()
     last = dest.shape[0] // BLK_IN - 1
@@ -77,10 +85,14 @@
         owner = jnp.where(target >= 0, target // CAP, -9)
         to_down = jnp.where(owner == device - 1, j, to_down)
         to_up = jnp.where(owner == device + 1, j, to_up)
-    leaving = jnp.where(core == 0, to_down, to_up)
-    plan[2 * CAP] = jnp.where(core == 0, to_up, to_down)
-    copy = pltpu.make_async_copy(frames.at[leaving], far, sem)
-    copy.start()
+    to_far = jnp.where(core == 0, to_down, to_up)
+    to_near = jnp.where(core == 0, to_up, to_down)
+    copies = [
+        pltpu.make_async_copy(frames.at[to_far], far, sems.at[0]),
+        pltpu.make_async_copy(frames.at[to_near], near, sems.at[1]),
+    ]
+    for copy in copies:
+        copy.start()
     for j in range(BLK_IN):
 
         @pl.when(device > 0)
@@ -106,20 +118,22 @@
     used = TILES * K_DEV
     stage[used:, :] = jnp.zeros((PACKED - used, 128), F32)
     packed[...] = stage[...].astype(BF16)
-    copy.wait()
+    for copy in copies:
+        copy.wait()
 
 
 def plan_call(block_utt, block_dest, frames, w_qkv, w_out, w_proj):
     return pl.pallas_call(
         plan_kernel,
         out_shape=(
-            jax.ShapeDtypeStruct((2 * CAP + 1,), jnp.int32),
+            jax.ShapeDtypeStruct((2 * CAP,), jnp.int32),
             jax.ShapeDtypeStruct((PACKED, 128), BF16),
             jax.ShapeDtypeStruct((FRAMES, D), BF16),
+            jax.ShapeDtypeStruct((FRAMES, D), BF16),
         ),
         in_specs=[SMEM(), SMEM(), ANY(), VMEM(), VMEM(), VMEM()],
-        out_specs=(SMEM(), VMEM(), VMEM()),
-        scratch_shapes=[pltpu.VMEM((PACKED, 128), F32), pltpu.SemaphoreType.DMA],
+        out_specs=(SMEM(), VMEM(), VMEM(), VMEM()),
+        scratch_shapes=[pltpu.VMEM((PACKED, 128), F32), pltpu.SemaphoreType.DMA((2,))],
         compiler_params=pltpu.CompilerParams(vmem_limit_bytes=WIDE),
         name="plan",
     )(block_utt, block_dest, frames, w_qkv.transpose(1, 0, 2), w_out.T, w_proj)
@@ -151,29 +165,10 @@
             pltpu.VMEM((PACKED, 128), F32),
             pltpu.VMEM((rows, D + PROJ), F32),
         ],
-        compiler_params=pltpu.CompilerParams(vmem_limit_bytes=WIDE),
+        compiler_params=pltpu.CompilerParams(vmem_limit_bytes=32 * MIB),
         cost_estimate=pl.CostEstimate(flops=0, bytes_accessed=2 * MIB, transcendentals=0),
         name="unpack",
     )(gathered)
-
-
-def leave_kernel(plan, frames, near, sem):
-    copy = pltpu.make_async_copy(frames.at[plan[2 * CAP]], near, sem)
-    copy.start()
-    copy.wait()
-
-
-def leave_call(plan, frames):
-    return pl.pallas_call(
-        leave_kernel,
-        out_shape=jax.ShapeDtypeStruct((FRAMES, D), BF16),
-        in_specs=[SMEM(), ANY()],
-        out_specs=VMEM(),
-        scratch_shapes=[pltpu.SemaphoreType.DMA],
-        compiler_params=pltpu.CompilerParams(vmem_limit_bytes=WIDE),
-        cost_estimate=pl.CostEstimate(flops=0, bytes_accessed=2 * MIB, transcendentals=0),
-        name="leave",
-    )(plan, frames)
 
 
 def layer_norm(values, gain, shift):
@@ -191,8 +186,21 @@
     return [high, middle, low]
 
 
+def parity_rows():
+    rows = lax.broadcasted_iota(jnp.int32, (FRAMES, FRAMES), 0)
+    cols = lax.broadcasted_iota(jnp.int32, (FRAMES, FRAMES), 1)
+    picked = jnp.where(rows < HALF, 2 * rows, 2 * (rows - HALF) + 1)
+    return jnp.where(cols == picked, 1.0, 0.0).astype(BF16)
+
+
+def feature_select(start):
+    feature = lax.broadcasted_iota(jnp.int32, (D, 256), 0)
+    position = lax.broadcasted_iota(jnp.int32, (1, 256), 1) + start
+    return jnp.where(feature == feature_at(position), 1.0, 0.0).astype(BF16)
+
+
 def prepare_kernel(
-    plan, frames, far, near, gain, shift, post_gain, post_shift, order,
+    plan, frames, near, gain, shift, post_gain, post_shift,
     normed, residual, post, blocks, stack, sems,
 ):
     for g in range(CAP):
@@ -202,15 +210,11 @@
         def _():
             pltpu.make_async_copy(frames.at[source], blocks.at[g], sems.at[g]).start()
 
-        @pl.when(source == BLK_IN)
-        def _():
-            pltpu.make_async_copy(far, blocks.at[g], sems.at[g]).start()
-
         @pl.when(source == BLK_IN + 1)
         def _():
             pltpu.make_async_copy(near, blocks.at[g], sems.at[g]).start()
 
-        @pl.when(source < 0)
+        @pl.when((source < 0) | (source == BLK_IN))
         def _():
             blocks[g] = jnp.zeros((FRAMES, D), BF16)
 
@@ -223,14 +227,11 @@
     )
     for g in range(CAP):
 
-        @pl.when(plan[g] >= 0)
-        def _():
-            pltpu.make_async_copy(far, blocks.at[g], sems.at[g]).wait()
-
-    rows = lax.broadcasted_iota(jnp.int32, (FRAMES, FRAMES), 0)
-    cols = lax.broadcasted_iota(jnp.int32, (FRAMES, FRAMES), 1)
-    picked = jnp.where(rows < HALF, 2 * rows, 2 * (rows - HALF) + 1)
-    parity = jnp.where(cols == picked, 1.0, 0.0).astype(BF16)
+        @pl.when((plan[g] >= 0) & (plan[g] != BLK_IN))
+        def _():
+            pltpu.make_async_copy(near, blocks.at[g], sems.at[g]).wait()
+
+    parity = parity_rows()
     for g in range(CAP):
         sorted_rows = jnp.dot(parity, blocks[g], preferred_element_type=F32)
         done = layer_norm(sorted_rows, gain, shift).astype(BF16)
@@ -241,9 +242,7 @@
         parity, own, preferred_element_type=F32
     ).astype(BF16)
     for start in range(0, D, 256):
-        feature = lax.broadcasted_iota(jnp.int32, (D, 256), 0)
-        wanted = order[:, start : start + 256]
-        select = jnp.where(feature == wanted, 1.0, 0.0).astype(BF16)
+        select = feature_select(start)
         moved = jnp.dot(stack[...], select, preferred_element_type=F32)
         span = slice(start, start + 256)
         normed[:, span] = moved[:ROWS].astype(BF16)
@@ -255,7 +254,7 @@
         post[1:2, span] = tail[3:4] + (tail[4:5] + tail[5:6])
 
 
-def prepare_call(plan, frames, far, near, vectors, order):
+def prepare_call(plan, frames, near, vectors):
     return pl.pallas_call(
         prepare_kernel,
         out_shape=(
@@ -263,52 +262,88 @@
             jax.ShapeDtypeStruct((HALF, D), F32),
             jax.ShapeDtypeStruct((2, D), F32),
         ),
-        in_specs=[SMEM(), ANY(), ANY(), ANY()] + [VMEM()] * 5,
+        in_specs=[SMEM(), ANY(), ANY()] + [VMEM()] * 4,
         out_specs=(VMEM(), VMEM(), VMEM()),
         scratch_shapes=[
             pltpu.VMEM((CAP, FRAMES, D), BF16),
             pltpu.VMEM((ROWS + FRAMES + 16, D), BF16),
             pltpu.SemaphoreType.DMA((CAP,)),
         ],
-        compiler_params=pltpu.CompilerParams(vmem_limit_bytes=WIDE),
+        compiler_params=pltpu.CompilerParams(vmem_limit_bytes=24 * MIB),
         cost_estimate=pl.CostEstimate(
-            flops=8 * 656 * D * D, bytes_accessed=8 * MIB, transcendentals=0
+            flops=10**8, bytes_accessed=MIB, transcendentals=0
         ),
         name="prepare",
-    )(plan, frames, far, near, *vectors, order)
-
-
-def main_order(y, core):
-    return [(y + r) % NY for r in Y_ORDER]
-
-
-def proj_order(y, core):
-    first = jnp.where(core == 0, y ^ 1, y ^ 3)
-    second = jnp.where(core == 0, y ^ 3, y ^ 1)
-    return [y, first, second, y ^ 2]
-
-
-def slab_copies(order, mine, other, weights, sems):
-    core = lax.axis_index("core")
-    y = lax.axis_index("y")
-    copies = []
-    for i, (source, side) in enumerate(((mine, core), (other, 1 - core))):
-        for j, place in enumerate(order(y, side)):
-            row = pl.multiple_of((place * NC + side) * SLAB, 32)
-            copies.append(
-                pltpu.make_async_copy(
-                    source.at[pl.ds(j * SLAB, SLAB)],
-                    weights.at[pl.ds(row, SLAB)],
-                    sems.at[i * NY + j],
-                )
+    )(plan, frames, near, *vectors)
+
+
+def add_far_kernel(
+    plan, far, gain, shift, normed_in, residual_in, normed, residual,
+    stack, moved, pooled, sems,
+):
+    slot = jnp.int32(-1)
+    for g in range(CAP):
+        slot = jnp.where(plan[g] == BLK_IN, g, slot)
+    own = slot == lax.axis_index("section")
+
+    @pl.when(slot >= 0)
+    def _():
+        row = (1, D)
+        placed = jnp.dot(parity_rows(), far[...], preferred_element_type=F32)
+        done = layer_norm(placed, gain[...].reshape(row), shift[...].reshape(row))
+        stack[:FRAMES, :] = done.astype(BF16)
+        stack[FRAMES:, :] = placed.astype(BF16)
+        for start in range(0, D, 256):
+            span = slice(start, start + 256)
+            out = jnp.dot(stack[...], feature_select(start), preferred_element_type=F32)
+            moved[:, span] = out[:FRAMES].astype(BF16)
+            pooled[:, span] = 0.5 * (out[FRAMES : FRAMES + HALF] + out[FRAMES + HALF :])
+        copies = [
+            pltpu.make_async_copy(
+                moved.at[pl.ds(i * HALF, HALF)],
+                normed.at[pl.ds(pl.multiple_of(i * POOLED + slot * HALF, HALF), HALF)],
+                sems.at[i],
             )
-    return copies
-
-
-def attend_kernel(plan, normed, mine, other, terms, weights, sems):
-    copies = slab_copies(main_order, mine, other, weights, sems)
-    for copy in copies:
-        copy.start()
+            for i in range(2)
+        ]
+        for copy in copies:
+            copy.start()
+
+        @pl.when(own)
+        def _():
+            copy = pltpu.make_async_copy(pooled, residual, sems.at[2])
+            copy.start()
+            copy.wait()
+
+        for copy in copies:
+            copy.wait()
+
+
+def add_far_call(plan, far, gain, shift, normed, residual):
+    return pl.pallas_call(
+        add_far_kernel,
+        out_shape=(
+            jax.ShapeDtypeStruct((ROWS, D), BF16),
+            jax.ShapeDtypeStruct((HALF, D), F32),
+        ),
+        in_specs=[SMEM(), VMEM(), VMEM(), VMEM(), ANY(), ANY()],
+        out_specs=(ANY(), ANY()),
+        scratch_shapes=[
+            pltpu.VMEM((2 * FRAMES, D), BF16),
+            pltpu.VMEM((FRAMES, D), BF16),
+            pltpu.VMEM((HALF, D), F32),
+            pltpu.SemaphoreType.DMA((3,)),
+        ],
+        input_output_aliases={4: 0, 5: 1},
+        compiler_params=pltpu.CompilerParams(vmem_limit_bytes=24 * MIB),
+        cost_estimate=pl.CostEstimate(
+            flops=10**8, bytes_accessed=MIB, transcendentals=0
+        ),
+        name="add_far",
+    )(plan, far, gain, shift, normed, residual)
+
+
+def attend_kernel(plan, normed, mine, other, terms):
     slot_row = lax.broadcasted_iota(jnp.int32, (ROWS, 1), 0) % POOLED // HALF
     slot_col = lax.broadcasted_iota(jnp.int32, (1, ROWS), 1) % POOLED // HALF
     owner_row = jnp.full((ROWS, 1), -1, jnp.int32)
@@ -319,21 +354,22 @@
         owner_col = jnp.where(slot_col == g, owner, owner_col)
     same = owner_row == owner_col
     low = lax.broadcasted_iota(jnp.int32, (1, 128), 1) < HEAD
-    for copy in copies:
-        copy.wait()
-    x = normed[...]
+    left, right = normed[:, :HALF_D], normed[:, HALF_D:]
 
     def project(start, size):
-        return jnp.dot(x, weights[:, start : start + size], preferred_element_type=F32)
+        span = slice(start, start + size)
+        return jnp.dot(left, mine[:, span], preferred_element_type=F32) + jnp.dot(
+            right, other[:, span], preferred_element_type=F32
+        )
 
     def head(query, keyed, valued, use_low):
-        query = jnp.where(low == use_low, query, 0.0).astype(BF16)
+        query = jnp.where(low == use_low, query * HEAD ** (-0.5), 0.0).astype(BF16)
         scores = lax.dot_general(query, keyed, NT, preferred_element_type=F32)
-        scores = jnp.where(same, scores * HEAD ** (-0.5), NEG)
+        scores = jnp.where(same, scores, NEG)
         peak = jnp.max(scores, axis=1, keepdims=True)
         weight = jnp.exp(scores - peak)
         total = jnp.sum(weight, axis=1, keepdims=True)
-        weight = (weight / total).astype(BF16)
+        weight = (weight * (1.0 / total)).astype(BF16)
         out = jnp.dot(weight, valued, preferred_element_type=F32)
         return 0.5 * (out[:POOLED] + out[POOLED:])
 
@@ -354,27 +390,25 @@
     fifth = pltpu.roll(fifth, HEAD, 1)
     fifth = jnp.where(low, 0.0, fifth).astype(BF16)
     pooled = jnp.concatenate(pieces + [fifth], axis=1)
-    for start in range(0, D, 256):
-        rows = slice(start, start + 256)
-        out = lax.dot_general(
-            pooled[:, :256], weights[rows, 768:1024], NT, preferred_element_type=F32
-        ) + lax.dot_general(
-            pooled[:, 256:], weights[rows, 1152:1280], NT, preferred_element_type=F32
-        )
-        terms[:, rows] = out.astype(BF16)
+    for side, weights in enumerate((mine, other)):
+        for start in range(0, HALF_D, 128):
+            rows = slice(start, start + 128)
+            out = lax.dot_general(
+                pooled[:, :256], weights[rows, 768:1024], NT, preferred_element_type=F32
+            ) + lax.dot_general(
+                pooled[:, 256:], weights[rows, 1152:1280], NT, preferred_element_type=F32
+            )
+            start += side * HALF_D
+            terms[:, start : start + 128] = out.astype(BF16)
 
 
 def attend_call(plan, normed, mine, other):
     return pl.pallas_call(
         attend_kernel,
         out_shape=jax.ShapeDtypeStruct((POOLED, D), BF16),
-        in_specs=[SMEM(), VMEM(), ANY(), ANY()],
+        in_specs=[SMEM(), VMEM(), VMEM(), VMEM()],
         out_specs=VMEM(),
-        scratch_shapes=[
-            pltpu.VMEM((D, D), BF16),
-            pltpu.SemaphoreType.DMA((2 * NY,)),
-        ],
-        compiler_params=pltpu.CompilerParams(vmem_limit_bytes=48 * MIB),
+        compiler_params=pltpu.CompilerParams(vmem_limit_bytes=24 * MIB),
         cost_estimate=pl.CostEstimate(
             flops=3 * 10**9, bytes_accessed=8 * MIB, transcendentals=5 * ROWS * ROWS
         ),
@@ -400,17 +434,41 @@
     )(terms, residual, post)
 
 
+def slab_copies(mine, other, weights, sems):
+    core = lax.axis_index("core")
+    y = lax.axis_index("y")
+    copies = []
+    for side, source in enumerate((mine, other)):
+        swapped = (core + side) % NC
+        first = jnp.where(swapped == 0, y ^ 1, y ^ 3)
+        second = jnp.where(swapped == 0, y ^ 3, y ^ 1)
+        for j, place in enumerate((y, first, second, y ^ 2)):
+            row = side * HALF_D + y_step((place - y + NY) % NY) * SLAB
+            copies.append(
+                pltpu.make_async_copy(
+                    source.at[pl.ds(j * SLAB, SLAB)],
+                    weights.at[pl.ds(pl.multiple_of(row, 32), SLAB)],
+                    sems.at[side * NY + j],
+                )
+            )
+    return copies
+
+
 def project_kernel(plan, rows, mine, other, bias, out, weights, sems):
-    copies = slab_copies(proj_order, mine, other, weights, sems)
+    copies = slab_copies(mine, other, weights, sems)
     for copy in copies:
         copy.start()
+    slot = lax.broadcasted_iota(jnp.int32, (POOLED, 1), 0) // HALF
+    live = jnp.full((POOLED, 1), -1, jnp.int32)
+    for g in range(CAP):
+        live = jnp.where(slot == g, plan[CAP + g], live)
     for copy in copies:
         copy.wait()
-    for g in range(CAP):
-        span = slice(g * HALF, (g + 1) * HALF)
-        value = jnp.dot(rows[span, :], weights[...], preferred_element_type=F32)
-        value = value + bias[...]
-        out[span, :] = jnp.where(plan[CAP + g] >= 0, value, 0.0).astype(BF16)
+    for start in range(0, PROJ, 256):
+        span = slice(start, start + 256)
+        value = jnp.dot(rows[...], weights[:, span], preferred_element_type=F32)
+        value = value + bias[:, span]
+        out[:, span] = jnp.where(live >= 0, value, 0.0).astype(BF16)
 
 
 def project_call(plan, rows, mine, other, bias):
@@ -423,7 +481,7 @@
             pltpu.VMEM((D, PROJ), BF16),
             pltpu.SemaphoreType.DMA((2 * NY,)),
         ],
-        compiler_params=pltpu.CompilerParams(vmem_limit_bytes=48 * MIB),
+        compiler_params=pltpu.CompilerParams(vmem_limit_bytes=24 * MIB),
         cost_estimate=pl.CostEstimate(
             flops=2 * POOLED * D * PROJ, bytes_accessed=4 * MIB, transcendentals=0
         ),
@@ -464,28 +522,24 @@
     w_proj,
     proj_bias,
 ):
-    plan, packed, far = plan_call(
+    plan, packed, far, near = plan_call(
         block_utt, block_dest, frames, w_qkv, w_out, w_proj
-    )
-    odd = range(1, lax.axis_size(DP) - 1, 2)
-    far = lax.ppermute(
-        far, DP, [(i, i + 1) for i in odd] + [(i + 1, i) for i in odd]
     )
     gathered = lax.all_gather(packed, "z", axis=0, tiled=True)
     main, proj = unpack_call(gathered)
-    main, plan = lax.optimization_barrier((main, plan))
+    main, far, near = lax.optimization_barrier((main, far, near))
     mine = y_slabs(main)
-    near = other_core(leave_call(plan, frames))
-    order = feature_order(lax.axis_size("z"))
+    odd = range(1, lax.axis_size(DP) - 1, 2)
+    far = lax.ppermute(far, DP, [(i, i + 1) for i in odd] + [(i + 1, i) for i in odd])
+    near, proj = lax.optimization_barrier((other_core(near), proj))
+    proj_pair = jnp.concatenate([proj, y_swap(proj, (1, 3))], axis=0)
     vectors = (ln_gain, ln_shift, post_gain, post_shift)
-    normed, residual, post = prepare_call(plan, frames, far, near, vectors, order)
-    mine, normed, proj = lax.optimization_barrier((mine, normed, proj))
+    normed, residual, post = prepare_call(plan, frames, near, vectors)
+    normed, residual = add_far_call(plan, far, ln_gain, ln_shift, normed, residual)
+    mine, normed, proj_pair = lax.optimization_barrier((mine, normed, proj_pair))
     other = other_core(mine)
-    proj_pair = y_swap(proj, (1, 3))
+    proj_rest = y_swap(proj_pair, (3, 1))
     terms = attend_call(plan, normed, mine, other)
-    terms, proj_pair = lax.optimization_barrier((terms, proj_pair))
-    proj_pair = jnp.concatenate([proj, proj_pair], axis=0)
-    proj_rest = y_swap(proj_pair, (3, 1))
     terms = lax.all_to_all(terms, "section", split_axis=0, concat_axis=0, tiled=True)
     pooled_norm = finish_call(terms, residual, post)
     pooled_norm, proj_rest = lax.optimization_barrier((pooled_norm, proj_rest))

time: 147 us -> 129 us (0.88)
  the two profiles are of different devices: /device:TPU:8 before, /device:TPU:32 now
where the time goes in v3:
time: 129 us
  blocking collectives  62.4 us (48%)
  starting transfers between devices  31.9 us (25%)
  Pallas kernels  19 us (15%)
  waiting for transfers between devices  12.5 us (10%)
  local copies, waits for them, and re-layouts  2.7 us (2%)
    all_gather x1, blocking collectives, shards(): gathered = lax.all_gather(packed, 'z', axis=0, tiled=True)  37.9 us
    all_gather x1, blocking collectives, shards(): rows = lax.all_gather(pooled_norm, 'section', axis=0, tiled=True)  13.8 us
    all_to_all x1, waiting for transfers between devices, shards(): lax.all_to_all(terms, 'section', split_axis=0, concat_axis=0, tiled=True)  11.8 us
    ppermute x3, starting transfers between devices, y_slabs(): lax.ppermute(slab, 'y', [((i + r) % NY, i) for i in range(NY)])  10.9 us
    all_to_all x1, blocking collectives, shards(): lax.all_to_all(lm_local, 'section', split_axis=0, concat_axis=1, tiled=True)  10.6 us
    ppermute x1, starting transfers between devices, shards(): lax.ppermute(far, DP, [(i, i + 1) for i in odd] + [(i + 1, i) for i in odd])  6.3 us
    pallas_call x1, Pallas kernels, attend_call(): pl.pallas_call(attend_kernel, out_shape=jax.ShapeDtypeStruct((POOLED, D),...  6.15 us
    ppermute x3, starting transfers between devices, other_core(): return lax.ppermute(slabs, 'core', [(0, 1), (1, 0)])  5.76 us
  transfers between devices with their start and end apart: 10, of which 2 were waited for; matrix products, arithmetic and copies ran while one was open for 0% of the time, Pallas kernels for 10%

profile of v3, /device:TPU:32, one launch (start us, length us, event | category | flops | bytes accessed | tf_op | source)
XLA Modules:
  0.0 128.9 jit_solution(1234115381704583357)
XLA Ops:
  0.0 3.0 %plan.1 = (s32[8]{0:T(128)}, bf16[192,128]{1,0:T(8,128)(2,1)}, bf16[128,1280]{1,0:T(8,128)(2,1)}, bf16[128,1280]{1,0:T(8,128)(2,1)}) custom-call(s32[768]{0:T(1024)} %utt.1, s32[768]{0:T(1024)} %dest.1, bf16[6,128,1280]{2,1,0:T(8,128)(2,1)} %frames.3, bf16[10,3,320]{2,1,0:T(4,128)(2,1)} %bitcast.13, bf16[10,320]{1,0:T(8,128)(2,1)} %bitcast.14, ...), custom_call_target="tpu_custom_call" | custom-call | tf_op jit(solution)/shard_map/plan/pallas_call | solution.py:126
  3.0 37.9 %all_gather.6.gathered = bf16[3072,128]{1,0:T(8,128)(2,1)S(1)} all-gather(bf16[192,128]{1,0:T(8,128)(2,1)} %get-tuple-element.27), channel_id=1, replica_groups=mesh['z'=16,'y'=4,'core'=2,'section'=4] {'z'}, dimensions={0}, use_global_device_ids=true | all-gather | bytes 835584 | tf_op jit(solution)/shard_map/all_gather | solution.py:528
  40.9 0.3 unpack.1
  41.3 5.1 %collective-permute-start = (bf16[160,1280]{1,0:T(8,128)(2,1)S(1)}, bf16[160,1280]{1,0:T(8,128)(2,1)S(1)}, u32[]{:S(2)}, u32[]{:S(2)}) collective-permute-start(bf16[160,1280]{1,0:T(8,128)(2,1)S(1)} %get-tuple-element.31), channel_id=1, source_target_pairs={{16,0},{24,8},{0,16},{8,24},{17,1},{25,9},{1,17},{9,25},{18,2},{26... | collective-permute-start | bytes 1228808 | tf_op jit(solution)/shard_map/ppermute | solution.py:495
  46.4 3.0 %collective-permute-start.1 = (bf16[160,1280]{1,0:T(8,128)(2,1)S(1)}, bf16[160,1280]{1,0:T(8,128)(2,1)S(1)}, u32[]{:S(2)}, u32[]{:S(2)}) collective-permute-start(bf16[160,1280]{1,0:T(8,128)(2,1)S(1)} %get-tuple-element.31), channel_id=1, source_target_pairs={{8,0},{16,8},{24,16},{0,24},{9,1},{17,9},{25,17},{1,25},{10,2},{18... | collective-permute-start | bytes 1228808 | tf_op jit(solution)/shard_map/ppermute | solution.py:495
  49.4 2.9 %collective-permute-start.2 = (bf16[160,1280]{1,0:T(8,128)(2,1)S(1)}, bf16[160,1280]{1,0:T(8,128)(2,1)S(1)}, u32[]{:S(2)}, u32[]{:S(2)}) collective-permute-start(bf16[160,1280]{1,0:T(8,128)(2,1)S(1)} %get-tuple-element.31), channel_id=1, source_target_pairs={{24,0},{0,8},{8,16},{16,24},{25,1},{1,9},{9,17},{17,25},{26,2},{2,... | collective-permute-start | bytes 1228808 | tf_op jit(solution)/shard_map/ppermute | solution.py:495
  52.2 1.9 %collective-permute-start.4 = (bf16[128,1280]{1,0:T(8,128)(2,1)}, bf16[128,1280]{1,0:T(8,128)(2,1)S(1)}, u32[]{:S(2)}, u32[]{:S(2)}) collective-permute-start(bf16[128,1280]{1,0:T(8,128)(2,1)} %get-tuple-element.33), channel_id=1, source_target_pairs={{0,4},{4,0},{1,5},{5,1},{2,6},{6,2},{3,7},{7,3},{8,12},{12,8},{9,1... | collective-permute-start | bytes 983048 | tf_op jit(solution)/shard_map/ppermute | solution.py:509
  54.2 6.3 %collective-permute-start.3 = (bf16[128,1280]{1,0:T(8,128)(2,1)}, bf16[128,1280]{1,0:T(8,128)(2,1)S(1)}, u32[]{:S(2)}, u32[]{:S(2)}) collective-permute-start(bf16[128,1280]{1,0:T(8,128)(2,1)} %get-tuple-element.32), channel_id=1, source_target_pairs={{4,8},{12,16},{20,24},{28,32},{36,40},{44,48},{52,56},{60,64},{68,... | collective-permute-start | bytes 983048 | tf_op jit(solution)/shard_map/ppermute | solution.py:533
  60.5 1.9 %collective-permute-start.5 = (bf16[160,1024]{1,0:T(8,128)(2,1)S(1)}, bf16[160,1024]{1,0:T(8,128)(2,1)S(1)}, u32[]{:S(2)}, u32[]{:S(2)}) collective-permute-start(bf16[160,1024]{1,0:T(8,128)(2,1)S(1)} %get-tuple-element.39), channel_id=1, source_target_pairs={{0,8},{4,28},{8,0},{12,20},{16,24},{20,12},{24,16},{28,4},{1,9},{5... | collective-permute-start | bytes 983048 | tf_op jit(solution)/shard_map/ppermute | solution.py:505
  62.5 0.7 copy-done.5
  63.1 4.2 %prepare.1 = (bf16[512,1280]{1,0:T(8,128)(2,1)S(1)}, f32[64,1280]{1,0:T(8,128)S(1)}, f32[2,1280]{1,0:T(2,128)S(1)}) custom-call(s32[8]{0:T(128)S(1)} %copy-done.5, bf16[6,128,1280]{2,1,0:T(8,128)(2,1)S(1)} %copy-done, bf16[128,1280]{1,0:T(8,128)(2,1)S(1)} %collective-permute-done.4.near, f32[1280]{0:T(1024)S(1)} %copy-done.1, f32[1280]{0:T(1024)S(1)} %copy-done.2, ...), custom_call_target="tpu_custom_call" | custom-call | flops 100000000 | bytes 1048576 | tf_op jit(solution)/shard_map/prepare/pallas_call | solution.py:258
  67.3 2.7 %add_far.1 = (bf16[512,1280]{1,0:T(8,128)(2,1)S(1)}, f32[64,1280]{1,0:T(8,128)S(1)}) custom-call(s32[8]{0:T(128)S(1)} %copy-done.5, bf16[128,1280]{1,0:T(8,128)(2,1)S(1)} %collective-permute-done.3.far, f32[1280]{0:T(1024)S(1)} %copy-done.1, f32[1280]{0:T(1024)S(1)} %copy-done.2, ...), custom_call_target="tpu_custom_call", output_to_operand_aliasing={{0}: (4, {}), {1}: (5, {})} | custom-call | flops 100000000 | bytes 1048576 | tf_op jit(solution)/shard_map/add_far/pallas_call | solution.py:323
  70.3 1.9 %collective-permute-start.6 = (bf16[640,1280]{1,0:T(8,128)(2,1)S(1)}, bf16[640,1280]{1,0:T(8,128)(2,1)S(1)}, u32[]{:S(2)}, u32[]{:S(2)}) collective-permute-start(bf16[640,1280]{1,0:T(8,128)(2,1)S(1)} %pad_maximum_fusion.mine), channel_id=1, source_target_pairs={{0,4},{4,0},{1,5},{5,1},{2,6},{6,2},{3,7},{7,3},{8,12},{12,8},{9,1... | collective-permute-start | bytes 4915208 | tf_op jit(solution)/shard_map/ppermute | solution.py:509
  72.2 2.8 %collective-permute-start.7 = (bf16[320,1024]{1,0:T(8,128)(2,1)S(1)}, bf16[320,1024]{1,0:T(8,128)(2,1)}, u32[]{:S(2)}, u32[]{:S(2)}) collective-permute-start(bf16[320,1024]{1,0:T(8,128)(2,1)S(1)} %pad_maximum_fusion.1), channel_id=1, source_target_pairs={{0,24},{4,12},{8,16},{12,4},{16,8},{20,28},{24,0},{28,20},{1,25},{... | collective-permute-start | bytes 1966088 | tf_op jit(solution)/shard_map/ppermute | solution.py:505
  75.0 0.7 collective-permute-done.6.other
  75.7 6.2 %attend.1 = bf16[256,1280]{1,0:T(8,128)(2,1)} custom-call(s32[8]{0:T(128)S(1)} %copy-done.5, bf16[512,1280]{1,0:T(8,128)(2,1)S(1)} %get-tuple-element.40.normed, bf16[640,1280]{1,0:T(8,128)(2,1)S(1)} %pad_maximum_fusion.mine, bf16[640,1280]{1,0:T(8,128)(2,1)S(1)} %collective-permute-done.6.other), custom_call_target="tpu_custom_call" | custom-call | flops 3000000000 | bytes 8388608 | tf_op jit(solution)/shard_map/attend/pallas_call | solution.py:406
  81.9 4.2 %all-to-all-start = ((bf16[4,64,1280]{2,1,0:T(8,128)(2,1)}), bf16[4,64,1280]{2,1,0:T(8,128)(2,1)S(1)}, u32[]{:S(2)}, u32[]{:S(2)}) async-start(bf16[4,64,1280]{2,1,0:T(8,128)(2,1)} %bitcast.2), calls=%async_computation | async-start | bytes 1310720 | tf_op jit(solution)/shard_map/all_to_all | solution.py:543
  86.1 11.8 %all-to-all-done = bf16[4,64,1280]{2,1,0:T(8,128)(2,1)S(1)} async-done(((bf16[4,64,1280]{2,1,0:T(8,128)(2,1)}), bf16[4,64,1280]{2,1,0:T(8,128)(2,1)S(1)}, u32[]{:S(2)}, u32[]{:S(2)}) %all-to-all-start) | async-done | bytes 655392 | tf_op jit(solution)/shard_map/all_to_all | solution.py:543
  98.2 1.1 constant_dynamic-update-slice_fusion.mine
  99.3 1.9 %collective-permute-start.8 = (bf16[640,1024]{1,0:T(8,128)(2,1)S(1)}, bf16[640,1024]{1,0:T(8,128)(2,1)S(1)}, u32[]{:S(2)}, u32[]{:S(2)}) collective-permute-start(bf16[640,1024]{1,0:T(8,128)(2,1)S(1)} %constant_dynamic-update-slice_fusion.mine), channel_id=1, source_target_pairs={{0,4},{4,0},{1,5},{5,1},{2,6},{6,2},{3,7},{7,3},{8,12},{12,8},{9,1... | collective-permute-start | bytes 3932168 | tf_op jit(solution)/shard_map/ppermute | solution.py:509
  101.2 13.8 %all_gather.7.rows = bf16[256,1280]{1,0:T(8,128)(2,1)S(1)} all-gather(bf16[64,1280]{1,0:T(8,128)(2,1)S(1)} %finish.1), channel_id=1, replica_groups=mesh['z'=16,'y'=4,'core'=2,'section'=4] {'section'}, dimensions={0}, use_global_device_ids=true | all-gather | bytes 819200 | tf_op jit(solution)/shard_map/all_gather | solution.py:548
  115.1 2.4 %project.1 = bf16[256,1024]{1,0:T(8,128)(2,1)S(1)} custom-call(s32[8]{0:T(128)S(1)} %copy-done.6, bf16[256,1280]{1,0:T(8,128)(2,1)S(1)} %all_gather.7.rows, bf16[640,1024]{1,0:T(8,128)(2,1)S(1)} %constant_dynamic-update-slice_fusion.mine, bf16[640,1024]{1,0:T(8,128)(2,1)S(1)} %collective-permute-done.8.other, f32[1,1024]{1,0:T(1,128)S(1)} %bitcast.11), custom_call_target="tpu_custom_call" | custom-call | flops 671088640 | bytes 4194304 | tf_op jit(solution)/shard_map/project/pallas_call | solution.py:475
  117.5 10.6 %all_to_all.30 = bf16[4,64,1024]{2,1,0:T(8,128)(2,1)S(1)} all-to-all(bf16[4,64,1024]{2,1,0:T(8,128)(2,1)S(1)} %bitcast.10), channel_id=1, replica_groups=mesh['z'=16,'y'=4,'core'=2,'section'=4] {'section'}, dimensions={0} | all-to-all | bytes 1048576 | tf_op jit(solution)/shard_map/all_to_all | solution.py:551
  128.1 0.8 copy.15
  (27 shorter events, 0.5 us)
Async XLA Ops:
  0.0 62.4 %copy-start = (bf16[6,128,1280]{2,1,0:T(8,128)(2,1)S(1)}, bf16[6,128,1280]{2,1,0:T(8,128)(2,1)}, u32[]{:S(2)}) copy-start(bf16[6,128,1280]{2,1,0:T(8,128)(2,1)} %frames.3) | copy-start | bytes 5898244
  0.0 62.4 %copy-start.1 = (f32[1280]{0:T(1024)S(1)}, f32[1280]{0:T(1024)}, u32[]{:S(2)}) copy-start(f32[1280]{0:T(1024)} %gain.3) | copy-start | bytes 15364
  0.0 62.4 %copy-start.2 = (f32[1280]{0:T(1024)S(1)}, f32[1280]{0:T(1024)}, u32[]{:S(2)}) copy-start(f32[1280]{0:T(1024)} %shift.3) | copy-start | bytes 15364
  0.0 62.4 %copy-start.3 = (f32[1280]{0:T(1024)S(1)}, f32[1280]{0:T(1024)}, u32[]{:S(2)}) copy-start(f32[1280]{0:T(1024)} %post_gain.1) | copy-start | bytes 15364
  0.0 62.4 %copy-start.4 = (f32[1280]{0:T(1024)S(1)}, f32[1280]{0:T(1024)}, u32[]{:S(2)}) copy-start(f32[1280]{0:T(1024)} %post_shift.1) | copy-start | bytes 15364
  41.3 28.8 %collective-permute-start = (bf16[160,1280]{1,0:T(8,128)(2,1)S(1)}, bf16[160,1280]{1,0:T(8,128)(2,1)S(1)}, u32[]{:S(2)}, u32[]{:S(2)}) collective-permute-start(bf16[160,1280]{1,0:T(8,128)(2,1)S(1)} %get-tuple-element.31), channel_id=1, source_target_pairs={{16,0},{24,8},{0,16},{8,24},{17,1},{25,9},{1,17},{9,25},{18,2},{26... | collective-permute-start | bytes 1228808 | tf_op jit(solution)/shard_map/ppermute | solution.py:495
  46.4 23.7 %collective-permute-start.1 = (bf16[160,1280]{1,0:T(8,128)(2,1)S(1)}, bf16[160,1280]{1,0:T(8,128)(2,1)S(1)}, u32[]{:S(2)}, u32[]{:S(2)}) collective-permute-start(bf16[160,1280]{1,0:T(8,128)(2,1)S(1)} %get-tuple-element.31), channel_id=1, source_target_pairs={{8,0},{16,8},{24,16},{0,24},{9,1},{17,9},{25,17},{1,25},{10,2},{18... | collective-permute-start | bytes 1228808 | tf_op jit(solution)/shard_map/ppermute | solution.py:495
  49.4 20.8 %collective-permute-start.2 = (bf16[160,1280]{1,0:T(8,128)(2,1)S(1)}, bf16[160,1280]{1,0:T(8,128)(2,1)S(1)}, u32[]{:S(2)}, u32[]{:S(2)}) collective-permute-start(bf16[160,1280]{1,0:T(8,128)(2,1)S(1)} %get-tuple-element.31), channel_id=1, source_target_pairs={{24,0},{0,8},{8,16},{16,24},{25,1},{1,9},{9,17},{17,25},{26,2},{2,... | collective-permute-start | bytes 1228808 | tf_op jit(solution)/shard_map/ppermute | solution.py:495
  52.2 8.2 %collective-permute-start.4 = (bf16[128,1280]{1,0:T(8,128)(2,1)}, bf16[128,1280]{1,0:T(8,128)(2,1)S(1)}, u32[]{:S(2)}, u32[]{:S(2)}) collective-permute-start(bf16[128,1280]{1,0:T(8,128)(2,1)} %get-tuple-element.33), channel_id=1, source_target_pairs={{0,4},{4,0},{1,5},{5,1},{2,6},{6,2},{3,7},{7,3},{8,12},{12,8},{9,1... | collective-permute-start | bytes 983048 | tf_op jit(solution)/shard_map/ppermute | solution.py:509
  54.2 13.2 %collective-permute-start.3 = (bf16[128,1280]{1,0:T(8,128)(2,1)}, bf16[128,1280]{1,0:T(8,128)(2,1)S(1)}, u32[]{:S(2)}, u32[]{:S(2)}) collective-permute-start(bf16[128,1280]{1,0:T(8,128)(2,1)} %get-tuple-element.32), channel_id=1, source_target_pairs={{4,8},{12,16},{20,24},{28,32},{36,40},{44,48},{52,56},{60,64},{68,... | collective-permute-start | bytes 983048 | tf_op jit(solution)/shard_map/ppermute | solution.py:533
  60.5 9.8 %collective-permute-start.5 = (bf16[160,1024]{1,0:T(8,128)(2,1)S(1)}, bf16[160,1024]{1,0:T(8,128)(2,1)S(1)}, u32[]{:S(2)}, u32[]{:S(2)}) collective-permute-start(bf16[160,1024]{1,0:T(8,128)(2,1)S(1)} %get-tuple-element.39), channel_id=1, source_target_pairs={{0,8},{4,28},{8,0},{12,20},{16,24},{20,12},{24,16},{28,4},{1,9},{5... | collective-permute-start | bytes 983048 | tf_op jit(solution)/shard_map/ppermute | solution.py:505
  62.5 0.7 copy-start.5
  70.3 5.4 %collective-permute-start.6 = (bf16[640,1280]{1,0:T(8,128)(2,1)S(1)}, bf16[640,1280]{1,0:T(8,128)(2,1)S(1)}, u32[]{:S(2)}, u32[]{:S(2)}) collective-permute-start(bf16[640,1280]{1,0:T(8,128)(2,1)S(1)} %pad_maximum_fusion.mine), channel_id=1, source_target_pairs={{0,4},{4,0},{1,5},{5,1},{2,6},{6,2},{3,7},{7,3},{8,12},{12,8},{9,1... | collective-permute-start | bytes 4915208 | tf_op jit(solution)/shard_map/ppermute | solution.py:509
  72.2 25.9 %collective-permute-start.7 = (bf16[320,1024]{1,0:T(8,128)(2,1)S(1)}, bf16[320,1024]{1,0:T(8,128)(2,1)}, u32[]{:S(2)}, u32[]{:S(2)}) collective-permute-start(bf16[320,1024]{1,0:T(8,128)(2,1)S(1)} %pad_maximum_fusion.1), channel_id=1, source_target_pairs={{0,24},{4,12},{8,16},{12,4},{16,8},{20,28},{24,0},{28,20},{1,25},{... | collective-permute-start | bytes 1966088 | tf_op jit(solution)/shard_map/ppermute | solution.py:505
  81.9 16.0 %all-to-all-start = ((bf16[4,64,1280]{2,1,0:T(8,128)(2,1)}), bf16[4,64,1280]{2,1,0:T(8,128)(2,1)S(1)}, u32[]{:S(2)}, u32[]{:S(2)}) async-start(bf16[4,64,1280]{2,1,0:T(8,128)(2,1)} %bitcast.2), calls=%async_computation | async-start | bytes 1310720 | tf_op jit(solution)/shard_map/all_to_all | solution.py:543
  97.9 17.2 %copy-start.6 = (s32[8]{0:T(128)S(1)}, s32[8]{0:T(128)}, u32[]{:S(2)}) copy-start(s32[8]{0:T(128)} %get-tuple-element.26.plan) | copy-start | bytes 100
  97.9 17.2 %copy-start.7 = (f32[1024]{0:T(1024)S(1)}, f32[1024]{0:T(1024)}, u32[]{:S(2)}) copy-start(f32[1024]{0:T(1024)} %param.21) | copy-start | bytes 12292
  99.3 15.8 %collective-permute-start.8 = (bf16[640,1024]{1,0:T(8,128)(2,1)S(1)}, bf16[640,1024]{1,0:T(8,128)(2,1)S(1)}, u32[]{:S(2)}, u32[]{:S(2)}) collective-permute-start(bf16[640,1024]{1,0:T(8,128)(2,1)S(1)} %constant_dynamic-update-slice_fusion.mine), channel_id=1, source_target_pairs={{0,4},{4,0},{1,5},{5,1},{2,6},{6,2},{3,7},{7,3},{8,12},{12,8},{9,1... | collective-permute-start | bytes 3932168 | tf_op jit(solution)/shard_map/ppermute | solution.py:509

commit v4 on v3

--- a/solution.py
+++ b/solution.py
@@ -16,7 +16,6 @@
 PROJ = 1024
 NY = 4
 NC = 2
-Y_ORDER = (0, 2, 1, 3)
 K_DEV = 10
 TILES = 18
 PACKED = 192
@@ -44,14 +43,11 @@
     return (lax.axis_index("z") * NY + lax.axis_index("y")) * NC + lax.axis_index("core")
 
 
-def y_step(index):
-    return jnp.where(index == 1, 2, jnp.where(index == 2, 1, index))
-
-
 def feature_at(position):
     side, rest = position // HALF_D, position % HALF_D
-    place = (lax.axis_index("y") + y_step(rest // SLAB)) % NY
     core = (lax.axis_index("core") + side) % NC
+    steps = jnp.where(core == 0, rest // SLAB, NY - rest // SLAB)
+    place = (lax.axis_index("y") + steps) % NY
     rest = rest % SLAB
     owner = (rest // K_DEV * NY + place) * NC + core
     return owner * K_DEV + rest % K_DEV
@@ -434,39 +430,17 @@
     )(terms, residual, post)
 
 
-def slab_copies(mine, other, weights, sems):
-    core = lax.axis_index("core")
-    y = lax.axis_index("y")
-    copies = []
-    for side, source in enumerate((mine, other)):
-        swapped = (core + side) % NC
-        first = jnp.where(swapped == 0, y ^ 1, y ^ 3)
-        second = jnp.where(swapped == 0, y ^ 3, y ^ 1)
-        for j, place in enumerate((y, first, second, y ^ 2)):
-            row = side * HALF_D + y_step((place - y + NY) % NY) * SLAB
-            copies.append(
-                pltpu.make_async_copy(
-                    source.at[pl.ds(j * SLAB, SLAB)],
-                    weights.at[pl.ds(pl.multiple_of(row, 32), SLAB)],
-                    sems.at[side * NY + j],
-                )
-            )
-    return copies
-
-
-def project_kernel(plan, rows, mine, other, bias, out, weights, sems):
-    copies = slab_copies(mine, other, weights, sems)
-    for copy in copies:
-        copy.start()
+def project_kernel(plan, rows, mine, other, bias, out):
     slot = lax.broadcasted_iota(jnp.int32, (POOLED, 1), 0) // HALF
     live = jnp.full((POOLED, 1), -1, jnp.int32)
     for g in range(CAP):
         live = jnp.where(slot == g, plan[CAP + g], live)
-    for copy in copies:
-        copy.wait()
+    left, right = rows[:, :HALF_D], rows[:, HALF_D:]
     for start in range(0, PROJ, 256):
         span = slice(start, start + 256)
-        value = jnp.dot(rows[...], weights[:, span], preferred_element_type=F32)
+        value = jnp.dot(left, mine[:, span], preferred_element_type=F32) + jnp.dot(
+            right, other[:, span], preferred_element_type=F32
+        )
         value = value + bias[:, span]
         out[:, span] = jnp.where(live >= 0, value, 0.0).astype(BF16)
 
@@ -475,12 +449,8 @@
     return pl.pallas_call(
         project_kernel,
         out_shape=jax.ShapeDtypeStruct((POOLED, PROJ), BF16),
-        in_specs=[SMEM(), VMEM(), ANY(), ANY(), VMEM()],
+        in_specs=[SMEM(), VMEM(), VMEM(), VMEM(), VMEM()],
         out_specs=VMEM(),
-        scratch_shapes=[
-            pltpu.VMEM((D, PROJ), BF16),
-            pltpu.SemaphoreType.DMA((2 * NY,)),
-        ],
         compiler_params=pltpu.CompilerParams(vmem_limit_bytes=24 * MIB),
         cost_estimate=pl.CostEstimate(
             flops=2 * POOLED * D * PROJ, bytes_accessed=4 * MIB, transcendentals=0
@@ -489,16 +459,9 @@
     )(plan, rows, mine, other, bias)
 
 
-def y_slabs(slab):
-    slabs = [slab]
-    for r in Y_ORDER[1:]:
-        slabs.append(lax.ppermute(slab, "y", [((i + r) % NY, i) for i in range(NY)]))
-    return jnp.concatenate(slabs, axis=0)
-
-
-def y_swap(slabs, masks):
+def y_shift(slabs, steps):
     pairs = [
-        (y * NC + core, (y ^ masks[core]) * NC + core)
+        ((y + (NY - steps if core else steps)) % NY * NC + core, y * NC + core)
         for y in range(NY)
         for core in range(NC)
     ]
@@ -528,21 +491,24 @@
     gathered = lax.all_gather(packed, "z", axis=0, tiled=True)
     main, proj = unpack_call(gathered)
     main, far, near = lax.optimization_barrier((main, far, near))
-    mine = y_slabs(main)
+    slabs = {steps: y_shift(main, steps) for steps in (2, 1, 3)}
+    mine = jnp.concatenate([main, slabs[1], slabs[2], slabs[3]], axis=0)
     odd = range(1, lax.axis_size(DP) - 1, 2)
     far = lax.ppermute(far, DP, [(i, i + 1) for i in odd] + [(i + 1, i) for i in odd])
     near, proj = lax.optimization_barrier((other_core(near), proj))
-    proj_pair = jnp.concatenate([proj, y_swap(proj, (1, 3))], axis=0)
+    proj_pair = jnp.concatenate([proj, y_shift(proj, 1)], axis=0)
     vectors = (ln_gain, ln_shift, post_gain, post_shift)
     normed, residual, post = prepare_call(plan, frames, near, vectors)
     normed, residual = add_far_call(plan, far, ln_gain, ln_shift, normed, residual)
     mine, normed, proj_pair = lax.optimization_barrier((mine, normed, proj_pair))
     other = other_core(mine)
-    proj_rest = y_swap(proj_pair, (3, 1))
+    proj_rest = y_shift(proj_pair, 2)
     terms = attend_call(plan, normed, mine, other)
     terms = lax.all_to_all(terms, "section", split_axis=0, concat_axis=0, tiled=True)
     pooled_norm = finish_call(terms, residual, post)
-    pooled_norm, proj_rest = lax.optimization_barrier((pooled_norm, proj_rest))
+    pooled_norm, proj_pair, proj_rest = lax.optimization_barrier(
+        (pooled_norm, proj_pair, proj_rest)
+    )
     proj_mine = jnp.concatenate([proj_pair, proj_rest], axis=0)
     proj_other = other_core(proj_mine)
     rows = lax.all_gather(pooled_norm, "section", axis=0, tiled=True)

time: 129 us -> 127 us (0.984)
  the two profiles are of different devices: /device:TPU:32 before, /device:TPU:8 now
where the time goes in v4:
time: 127 us; the launch traced here: 126 us
  blocking collectives  80.2 us (63%)
  starting transfers between devices  24.5 us (19%)
  Pallas kernels  17.4 us (14%)
  waiting for transfers between devices  2.06 us (2%)
  local copies, waits for them, and re-layouts  1.55 us (1%)
    all_gather x1, blocking collectives, shards(): gathered = lax.all_gather(packed, 'z', axis=0, tiled=True)  40.4 us
    ppermute x5, starting transfers between devices, y_shift(): return lax.ppermute(slabs, ('y', 'core'), pairs)  16.6 us
    all_to_all x1, blocking collectives, shards(): lax.all_to_all(terms, 'section', split_axis=0, concat_axis=0, tiled=True)  15.4 us
    all_gather x1, blocking collectives, shards(): rows = lax.all_gather(pooled_norm, 'section', axis=0, tiled=True)  13.8 us
    all_to_all x1, blocking collectives, shards(): lax.all_to_all(lm_local, 'section', split_axis=0, concat_axis=1, tiled=True)  10.6 us
    ppermute x3, starting transfers between devices, other_core(): return lax.ppermute(slabs, 'core', [(0, 1), (1, 0)])  5.76 us
    pallas_call x1, Pallas kernels, attend_call(): pl.pallas_call(attend_kernel, out_shape=jax.ShapeDtypeStruct((POOLED, D),...  5.31 us
    pallas_call x1, Pallas kernels, prepare_call(): pl.pallas_call(prepare_kernel, out_shape=(jax.ShapeDtypeStruct((ROWS, D),...  4.26 us
  transfers between devices with their start and end apart: 9, of which 2 were waited for; matrix products, arithmetic and copies ran while one was open for 0% of the time, Pallas kernels for 10%

profile of v4, /device:TPU:8, one launch (start us, length us, event | category | flops | bytes accessed | tf_op | source)
XLA Modules:
  0.0 126.3 jit_solution(13271487514515434822)
XLA Ops:
  0.0 3.0 %plan.1 = (s32[8]{0:T(128)}, bf16[192,128]{1,0:T(8,128)(2,1)}, bf16[128,1280]{1,0:T(8,128)(2,1)}, bf16[128,1280]{1,0:T(8,128)(2,1)}) custom-call(s32[768]{0:T(1024)} %utt.1, s32[768]{0:T(1024)} %dest.1, bf16[6,128,1280]{2,1,0:T(8,128)(2,1)} %frames.3, bf16[10,3,320]{2,1,0:T(4,128)(2,1)} %bitcast.14, bf16[10,320]{1,0:T(8,128)(2,1)} %bitcast.15, ...), custom_call_target="tpu_custom_call" | custom-call | tf_op jit(solution)/shard_map/plan/pallas_call | solution.py:122
  3.0 40.4 %all_gather.6.gathered = bf16[3072,128]{1,0:T(8,128)(2,1)S(1)} all-gather(bf16[192,128]{1,0:T(8,128)(2,1)} %get-tuple-element.28), channel_id=1, replica_groups=mesh['z'=16,'y'=4,'core'=2,'section'=4] {'z'}, dimensions={0}, use_global_device_ids=true | all-gather | bytes 835584 | tf_op jit(solution)/shard_map/all_gather | solution.py:491
  43.4 0.3 unpack.1
  43.8 2.4 %collective-permute-start = (bf16[160,1280]{1,0:T(8,128)(2,1)S(1)}, bf16[160,1280]{1,0:T(8,128)(2,1)S(1)}, u32[]{:S(2)}, u32[]{:S(2)}) collective-permute-start(bf16[160,1280]{1,0:T(8,128)(2,1)S(1)} %get-tuple-element.32), channel_id=1, source_target_pairs={{8,0},{28,4},{16,8},{4,12},{24,16},{12,20},{0,24},{20,28},{9,1},{2... | collective-permute-start | bytes 1228808 | tf_op jit(solution)/shard_map/ppermute | solution.py:468
  46.1 4.5 %collective-permute-start.1 = (bf16[160,1280]{1,0:T(8,128)(2,1)S(1)}, bf16[160,1280]{1,0:T(8,128)(2,1)S(1)}, u32[]{:S(2)}, u32[]{:S(2)}) collective-permute-start(bf16[160,1280]{1,0:T(8,128)(2,1)S(1)} %get-tuple-element.32), channel_id=1, source_target_pairs={{16,0},{20,4},{24,8},{28,12},{0,16},{4,20},{8,24},{12,28},{17,1},{... | collective-permute-start | bytes 1228808 | tf_op jit(solution)/shard_map/ppermute | solution.py:468
  50.6 3.8 %collective-permute-start.2 = (bf16[160,1280]{1,0:T(8,128)(2,1)S(1)}, bf16[160,1280]{1,0:T(8,128)(2,1)S(1)}, u32[]{:S(2)}, u32[]{:S(2)}) collective-permute-start(bf16[160,1280]{1,0:T(8,128)(2,1)S(1)} %get-tuple-element.32), channel_id=1, source_target_pairs={{24,0},{12,4},{0,8},{20,12},{8,16},{28,20},{16,24},{4,28},{25,1},{... | collective-permute-start | bytes 1228808 | tf_op jit(solution)/shard_map/ppermute | solution.py:468
  54.4 1.9 %collective-permute-start.4 = (bf16[128,1280]{1,0:T(8,128)(2,1)}, bf16[128,1280]{1,0:T(8,128)(2,1)S(1)}, u32[]{:S(2)}, u32[]{:S(2)}) collective-permute-start(bf16[128,1280]{1,0:T(8,128)(2,1)} %get-tuple-element.34), channel_id=1, source_target_pairs={{0,4},{4,0},{1,5},{5,1},{2,6},{6,2},{3,7},{7,3},{8,12},{12,8},{9,1... | collective-permute-start | bytes 983048 | tf_op jit(solution)/shard_map/ppermute | solution.py:472
  56.4 2.1 %collective-permute-start.3 = (bf16[128,1280]{1,0:T(8,128)(2,1)}, bf16[128,1280]{1,0:T(8,128)(2,1)S(1)}, u32[]{:S(2)}, u32[]{:S(2)}) collective-permute-start(bf16[128,1280]{1,0:T(8,128)(2,1)} %get-tuple-element.33), channel_id=1, source_target_pairs={{4,8},{12,16},{20,24},{28,32},{36,40},{44,48},{52,56},{60,64},{68,... | collective-permute-start | bytes 983048 | tf_op jit(solution)/shard_map/ppermute | solution.py:497
  58.5 1.9 %collective-permute-start.5 = (bf16[160,1024]{1,0:T(8,128)(2,1)S(1)}, bf16[160,1024]{1,0:T(8,128)(2,1)S(1)}, u32[]{:S(2)}, u32[]{:S(2)}) collective-permute-start(bf16[160,1024]{1,0:T(8,128)(2,1)S(1)} %get-tuple-element.40), channel_id=1, source_target_pairs={{8,0},{28,4},{16,8},{4,12},{24,16},{12,20},{0,24},{20,28},{9,1},{2... | collective-permute-start | bytes 983048 | tf_op jit(solution)/shard_map/ppermute | solution.py:468
  60.5 0.6 copy-done.5
  61.1 4.3 %prepare.1 = (bf16[512,1280]{1,0:T(8,128)(2,1)S(1)}, f32[64,1280]{1,0:T(8,128)S(1)}, f32[2,1280]{1,0:T(2,128)S(1)}) custom-call(s32[8]{0:T(128)S(1)} %copy-done.5, bf16[6,128,1280]{2,1,0:T(8,128)(2,1)S(1)} %copy-done, bf16[128,1280]{1,0:T(8,128)(2,1)S(1)} %collective-permute-done.4.near, f32[1280]{0:T(1024)S(1)} %copy-done.1, f32[1280]{0:T(1024)S(1)} %copy-done.2, ...), custom_call_target="tpu_custom_call" | custom-call | flops 100000000 | bytes 1048576 | tf_op jit(solution)/shard_map/prepare/pallas_call | solution.py:254
  65.5 2.8 %add_far.1 = (bf16[512,1280]{1,0:T(8,128)(2,1)S(1)}, f32[64,1280]{1,0:T(8,128)S(1)}) custom-call(s32[8]{0:T(128)S(1)} %copy-done.5, bf16[128,1280]{1,0:T(8,128)(2,1)S(1)} %collective-permute-done.3.far, f32[1280]{0:T(1024)S(1)} %copy-done.1, f32[1280]{0:T(1024)S(1)} %copy-done.2, ...), custom_call_target="tpu_custom_call", output_to_operand_aliasing={{0}: (4, {}), {1}: (5, {})} | custom-call | flops 100000000 | bytes 1048576 | tf_op jit(solution)/shard_map/add_far/pallas_call | solution.py:319
  68.3 0.1 pad_maximum_fusion.mine
  68.4 1.9 %collective-permute-done.5 = bf16[160,1024]{1,0:T(8,128)(2,1)S(1)} collective-permute-done((bf16[160,1024]{1,0:T(8,128)(2,1)S(1)}, bf16[160,1024]{1,0:T(8,128)(2,1)S(1)}, u32[]{:S(2)}, u32[]{:S(2)}) %collective-permute-start.5) | collective-permute-done | bytes 327712 | tf_op jit(solution)/shard_map/ppermute | solution.py:468
  70.4 1.9 %collective-permute-start.6 = (bf16[640,1280]{1,0:T(8,128)(2,1)S(1)}, bf16[640,1280]{1,0:T(8,128)(2,1)S(1)}, u32[]{:S(2)}, u32[]{:S(2)}) collective-permute-start(bf16[640,1280]{1,0:T(8,128)(2,1)S(1)} %pad_maximum_fusion.mine), channel_id=1, source_target_pairs={{0,4},{4,0},{1,5},{5,1},{2,6},{6,2},{3,7},{7,3},{8,12},{12,8},{9,1... | collective-permute-start | bytes 4915208 | tf_op jit(solution)/shard_map/ppermute | solution.py:472
  72.3 4.0 %collective-permute-start.7 = (bf16[320,1024]{1,0:T(8,128)(2,1)S(1)}, bf16[320,1024]{1,0:T(8,128)(2,1)S(1)}, u32[]{:S(2)}, u32[]{:S(2)}) collective-permute-start(bf16[320,1024]{1,0:T(8,128)(2,1)S(1)} %pad_maximum_fusion.1), channel_id=1, source_target_pairs={{16,0},{20,4},{24,8},{28,12},{0,16},{4,20},{8,24},{12,28},{17,1},{... | collective-permute-start | bytes 1966088 | tf_op jit(solution)/shard_map/ppermute | solution.py:468
  76.4 5.3 %attend.1 = bf16[256,1280]{1,0:T(8,128)(2,1)S(1)} custom-call(s32[8]{0:T(128)S(1)} %copy-done.5, bf16[512,1280]{1,0:T(8,128)(2,1)S(1)} %get-tuple-element.41.normed, bf16[640,1280]{1,0:T(8,128)(2,1)S(1)} %pad_maximum_fusion.mine, bf16[640,1280]{1,0:T(8,128)(2,1)S(1)} %collective-permute-done.6.other), custom_call_target="tpu_custom_call" | custom-call | flops 3000000000 | bytes 8388608 | tf_op jit(solution)/shard_map/attend/pallas_call | solution.py:402
  81.7 15.4 %all_to_all.30 = bf16[4,64,1280]{2,1,0:T(8,128)(2,1)S(1)} all-to-all(bf16[4,64,1280]{2,1,0:T(8,128)(2,1)S(1)} %bitcast.11), channel_id=1, replica_groups=mesh['z'=16,'y'=4,'core'=2,'section'=4] {'section'}, dimensions={0} | all-to-all | bytes 1310720 | tf_op jit(solution)/shard_map/all_to_all | solution.py:507
  97.1 0.3 finish.1
  97.5 1.9 %collective-permute-start.8 = (bf16[640,1024]{1,0:T(8,128)(2,1)S(1)}, bf16[640,1024]{1,0:T(8,128)(2,1)S(1)}, u32[]{:S(2)}, u32[]{:S(2)}) collective-permute-start(bf16[640,1024]{1,0:T(8,128)(2,1)S(1)} %constant_dynamic-update-slice_fusion.mine), channel_id=1, source_target_pairs={{0,4},{4,0},{1,5},{5,1},{2,6},{6,2},{3,7},{7,3},{8,12},{12,8},{9,1... | collective-permute-start | bytes 3932168 | tf_op jit(solution)/shard_map/ppermute | solution.py:472
  99.4 13.8 %all_gather.7.rows = bf16[256,1280]{1,0:T(8,128)(2,1)S(1)} all-gather(bf16[64,1280]{1,0:T(8,128)(2,1)S(1)} %finish.1), channel_id=1, replica_groups=mesh['z'=16,'y'=4,'core'=2,'section'=4] {'section'}, dimensions={0}, use_global_device_ids=true | all-gather | bytes 819200 | tf_op jit(solution)/shard_map/all_gather | solution.py:514
  113.3 1.5 %project.1 = bf16[256,1024]{1,0:T(8,128)(2,1)S(1)} custom-call(s32[8]{0:T(128)S(1)} %copy-done.5, bf16[256,1280]{1,0:T(8,128)(2,1)S(1)} %all_gather.7.rows, bf16[640,1024]{1,0:T(8,128)(2,1)S(1)} %constant_dynamic-update-slice_fusion.mine, bf16[640,1024]{1,0:T(8,128)(2,1)S(1)} %collective-permute-done.8.other, f32[1,1024]{1,0:T(1,128)S(1)} %bitcast.12), custom_call_target="tpu_custom_call" | custom-call | flops 671088640 | bytes 4194304 | tf_op jit(solution)/shard_map/project/pallas_call | solution.py:449
  114.8 10.6 %all_to_all.31 = bf16[4,64,1024]{2,1,0:T(8,128)(2,1)S(1)} all-to-all(bf16[4,64,1024]{2,1,0:T(8,128)(2,1)S(1)} %bitcast.10), channel_id=1, replica_groups=mesh['z'=16,'y'=4,'core'=2,'section'=4] {'section'}, dimensions={0} | all-to-all | bytes 1048576 | tf_op jit(solution)/shard_map/all_to_all | solution.py:517
  125.4 0.8 copy.15
  (24 shorter events, 0.3 us)
Async XLA Ops:
  0.0 60.5 %copy-start = (bf16[6,128,1280]{2,1,0:T(8,128)(2,1)S(1)}, bf16[6,128,1280]{2,1,0:T(8,128)(2,1)}, u32[]{:S(2)}) copy-start(bf16[6,128,1280]{2,1,0:T(8,128)(2,1)} %frames.3) | copy-start | bytes 5898244
  0.0 60.5 %copy-start.1 = (f32[1280]{0:T(1024)S(1)}, f32[1280]{0:T(1024)}, u32[]{:S(2)}) copy-start(f32[1280]{0:T(1024)} %gain.3) | copy-start | bytes 15364
  0.0 60.5 %copy-start.2 = (f32[1280]{0:T(1024)S(1)}, f32[1280]{0:T(1024)}, u32[]{:S(2)}) copy-start(f32[1280]{0:T(1024)} %shift.3) | copy-start | bytes 15364
  0.0 60.5 %copy-start.3 = (f32[1280]{0:T(1024)S(1)}, f32[1280]{0:T(1024)}, u32[]{:S(2)}) copy-start(f32[1280]{0:T(1024)} %post_gain.1) | copy-start | bytes 15364
  0.0 60.5 %copy-start.4 = (f32[1280]{0:T(1024)S(1)}, f32[1280]{0:T(1024)}, u32[]{:S(2)}) copy-start(f32[1280]{0:T(1024)} %post_shift.1) | copy-start | bytes 15364
  43.8 24.5 %collective-permute-start = (bf16[160,1280]{1,0:T(8,128)(2,1)S(1)}, bf16[160,1280]{1,0:T(8,128)(2,1)S(1)}, u32[]{:S(2)}, u32[]{:S(2)}) collective-permute-start(bf16[160,1280]{1,0:T(8,128)(2,1)S(1)} %get-tuple-element.32), channel_id=1, source_target_pairs={{8,0},{28,4},{16,8},{4,12},{24,16},{12,20},{0,24},{20,28},{9,1},{2... | collective-permute-start | bytes 1228808 | tf_op jit(solution)/shard_map/ppermute | solution.py:468
  46.1 22.2 %collective-permute-start.1 = (bf16[160,1280]{1,0:T(8,128)(2,1)S(1)}, bf16[160,1280]{1,0:T(8,128)(2,1)S(1)}, u32[]{:S(2)}, u32[]{:S(2)}) collective-permute-start(bf16[160,1280]{1,0:T(8,128)(2,1)S(1)} %get-tuple-element.32), channel_id=1, source_target_pairs={{16,0},{20,4},{24,8},{28,12},{0,16},{4,20},{8,24},{12,28},{17,1},{... | collective-permute-start | bytes 1228808 | tf_op jit(solution)/shard_map/ppermute | solution.py:468
  50.6 17.7 %collective-permute-start.2 = (bf16[160,1280]{1,0:T(8,128)(2,1)S(1)}, bf16[160,1280]{1,0:T(8,128)(2,1)S(1)}, u32[]{:S(2)}, u32[]{:S(2)}) collective-permute-start(bf16[160,1280]{1,0:T(8,128)(2,1)S(1)} %get-tuple-element.32), channel_id=1, source_target_pairs={{24,0},{12,4},{0,8},{20,12},{8,16},{28,20},{16,24},{4,28},{25,1},{... | collective-permute-start | bytes 1228808 | tf_op jit(solution)/shard_map/ppermute | solution.py:468
  54.4 4.1 %collective-permute-start.4 = (bf16[128,1280]{1,0:T(8,128)(2,1)}, bf16[128,1280]{1,0:T(8,128)(2,1)S(1)}, u32[]{:S(2)}, u32[]{:S(2)}) collective-permute-start(bf16[128,1280]{1,0:T(8,128)(2,1)} %get-tuple-element.34), channel_id=1, source_target_pairs={{0,4},{4,0},{1,5},{5,1},{2,6},{6,2},{3,7},{7,3},{8,12},{12,8},{9,1... | collective-permute-start | bytes 983048 | tf_op jit(solution)/shard_map/ppermute | solution.py:472
  56.4 9.1 %collective-permute-start.3 = (bf16[128,1280]{1,0:T(8,128)(2,1)}, bf16[128,1280]{1,0:T(8,128)(2,1)S(1)}, u32[]{:S(2)}, u32[]{:S(2)}) collective-permute-start(bf16[128,1280]{1,0:T(8,128)(2,1)} %get-tuple-element.33), channel_id=1, source_target_pairs={{4,8},{12,16},{20,24},{28,32},{36,40},{44,48},{52,56},{60,64},{68,... | collective-permute-start | bytes 983048 | tf_op jit(solution)/shard_map/ppermute | solution.py:497
  58.5 11.8 %collective-permute-start.5 = (bf16[160,1024]{1,0:T(8,128)(2,1)S(1)}, bf16[160,1024]{1,0:T(8,128)(2,1)S(1)}, u32[]{:S(2)}, u32[]{:S(2)}) collective-permute-start(bf16[160,1024]{1,0:T(8,128)(2,1)S(1)} %get-tuple-element.40), channel_id=1, source_target_pairs={{8,0},{28,4},{16,8},{4,12},{24,16},{12,20},{0,24},{20,28},{9,1},{2... | collective-permute-start | bytes 983048 | tf_op jit(solution)/shard_map/ppermute | solution.py:468
  60.5 0.6 copy-start.5
  70.4 6.0 %collective-permute-start.6 = (bf16[640,1280]{1,0:T(8,128)(2,1)S(1)}, bf16[640,1280]{1,0:T(8,128)(2,1)S(1)}, u32[]{:S(2)}, u32[]{:S(2)}) collective-permute-start(bf16[640,1280]{1,0:T(8,128)(2,1)S(1)} %pad_maximum_fusion.mine), channel_id=1, source_target_pairs={{0,4},{4,0},{1,5},{5,1},{2,6},{6,2},{3,7},{7,3},{8,12},{12,8},{9,1... | collective-permute-start | bytes 4915208 | tf_op jit(solution)/shard_map/ppermute | solution.py:472
  72.3 25.0 %collective-permute-start.7 = (bf16[320,1024]{1,0:T(8,128)(2,1)S(1)}, bf16[320,1024]{1,0:T(8,128)(2,1)S(1)}, u32[]{:S(2)}, u32[]{:S(2)}) collective-permute-start(bf16[320,1024]{1,0:T(8,128)(2,1)S(1)} %pad_maximum_fusion.1), channel_id=1, source_target_pairs={{16,0},{20,4},{24,8},{28,12},{0,16},{4,20},{8,24},{12,28},{17,1},{... | collective-permute-start | bytes 1966088 | tf_op jit(solution)/shard_map/ppermute | solution.py:468
  97.4 15.9 %copy-start.6 = (f32[1024]{0:T(1024)S(1)}, f32[1024]{0:T(1024)}, u32[]{:S(2)}) copy-start(f32[1024]{0:T(1024)} %param.21) | copy-start | bytes 12292
  97.5 15.8 %collective-permute-start.8 = (bf16[640,1024]{1,0:T(8,128)(2,1)S(1)}, bf16[640,1024]{1,0:T(8,128)(2,1)S(1)}, u32[]{:S(2)}, u32[]{:S(2)}) collective-permute-start(bf16[640,1024]{1,0:T(8,128)(2,1)S(1)} %constant_dynamic-update-slice_fusion.mine), channel_id=1, source_target_pairs={{0,4},{4,0},{1,5},{5,1},{2,6},{6,2},{3,7},{7,3},{8,12},{12,8},{9,1... | collective-permute-start | bytes 3932168 | tf_op jit(solution)/shard_map/ppermute | solution.py:472

commit v5 on v4

--- a/solution.py
+++ b/solution.py
@@ -365,9 +365,9 @@
         peak = jnp.max(scores, axis=1, keepdims=True)
         weight = jnp.exp(scores - peak)
         total = jnp.sum(weight, axis=1, keepdims=True)
-        weight = (weight * (1.0 / total)).astype(BF16)
-        out = jnp.dot(weight, valued, preferred_element_type=F32)
-        return 0.5 * (out[:POOLED] + out[POOLED:])
+        weight = weight * (0.5 / total)
+        weight = (weight[:POOLED] + weight[POOLED:]).astype(BF16)
+        return jnp.dot(weight, valued, preferred_element_type=F32)
 
     queries = project(0, 256)
     keys = project(256, 256).astype(BF16)

time: 127 us -> 127 us (level)
  no operation moved by 1% of the time
where the time goes in v5:
time: 127 us
  blocking collectives  80.2 us (63%)
  starting transfers between devices  24.5 us (19%)
  Pallas kernels  17.7 us (14%)
  waiting for transfers between devices  2.16 us (2%)
  local copies, waits for them, and re-layouts  1.55 us (1%)
    all_gather x1, blocking collectives, shards(): gathered = lax.all_gather(packed, 'z', axis=0, tiled=True)  40.4 us
    ppermute x5, starting transfers between devices, y_shift(): return lax.ppermute(slabs, ('y', 'core'), pairs)  16.6 us
    all_to_all x1, blocking collectives, shards(): lax.all_to_all(terms, 'section', split_axis=0, concat_axis=0, tiled=True)  15.4 us
    all_gather x1, blocking collectives, shards(): rows = lax.all_gather(pooled_norm, 'section', axis=0, tiled=True)  13.8 us
    all_to_all x1, blocking collectives, shards(): lax.all_to_all(lm_local, 'section', split_axis=0, concat_axis=1, tiled=True)  10.6 us
    ppermute x3, starting transfers between devices, other_core(): return lax.ppermute(slabs, 'core', [(0, 1), (1, 0)])  5.76 us
    pallas_call x1, Pallas kernels, attend_call(): pl.pallas_call(attend_kernel, out_shape=jax.ShapeDtypeStruct((POOLED, D),...  5.68 us
    pallas_call x1, Pallas kernels, prepare_call(): pl.pallas_call(prepare_kernel, out_shape=(jax.ShapeDtypeStruct((ROWS, D),...  4.26 us
  transfers between devices with their start and end apart: 9, of which 2 were waited for; matrix products, arithmetic and copies ran while one was open for 0% of the time, Pallas kernels for 10%

profile of v5, /device:TPU:8, one launch (start us, length us, event | category | flops | bytes accessed | tf_op | source)
XLA Modules:
  0.0 126.6 jit_solution(14072025841916978597)
XLA Ops:
  0.0 3.0 %plan.1 = (s32[8]{0:T(128)}, bf16[192,128]{1,0:T(8,128)(2,1)}, bf16[128,1280]{1,0:T(8,128)(2,1)}, bf16[128,1280]{1,0:T(8,128)(2,1)}) custom-call(s32[768]{0:T(1024)} %utt.1, s32[768]{0:T(1024)} %dest.1, bf16[6,128,1280]{2,1,0:T(8,128)(2,1)} %frames.3, bf16[10,3,320]{2,1,0:T(4,128)(2,1)} %bitcast.14, bf16[10,320]{1,0:T(8,128)(2,1)} %bitcast.15, ...), custom_call_target="tpu_custom_call" | custom-call | tf_op jit(solution)/shard_map/plan/pallas_call | solution.py:122
  3.0 40.4 %all_gather.6.gathered = bf16[3072,128]{1,0:T(8,128)(2,1)S(1)} all-gather(bf16[192,128]{1,0:T(8,128)(2,1)} %get-tuple-element.28), channel_id=1, replica_groups=mesh['z'=16,'y'=4,'core'=2,'section'=4] {'z'}, dimensions={0}, use_global_device_ids=true | all-gather | bytes 835584 | tf_op jit(solution)/shard_map/all_gather | solution.py:491
  43.4 0.3 unpack.1
  43.8 2.4 %collective-permute-start = (bf16[160,1280]{1,0:T(8,128)(2,1)S(1)}, bf16[160,1280]{1,0:T(8,128)(2,1)S(1)}, u32[]{:S(2)}, u32[]{:S(2)}) collective-permute-start(bf16[160,1280]{1,0:T(8,128)(2,1)S(1)} %get-tuple-element.32), channel_id=1, source_target_pairs={{8,0},{28,4},{16,8},{4,12},{24,16},{12,20},{0,24},{20,28},{9,1},{2... | collective-permute-start | bytes 1228808 | tf_op jit(solution)/shard_map/ppermute | solution.py:468
  46.1 4.5 %collective-permute-start.1 = (bf16[160,1280]{1,0:T(8,128)(2,1)S(1)}, bf16[160,1280]{1,0:T(8,128)(2,1)S(1)}, u32[]{:S(2)}, u32[]{:S(2)}) collective-permute-start(bf16[160,1280]{1,0:T(8,128)(2,1)S(1)} %get-tuple-element.32), channel_id=1, source_target_pairs={{16,0},{20,4},{24,8},{28,12},{0,16},{4,20},{8,24},{12,28},{17,1},{... | collective-permute-start | bytes 1228808 | tf_op jit(solution)/shard_map/ppermute | solution.py:468
  50.6 3.8 %collective-permute-start.2 = (bf16[160,1280]{1,0:T(8,128)(2,1)S(1)}, bf16[160,1280]{1,0:T(8,128)(2,1)S(1)}, u32[]{:S(2)}, u32[]{:S(2)}) collective-permute-start(bf16[160,1280]{1,0:T(8,128)(2,1)S(1)} %get-tuple-element.32), channel_id=1, source_target_pairs={{24,0},{12,4},{0,8},{20,12},{8,16},{28,20},{16,24},{4,28},{25,1},{... | collective-permute-start | bytes 1228808 | tf_op jit(solution)/shard_map/ppermute | solution.py:468
  54.4 1.9 %collective-permute-start.4 = (bf16[128,1280]{1,0:T(8,128)(2,1)}, bf16[128,1280]{1,0:T(8,128)(2,1)S(1)}, u32[]{:S(2)}, u32[]{:S(2)}) collective-permute-start(bf16[128,1280]{1,0:T(8,128)(2,1)} %get-tuple-element.34), channel_id=1, source_target_pairs={{0,4},{4,0},{1,5},{5,1},{2,6},{6,2},{3,7},{7,3},{8,12},{12,8},{9,1... | collective-permute-start | bytes 983048 | tf_op jit(solution)/shard_map/ppermute | solution.py:472
  56.4 2.1 %collective-permute-start.3 = (bf16[128,1280]{1,0:T(8,128)(2,1)}, bf16[128,1280]{1,0:T(8,128)(2,1)S(1)}, u32[]{:S(2)}, u32[]{:S(2)}) collective-permute-start(bf16[128,1280]{1,0:T(8,128)(2,1)} %get-tuple-element.33), channel_id=1, source_target_pairs={{4,8},{12,16},{20,24},{28,32},{36,40},{44,48},{52,56},{60,64},{68,... | collective-permute-start | bytes 983048 | tf_op jit(solution)/shard_map/ppermute | solution.py:497
  58.5 1.9 %collective-permute-start.5 = (bf16[160,1024]{1,0:T(8,128)(2,1)S(1)}, bf16[160,1024]{1,0:T(8,128)(2,1)S(1)}, u32[]{:S(2)}, u32[]{:S(2)}) collective-permute-start(bf16[160,1024]{1,0:T(8,128)(2,1)S(1)} %get-tuple-element.40), channel_id=1, source_target_pairs={{8,0},{28,4},{16,8},{4,12},{24,16},{12,20},{0,24},{20,28},{9,1},{2... | collective-permute-start | bytes 983048 | tf_op jit(solution)/shard_map/ppermute | solution.py:468
  60.5 0.6 copy-done.5
  61.1 4.3 %prepare.1 = (bf16[512,1280]{1,0:T(8,128)(2,1)S(1)}, f32[64,1280]{1,0:T(8,128)S(1)}, f32[2,1280]{1,0:T(2,128)S(1)}) custom-call(s32[8]{0:T(128)S(1)} %copy-done.5, bf16[6,128,1280]{2,1,0:T(8,128)(2,1)S(1)} %copy-done, bf16[128,1280]{1,0:T(8,128)(2,1)S(1)} %collective-permute-done.4.near, f32[1280]{0:T(1024)S(1)} %copy-done.1, f32[1280]{0:T(1024)S(1)} %copy-done.2, ...), custom_call_target="tpu_custom_call" | custom-call | flops 100000000 | bytes 1048576 | tf_op jit(solution)/shard_map/prepare/pallas_call | solution.py:254
  65.5 2.7 %add_far.1 = (bf16[512,1280]{1,0:T(8,128)(2,1)S(1)}, f32[64,1280]{1,0:T(8,128)S(1)}) custom-call(s32[8]{0:T(128)S(1)} %copy-done.5, bf16[128,1280]{1,0:T(8,128)(2,1)S(1)} %collective-permute-done.3.far, f32[1280]{0:T(1024)S(1)} %copy-done.1, f32[1280]{0:T(1024)S(1)} %copy-done.2, ...), custom_call_target="tpu_custom_call", output_to_operand_aliasing={{0}: (4, {}), {1}: (5, {})} | custom-call | flops 100000000 | bytes 1048576 | tf_op jit(solution)/shard_map/add_far/pallas_call | solution.py:319
  68.2 0.1 pad_maximum_fusion.mine
  68.3 2.0 %collective-permute-done.5 = bf16[160,1024]{1,0:T(8,128)(2,1)S(1)} collective-permute-done((bf16[160,1024]{1,0:T(8,128)(2,1)S(1)}, bf16[160,1024]{1,0:T(8,128)(2,1)S(1)}, u32[]{:S(2)}, u32[]{:S(2)}) %collective-permute-start.5) | collective-permute-done | bytes 327712 | tf_op jit(solution)/shard_map/ppermute | solution.py:468
  70.4 1.9 %collective-permute-start.6 = (bf16[640,1280]{1,0:T(8,128)(2,1)S(1)}, bf16[640,1280]{1,0:T(8,128)(2,1)S(1)}, u32[]{:S(2)}, u32[]{:S(2)}) collective-permute-start(bf16[640,1280]{1,0:T(8,128)(2,1)S(1)} %pad_maximum_fusion.mine), channel_id=1, source_target_pairs={{0,4},{4,0},{1,5},{5,1},{2,6},{6,2},{3,7},{7,3},{8,12},{12,8},{9,1... | collective-permute-start | bytes 4915208 | tf_op jit(solution)/shard_map/ppermute | solution.py:472
  72.3 4.0 %collective-permute-start.7 = (bf16[320,1024]{1,0:T(8,128)(2,1)S(1)}, bf16[320,1024]{1,0:T(8,128)(2,1)S(1)}, u32[]{:S(2)}, u32[]{:S(2)}) collective-permute-start(bf16[320,1024]{1,0:T(8,128)(2,1)S(1)} %pad_maximum_fusion.1), channel_id=1, source_target_pairs={{16,0},{20,4},{24,8},{28,12},{0,16},{4,20},{8,24},{12,28},{17,1},{... | collective-permute-start | bytes 1966088 | tf_op jit(solution)/shard_map/ppermute | solution.py:468
  76.4 5.7 %attend.1 = bf16[256,1280]{1,0:T(8,128)(2,1)S(1)} custom-call(s32[8]{0:T(128)S(1)} %copy-done.5, bf16[512,1280]{1,0:T(8,128)(2,1)S(1)} %get-tuple-element.41.normed, bf16[640,1280]{1,0:T(8,128)(2,1)S(1)} %pad_maximum_fusion.mine, bf16[640,1280]{1,0:T(8,128)(2,1)S(1)} %collective-permute-done.6.other), custom_call_target="tpu_custom_call" | custom-call | flops 3000000000 | bytes 8388608 | tf_op jit(solution)/shard_map/attend/pallas_call | solution.py:402
  82.1 15.4 %all_to_all.30 = bf16[4,64,1280]{2,1,0:T(8,128)(2,1)S(1)} all-to-all(bf16[4,64,1280]{2,1,0:T(8,128)(2,1)S(1)} %bitcast.11), channel_id=1, replica_groups=mesh['z'=16,'y'=4,'core'=2,'section'=4] {'section'}, dimensions={0} | all-to-all | bytes 1310720 | tf_op jit(solution)/shard_map/all_to_all | solution.py:507
  97.5 0.3 finish.1
  97.9 1.9 %collective-permute-start.8 = (bf16[640,1024]{1,0:T(8,128)(2,1)S(1)}, bf16[640,1024]{1,0:T(8,128)(2,1)S(1)}, u32[]{:S(2)}, u32[]{:S(2)}) collective-permute-start(bf16[640,1024]{1,0:T(8,128)(2,1)S(1)} %constant_dynamic-update-slice_fusion.mine), channel_id=1, source_target_pairs={{0,4},{4,0},{1,5},{5,1},{2,6},{6,2},{3,7},{7,3},{8,12},{12,8},{9,1... | collective-permute-start | bytes 3932168 | tf_op jit(solution)/shard_map/ppermute | solution.py:472
  99.8 13.8 %all_gather.7.rows = bf16[256,1280]{1,0:T(8,128)(2,1)S(1)} all-gather(bf16[64,1280]{1,0:T(8,128)(2,1)S(1)} %finish.1), channel_id=1, replica_groups=mesh['z'=16,'y'=4,'core'=2,'section'=4] {'section'}, dimensions={0}, use_global_device_ids=true | all-gather | bytes 819200 | tf_op jit(solution)/shard_map/all_gather | solution.py:514
  113.7 1.5 %project.1 = bf16[256,1024]{1,0:T(8,128)(2,1)S(1)} custom-call(s32[8]{0:T(128)S(1)} %copy-done.5, bf16[256,1280]{1,0:T(8,128)(2,1)S(1)} %all_gather.7.rows, bf16[640,1024]{1,0:T(8,128)(2,1)S(1)} %constant_dynamic-update-slice_fusion.mine, bf16[640,1024]{1,0:T(8,128)(2,1)S(1)} %collective-permute-done.8.other, f32[1,1024]{1,0:T(1,128)S(1)} %bitcast.12), custom_call_target="tpu_custom_call" | custom-call | flops 671088640 | bytes 4194304 | tf_op jit(solution)/shard_map/project/pallas_call | solution.py:449
  115.2 10.6 %all_to_all.31 = bf16[4,64,1024]{2,1,0:T(8,128)(2,1)S(1)} all-to-all(bf16[4,64,1024]{2,1,0:T(8,128)(2,1)S(1)} %bitcast.10), channel_id=1, replica_groups=mesh['z'=16,'y'=4,'core'=2,'section'=4] {'section'}, dimensions={0} | all-to-all | bytes 1048576 | tf_op jit(solution)/shard_map/all_to_all | solution.py:517
  125.8 0.8 copy.15
  (24 shorter events, 0.3 us)
Async XLA Ops:
  0.0 60.5 %copy-start = (bf16[6,128,1280]{2,1,0:T(8,128)(2,1)S(1)}, bf16[6,128,1280]{2,1,0:T(8,128)(2,1)}, u32[]{:S(2)}) copy-start(bf16[6,128,1280]{2,1,0:T(8,128)(2,1)} %frames.3) | copy-start | bytes 5898244
  0.0 60.5 %copy-start.1 = (f32[1280]{0:T(1024)S(1)}, f32[1280]{0:T(1024)}, u32[]{:S(2)}) copy-start(f32[1280]{0:T(1024)} %gain.3) | copy-start | bytes 15364
  0.0 60.5 %copy-start.2 = (f32[1280]{0:T(1024)S(1)}, f32[1280]{0:T(1024)}, u32[]{:S(2)}) copy-start(f32[1280]{0:T(1024)} %shift.3) | copy-start | bytes 15364
  0.0 60.5 %copy-start.3 = (f32[1280]{0:T(1024)S(1)}, f32[1280]{0:T(1024)}, u32[]{:S(2)}) copy-start(f32[1280]{0:T(1024)} %post_gain.1) | copy-start | bytes 15364
  0.0 60.5 %copy-start.4 = (f32[1280]{0:T(1024)S(1)}, f32[1280]{0:T(1024)}, u32[]{:S(2)}) copy-start(f32[1280]{0:T(1024)} %post_shift.1) | copy-start | bytes 15364
  43.8 24.4 %collective-permute-start = (bf16[160,1280]{1,0:T(8,128)(2,1)S(1)}, bf16[160,1280]{1,0:T(8,128)(2,1)S(1)}, u32[]{:S(2)}, u32[]{:S(2)}) collective-permute-start(bf16[160,1280]{1,0:T(8,128)(2,1)S(1)} %get-tuple-element.32), channel_id=1, source_target_pairs={{8,0},{28,4},{16,8},{4,12},{24,16},{12,20},{0,24},{20,28},{9,1},{2... | collective-permute-start | bytes 1228808 | tf_op jit(solution)/shard_map/ppermute | solution.py:468
  46.1 22.1 %collective-permute-start.1 = (bf16[160,1280]{1,0:T(8,128)(2,1)S(1)}, bf16[160,1280]{1,0:T(8,128)(2,1)S(1)}, u32[]{:S(2)}, u32[]{:S(2)}) collective-permute-start(bf16[160,1280]{1,0:T(8,128)(2,1)S(1)} %get-tuple-element.32), channel_id=1, source_target_pairs={{16,0},{20,4},{24,8},{28,12},{0,16},{4,20},{8,24},{12,28},{17,1},{... | collective-permute-start | bytes 1228808 | tf_op jit(solution)/shard_map/ppermute | solution.py:468
  50.6 17.6 %collective-permute-start.2 = (bf16[160,1280]{1,0:T(8,128)(2,1)S(1)}, bf16[160,1280]{1,0:T(8,128)(2,1)S(1)}, u32[]{:S(2)}, u32[]{:S(2)}) collective-permute-start(bf16[160,1280]{1,0:T(8,128)(2,1)S(1)} %get-tuple-element.32), channel_id=1, source_target_pairs={{24,0},{12,4},{0,8},{20,12},{8,16},{28,20},{16,24},{4,28},{25,1},{... | collective-permute-start | bytes 1228808 | tf_op jit(solution)/shard_map/ppermute | solution.py:468
  54.4 4.1 %collective-permute-start.4 = (bf16[128,1280]{1,0:T(8,128)(2,1)}, bf16[128,1280]{1,0:T(8,128)(2,1)S(1)}, u32[]{:S(2)}, u32[]{:S(2)}) collective-permute-start(bf16[128,1280]{1,0:T(8,128)(2,1)} %get-tuple-element.34), channel_id=1, source_target_pairs={{0,4},{4,0},{1,5},{5,1},{2,6},{6,2},{3,7},{7,3},{8,12},{12,8},{9,1... | collective-permute-start | bytes 983048 | tf_op jit(solution)/shard_map/ppermute | solution.py:472
  56.4 9.1 %collective-permute-start.3 = (bf16[128,1280]{1,0:T(8,128)(2,1)}, bf16[128,1280]{1,0:T(8,128)(2,1)S(1)}, u32[]{:S(2)}, u32[]{:S(2)}) collective-permute-start(bf16[128,1280]{1,0:T(8,128)(2,1)} %get-tuple-element.33), channel_id=1, source_target_pairs={{4,8},{12,16},{20,24},{28,32},{36,40},{44,48},{52,56},{60,64},{68,... | collective-permute-start | bytes 983048 | tf_op jit(solution)/shard_map/ppermute | solution.py:497
  58.5 11.8 %collective-permute-start.5 = (bf16[160,1024]{1,0:T(8,128)(2,1)S(1)}, bf16[160,1024]{1,0:T(8,128)(2,1)S(1)}, u32[]{:S(2)}, u32[]{:S(2)}) collective-permute-start(bf16[160,1024]{1,0:T(8,128)(2,1)S(1)} %get-tuple-element.40), channel_id=1, source_target_pairs={{8,0},{28,4},{16,8},{4,12},{24,16},{12,20},{0,24},{20,28},{9,1},{2... | collective-permute-start | bytes 983048 | tf_op jit(solution)/shard_map/ppermute | solution.py:468
  60.5 0.6 copy-start.5
  70.4 6.0 %collective-permute-start.6 = (bf16[640,1280]{1,0:T(8,128)(2,1)S(1)}, bf16[640,1280]{1,0:T(8,128)(2,1)S(1)}, u32[]{:S(2)}, u32[]{:S(2)}) collective-permute-start(bf16[640,1280]{1,0:T(8,128)(2,1)S(1)} %pad_maximum_fusion.mine), channel_id=1, source_target_pairs={{0,4},{4,0},{1,5},{5,1},{2,6},{6,2},{3,7},{7,3},{8,12},{12,8},{9,1... | collective-permute-start | bytes 4915208 | tf_op jit(solution)/shard_map/ppermute | solution.py:472
  72.3 25.4 %collective-permute-start.7 = (bf16[320,1024]{1,0:T(8,128)(2,1)S(1)}, bf16[320,1024]{1,0:T(8,128)(2,1)S(1)}, u32[]{:S(2)}, u32[]{:S(2)}) collective-permute-start(bf16[320,1024]{1,0:T(8,128)(2,1)S(1)} %pad_maximum_fusion.1), channel_id=1, source_target_pairs={{16,0},{20,4},{24,8},{28,12},{0,16},{4,20},{8,24},{12,28},{17,1},{... | collective-permute-start | bytes 1966088 | tf_op jit(solution)/shard_map/ppermute | solution.py:468
  97.7 15.9 %copy-start.6 = (f32[1024]{0:T(1024)S(1)}, f32[1024]{0:T(1024)}, u32[]{:S(2)}) copy-start(f32[1024]{0:T(1024)} %param.21) | copy-start | bytes 12292
  97.9 15.8 %collective-permute-start.8 = (bf16[640,1024]{1,0:T(8,128)(2,1)S(1)}, bf16[640,1024]{1,0:T(8,128)(2,1)S(1)}, u32[]{:S(2)}, u32[]{:S(2)}) collective-permute-start(bf16[640,1024]{1,0:T(8,128)(2,1)S(1)} %constant_dynamic-update-slice_fusion.mine), channel_id=1, source_target_pairs={{0,4},{4,0},{1,5},{5,1},{2,6},{6,2},{3,7},{7,3},{8,12},{12,8},{9,1... | collective-permute-start | bytes 3932168 | tf_op jit(solution)/shard_map/ppermute | solution.py:472

commit v6 on v5

--- a/solution.py
+++ b/solution.py
@@ -365,9 +365,9 @@
         peak = jnp.max(scores, axis=1, keepdims=True)
         weight = jnp.exp(scores - peak)
         total = jnp.sum(weight, axis=1, keepdims=True)
-        weight = weight * (0.5 / total)
-        weight = (weight[:POOLED] + weight[POOLED:]).astype(BF16)
-        return jnp.dot(weight, valued, preferred_element_type=F32)
+        out = jnp.dot(weight.astype(BF16), valued, preferred_element_type=F32)
+        out = out * (0.5 / total)
+        return out[:POOLED] + out[POOLED:]
 
     queries = project(0, 256)
     keys = project(256, 256).astype(BF16)

time: 127 us -> 126 us (level)
  no operation moved by 1% of the time
where the time goes in v6:
time: 126 us
  blocking collectives  80.2 us (64%)
  starting transfers between devices  24.5 us (19%)
  Pallas kernels  17 us (13%)
  waiting for transfers between devices  2.16 us (2%)
  local copies, waits for them, and re-layouts  1.55 us (1%)
    all_gather x1, blocking collectives, shards(): gathered = lax.all_gather(packed, 'z', axis=0, tiled=True)  40.4 us
    ppermute x5, starting transfers between devices, y_shift(): return lax.ppermute(slabs, ('y', 'core'), pairs)  16.6 us
    all_to_all x1, blocking collectives, shards(): lax.all_to_all(terms, 'section', split_axis=0, concat_axis=0, tiled=True)  15.4 us
    all_gather x1, blocking collectives, shards(): rows = lax.all_gather(pooled_norm, 'section', axis=0, tiled=True)  13.8 us
    all_to_all x1, blocking collectives, shards(): lax.all_to_all(lm_local, 'section', split_axis=0, concat_axis=1, tiled=True)  10.6 us
    ppermute x3, starting transfers between devices, other_core(): return lax.ppermute(slabs, 'core', [(0, 1), (1, 0)])  5.76 us
    pallas_call x1, Pallas kernels, attend_call(): pl.pallas_call(attend_kernel, out_shape=jax.ShapeDtypeStruct((POOLED, D),...  4.96 us
    pallas_call x1, Pallas kernels, prepare_call(): pl.pallas_call(prepare_kernel, out_shape=(jax.ShapeDtypeStruct((ROWS, D),...  4.26 us
  transfers between devices with their start and end apart: 9, of which 2 were waited for; matrix products, arithmetic and copies ran while one was open for 0% of the time, Pallas kernels for 10%

profile of v6, /device:TPU:8, one launch (start us, length us, event | category | flops | bytes accessed | tf_op | source)
XLA Modules:
  0.0 125.9 jit_solution(6295931451211420115)
XLA Ops:
  0.0 3.0 %plan.1 = (s32[8]{0:T(128)}, bf16[192,128]{1,0:T(8,128)(2,1)}, bf16[128,1280]{1,0:T(8,128)(2,1)}, bf16[128,1280]{1,0:T(8,128)(2,1)}) custom-call(s32[768]{0:T(1024)} %utt.1, s32[768]{0:T(1024)} %dest.1, bf16[6,128,1280]{2,1,0:T(8,128)(2,1)} %frames.3, bf16[10,3,320]{2,1,0:T(4,128)(2,1)} %bitcast.14, bf16[10,320]{1,0:T(8,128)(2,1)} %bitcast.15, ...), custom_call_target="tpu_custom_call" | custom-call | tf_op jit(solution)/shard_map/plan/pallas_call | solution.py:122
  3.0 40.4 %all_gather.6.gathered = bf16[3072,128]{1,0:T(8,128)(2,1)S(1)} all-gather(bf16[192,128]{1,0:T(8,128)(2,1)} %get-tuple-element.28), channel_id=1, replica_groups=mesh['z'=16,'y'=4,'core'=2,'section'=4] {'z'}, dimensions={0}, use_global_device_ids=true | all-gather | bytes 835584 | tf_op jit(solution)/shard_map/all_gather | solution.py:491
  43.4 0.3 unpack.1
  43.8 2.4 %collective-permute-start = (bf16[160,1280]{1,0:T(8,128)(2,1)S(1)}, bf16[160,1280]{1,0:T(8,128)(2,1)S(1)}, u32[]{:S(2)}, u32[]{:S(2)}) collective-permute-start(bf16[160,1280]{1,0:T(8,128)(2,1)S(1)} %get-tuple-element.32), channel_id=1, source_target_pairs={{8,0},{28,4},{16,8},{4,12},{24,16},{12,20},{0,24},{20,28},{9,1},{2... | collective-permute-start | bytes 1228808 | tf_op jit(solution)/shard_map/ppermute | solution.py:468
  46.1 4.5 %collective-permute-start.1 = (bf16[160,1280]{1,0:T(8,128)(2,1)S(1)}, bf16[160,1280]{1,0:T(8,128)(2,1)S(1)}, u32[]{:S(2)}, u32[]{:S(2)}) collective-permute-start(bf16[160,1280]{1,0:T(8,128)(2,1)S(1)} %get-tuple-element.32), channel_id=1, source_target_pairs={{16,0},{20,4},{24,8},{28,12},{0,16},{4,20},{8,24},{12,28},{17,1},{... | collective-permute-start | bytes 1228808 | tf_op jit(solution)/shard_map/ppermute | solution.py:468
  50.6 3.8 %collective-permute-start.2 = (bf16[160,1280]{1,0:T(8,128)(2,1)S(1)}, bf16[160,1280]{1,0:T(8,128)(2,1)S(1)}, u32[]{:S(2)}, u32[]{:S(2)}) collective-permute-start(bf16[160,1280]{1,0:T(8,128)(2,1)S(1)} %get-tuple-element.32), channel_id=1, source_target_pairs={{24,0},{12,4},{0,8},{20,12},{8,16},{28,20},{16,24},{4,28},{25,1},{... | collective-permute-start | bytes 1228808 | tf_op jit(solution)/shard_map/ppermute | solution.py:468
  54.4 1.9 %collective-permute-start.4 = (bf16[128,1280]{1,0:T(8,128)(2,1)}, bf16[128,1280]{1,0:T(8,128)(2,1)S(1)}, u32[]{:S(2)}, u32[]{:S(2)}) collective-permute-start(bf16[128,1280]{1,0:T(8,128)(2,1)} %get-tuple-element.34), channel_id=1, source_target_pairs={{0,4},{4,0},{1,5},{5,1},{2,6},{6,2},{3,7},{7,3},{8,12},{12,8},{9,1... | collective-permute-start | bytes 983048 | tf_op jit(solution)/shard_map/ppermute | solution.py:472
  56.4 2.1 %collective-permute-start.3 = (bf16[128,1280]{1,0:T(8,128)(2,1)}, bf16[128,1280]{1,0:T(8,128)(2,1)S(1)}, u32[]{:S(2)}, u32[]{:S(2)}) collective-permute-start(bf16[128,1280]{1,0:T(8,128)(2,1)} %get-tuple-element.33), channel_id=1, source_target_pairs={{4,8},{12,16},{20,24},{28,32},{36,40},{44,48},{52,56},{60,64},{68,... | collective-permute-start | bytes 983048 | tf_op jit(solution)/shard_map/ppermute | solution.py:497
  58.5 1.9 %collective-permute-start.5 = (bf16[160,1024]{1,0:T(8,128)(2,1)S(1)}, bf16[160,1024]{1,0:T(8,128)(2,1)S(1)}, u32[]{:S(2)}, u32[]{:S(2)}) collective-permute-start(bf16[160,1024]{1,0:T(8,128)(2,1)S(1)} %get-tuple-element.40), channel_id=1, source_target_pairs={{8,0},{28,4},{16,8},{4,12},{24,16},{12,20},{0,24},{20,28},{9,1},{2... | collective-permute-start | bytes 983048 | tf_op jit(solution)/shard_map/ppermute | solution.py:468
  60.5 0.6 copy-done.5
  61.1 4.3 %prepare.1 = (bf16[512,1280]{1,0:T(8,128)(2,1)S(1)}, f32[64,1280]{1,0:T(8,128)S(1)}, f32[2,1280]{1,0:T(2,128)S(1)}) custom-call(s32[8]{0:T(128)S(1)} %copy-done.5, bf16[6,128,1280]{2,1,0:T(8,128)(2,1)S(1)} %copy-done, bf16[128,1280]{1,0:T(8,128)(2,1)S(1)} %collective-permute-done.4.near, f32[1280]{0:T(1024)S(1)} %copy-done.1, f32[1280]{0:T(1024)S(1)} %copy-done.2, ...), custom_call_target="tpu_custom_call" | custom-call | flops 100000000 | bytes 1048576 | tf_op jit(solution)/shard_map/prepare/pallas_call | solution.py:254
  65.5 2.7 %add_far.1 = (bf16[512,1280]{1,0:T(8,128)(2,1)S(1)}, f32[64,1280]{1,0:T(8,128)S(1)}) custom-call(s32[8]{0:T(128)S(1)} %copy-done.5, bf16[128,1280]{1,0:T(8,128)(2,1)S(1)} %collective-permute-done.3.far, f32[1280]{0:T(1024)S(1)} %copy-done.1, f32[1280]{0:T(1024)S(1)} %copy-done.2, ...), custom_call_target="tpu_custom_call", output_to_operand_aliasing={{0}: (4, {}), {1}: (5, {})} | custom-call | flops 100000000 | bytes 1048576 | tf_op jit(solution)/shard_map/add_far/pallas_call | solution.py:319
  68.2 0.1 pad_maximum_fusion.mine
  68.3 2.0 %collective-permute-done.5 = bf16[160,1024]{1,0:T(8,128)(2,1)S(1)} collective-permute-done((bf16[160,1024]{1,0:T(8,128)(2,1)S(1)}, bf16[160,1024]{1,0:T(8,128)(2,1)S(1)}, u32[]{:S(2)}, u32[]{:S(2)}) %collective-permute-start.5) | collective-permute-done | bytes 327712 | tf_op jit(solution)/shard_map/ppermute | solution.py:468
  70.4 1.9 %collective-permute-start.6 = (bf16[640,1280]{1,0:T(8,128)(2,1)S(1)}, bf16[640,1280]{1,0:T(8,128)(2,1)S(1)}, u32[]{:S(2)}, u32[]{:S(2)}) collective-permute-start(bf16[640,1280]{1,0:T(8,128)(2,1)S(1)} %pad_maximum_fusion.mine), channel_id=1, source_target_pairs={{0,4},{4,0},{1,5},{5,1},{2,6},{6,2},{3,7},{7,3},{8,12},{12,8},{9,1... | collective-permute-start | bytes 4915208 | tf_op jit(solution)/shard_map/ppermute | solution.py:472
  72.3 4.0 %collective-permute-start.7 = (bf16[320,1024]{1,0:T(8,128)(2,1)S(1)}, bf16[320,1024]{1,0:T(8,128)(2,1)S(1)}, u32[]{:S(2)}, u32[]{:S(2)}) collective-permute-start(bf16[320,1024]{1,0:T(8,128)(2,1)S(1)} %pad_maximum_fusion.1), channel_id=1, source_target_pairs={{16,0},{20,4},{24,8},{28,12},{0,16},{4,20},{8,24},{12,28},{17,1},{... | collective-permute-start | bytes 1966088 | tf_op jit(solution)/shard_map/ppermute | solution.py:468
  76.4 5.0 %attend.1 = bf16[256,1280]{1,0:T(8,128)(2,1)S(1)} custom-call(s32[8]{0:T(128)S(1)} %copy-done.5, bf16[512,1280]{1,0:T(8,128)(2,1)S(1)} %get-tuple-element.41.normed, bf16[640,1280]{1,0:T(8,128)(2,1)S(1)} %pad_maximum_fusion.mine, bf16[640,1280]{1,0:T(8,128)(2,1)S(1)} %collective-permute-done.6.other), custom_call_target="tpu_custom_call" | custom-call | flops 3000000000 | bytes 8388608 | tf_op jit(solution)/shard_map/attend/pallas_call | solution.py:402
  81.4 15.4 %all_to_all.30 = bf16[4,64,1280]{2,1,0:T(8,128)(2,1)S(1)} all-to-all(bf16[4,64,1280]{2,1,0:T(8,128)(2,1)S(1)} %bitcast.11), channel_id=1, replica_groups=mesh['z'=16,'y'=4,'core'=2,'section'=4] {'section'}, dimensions={0} | all-to-all | bytes 1310720 | tf_op jit(solution)/shard_map/all_to_all | solution.py:507
  96.7 0.3 finish.1
  97.1 1.9 %collective-permute-start.8 = (bf16[640,1024]{1,0:T(8,128)(2,1)S(1)}, bf16[640,1024]{1,0:T(8,128)(2,1)S(1)}, u32[]{:S(2)}, u32[]{:S(2)}) collective-permute-start(bf16[640,1024]{1,0:T(8,128)(2,1)S(1)} %constant_dynamic-update-slice_fusion.mine), channel_id=1, source_target_pairs={{0,4},{4,0},{1,5},{5,1},{2,6},{6,2},{3,7},{7,3},{8,12},{12,8},{9,1... | collective-permute-start | bytes 3932168 | tf_op jit(solution)/shard_map/ppermute | solution.py:472
  99.1 13.8 %all_gather.7.rows = bf16[256,1280]{1,0:T(8,128)(2,1)S(1)} all-gather(bf16[64,1280]{1,0:T(8,128)(2,1)S(1)} %finish.1), channel_id=1, replica_groups=mesh['z'=16,'y'=4,'core'=2,'section'=4] {'section'}, dimensions={0}, use_global_device_ids=true | all-gather | bytes 819200 | tf_op jit(solution)/shard_map/all_gather | solution.py:514
  112.9 1.5 %project.1 = bf16[256,1024]{1,0:T(8,128)(2,1)S(1)} custom-call(s32[8]{0:T(128)S(1)} %copy-done.5, bf16[256,1280]{1,0:T(8,128)(2,1)S(1)} %all_gather.7.rows, bf16[640,1024]{1,0:T(8,128)(2,1)S(1)} %constant_dynamic-update-slice_fusion.mine, bf16[640,1024]{1,0:T(8,128)(2,1)S(1)} %collective-permute-done.8.other, f32[1,1024]{1,0:T(1,128)S(1)} %bitcast.12), custom_call_target="tpu_custom_call" | custom-call | flops 671088640 | bytes 4194304 | tf_op jit(solution)/shard_map/project/pallas_call | solution.py:449
  114.5 10.6 %all_to_all.31 = bf16[4,64,1024]{2,1,0:T(8,128)(2,1)S(1)} all-to-all(bf16[4,64,1024]{2,1,0:T(8,128)(2,1)S(1)} %bitcast.10), channel_id=1, replica_groups=mesh['z'=16,'y'=4,'core'=2,'section'=4] {'section'}, dimensions={0} | all-to-all | bytes 1048576 | tf_op jit(solution)/shard_map/all_to_all | solution.py:517
  125.1 0.8 copy.15
  (24 shorter events, 0.3 us)
Async XLA Ops:
  0.0 60.5 %copy-start = (bf16[6,128,1280]{2,1,0:T(8,128)(2,1)S(1)}, bf16[6,128,1280]{2,1,0:T(8,128)(2,1)}, u32[]{:S(2)}) copy-start(bf16[6,128,1280]{2,1,0:T(8,128)(2,1)} %frames.3) | copy-start | bytes 5898244
  0.0 60.5 %copy-start.1 = (f32[1280]{0:T(1024)S(1)}, f32[1280]{0:T(1024)}, u32[]{:S(2)}) copy-start(f32[1280]{0:T(1024)} %gain.3) | copy-start | bytes 15364
  0.0 60.5 %copy-start.2 = (f32[1280]{0:T(1024)S(1)}, f32[1280]{0:T(1024)}, u32[]{:S(2)}) copy-start(f32[1280]{0:T(1024)} %shift.3) | copy-start | bytes 15364
  0.0 60.5 %copy-start.3 = (f32[1280]{0:T(1024)S(1)}, f32[1280]{0:T(1024)}, u32[]{:S(2)}) copy-start(f32[1280]{0:T(1024)} %post_gain.1) | copy-start | bytes 15364
  0.0 60.5 %copy-start.4 = (f32[1280]{0:T(1024)S(1)}, f32[1280]{0:T(1024)}, u32[]{:S(2)}) copy-start(f32[1280]{0:T(1024)} %post_shift.1) | copy-start | bytes 15364
  43.8 24.4 %collective-permute-start = (bf16[160,1280]{1,0:T(8,128)(2,1)S(1)}, bf16[160,1280]{1,0:T(8,128)(2,1)S(1)}, u32[]{:S(2)}, u32[]{:S(2)}) collective-permute-start(bf16[160,1280]{1,0:T(8,128)(2,1)S(1)} %get-tuple-element.32), channel_id=1, source_target_pairs={{8,0},{28,4},{16,8},{4,12},{24,16},{12,20},{0,24},{20,28},{9,1},{2... | collective-permute-start | bytes 1228808 | tf_op jit(solution)/shard_map/ppermute | solution.py:468
  46.1 22.1 %collective-permute-start.1 = (bf16[160,1280]{1,0:T(8,128)(2,1)S(1)}, bf16[160,1280]{1,0:T(8,128)(2,1)S(1)}, u32[]{:S(2)}, u32[]{:S(2)}) collective-permute-start(bf16[160,1280]{1,0:T(8,128)(2,1)S(1)} %get-tuple-element.32), channel_id=1, source_target_pairs={{16,0},{20,4},{24,8},{28,12},{0,16},{4,20},{8,24},{12,28},{17,1},{... | collective-permute-start | bytes 1228808 | tf_op jit(solution)/shard_map/ppermute | solution.py:468
  50.6 17.6 %collective-permute-start.2 = (bf16[160,1280]{1,0:T(8,128)(2,1)S(1)}, bf16[160,1280]{1,0:T(8,128)(2,1)S(1)}, u32[]{:S(2)}, u32[]{:S(2)}) collective-permute-start(bf16[160,1280]{1,0:T(8,128)(2,1)S(1)} %get-tuple-element.32), channel_id=1, source_target_pairs={{24,0},{12,4},{0,8},{20,12},{8,16},{28,20},{16,24},{4,28},{25,1},{... | collective-permute-start | bytes 1228808 | tf_op jit(solution)/shard_map/ppermute | solution.py:468
  54.4 4.1 %collective-permute-start.4 = (bf16[128,1280]{1,0:T(8,128)(2,1)}, bf16[128,1280]{1,0:T(8,128)(2,1)S(1)}, u32[]{:S(2)}, u32[]{:S(2)}) collective-permute-start(bf16[128,1280]{1,0:T(8,128)(2,1)} %get-tuple-element.34), channel_id=1, source_target_pairs={{0,4},{4,0},{1,5},{5,1},{2,6},{6,2},{3,7},{7,3},{8,12},{12,8},{9,1... | collective-permute-start | bytes 983048 | tf_op jit(solution)/shard_map/ppermute | solution.py:472
  56.4 9.1 %collective-permute-start.3 = (bf16[128,1280]{1,0:T(8,128)(2,1)}, bf16[128,1280]{1,0:T(8,128)(2,1)S(1)}, u32[]{:S(2)}, u32[]{:S(2)}) collective-permute-start(bf16[128,1280]{1,0:T(8,128)(2,1)} %get-tuple-element.33), channel_id=1, source_target_pairs={{4,8},{12,16},{20,24},{28,32},{36,40},{44,48},{52,56},{60,64},{68,... | collective-permute-start | bytes 983048 | tf_op jit(solution)/shard_map/ppermute | solution.py:497
  58.5 11.8 %collective-permute-start.5 = (bf16[160,1024]{1,0:T(8,128)(2,1)S(1)}, bf16[160,1024]{1,0:T(8,128)(2,1)S(1)}, u32[]{:S(2)}, u32[]{:S(2)}) collective-permute-start(bf16[160,1024]{1,0:T(8,128)(2,1)S(1)} %get-tuple-element.40), channel_id=1, source_target_pairs={{8,0},{28,4},{16,8},{4,12},{24,16},{12,20},{0,24},{20,28},{9,1},{2... | collective-permute-start | bytes 983048 | tf_op jit(solution)/shard_map/ppermute | solution.py:468
  60.5 0.6 copy-start.5
  70.4 6.0 %collective-permute-start.6 = (bf16[640,1280]{1,0:T(8,128)(2,1)S(1)}, bf16[640,1280]{1,0:T(8,128)(2,1)S(1)}, u32[]{:S(2)}, u32[]{:S(2)}) collective-permute-start(bf16[640,1280]{1,0:T(8,128)(2,1)S(1)} %pad_maximum_fusion.mine), channel_id=1, source_target_pairs={{0,4},{4,0},{1,5},{5,1},{2,6},{6,2},{3,7},{7,3},{8,12},{12,8},{9,1... | collective-permute-start | bytes 4915208 | tf_op jit(solution)/shard_map/ppermute | solution.py:472
  72.3 24.7 %collective-permute-start.7 = (bf16[320,1024]{1,0:T(8,128)(2,1)S(1)}, bf16[320,1024]{1,0:T(8,128)(2,1)S(1)}, u32[]{:S(2)}, u32[]{:S(2)}) collective-permute-start(bf16[320,1024]{1,0:T(8,128)(2,1)S(1)} %pad_maximum_fusion.1), channel_id=1, source_target_pairs={{16,0},{20,4},{24,8},{28,12},{0,16},{4,20},{8,24},{12,28},{17,1},{... | collective-permute-start | bytes 1966088 | tf_op jit(solution)/shard_map/ppermute | solution.py:468
  97.0 15.9 %copy-start.6 = (f32[1024]{0:T(1024)S(1)}, f32[1024]{0:T(1024)}, u32[]{:S(2)}) copy-start(f32[1024]{0:T(1024)} %param.21) | copy-start | bytes 12292
  97.1 15.8 %collective-permute-start.8 = (bf16[640,1024]{1,0:T(8,128)(2,1)S(1)}, bf16[640,1024]{1,0:T(8,128)(2,1)S(1)}, u32[]{:S(2)}, u32[]{:S(2)}) collective-permute-start(bf16[640,1024]{1,0:T(8,128)(2,1)S(1)} %constant_dynamic-update-slice_fusion.mine), channel_id=1, source_target_pairs={{0,4},{4,0},{1,5},{5,1},{2,6},{6,2},{3,7},{7,3},{8,12},{12,8},{9,1... | collective-permute-start | bytes 3932168 | tf_op jit(solution)/shard_map/ppermute | solution.py:472
